TPU v7x, 32 devices: a whole 2x2x4 slice. The times are simulated.
32 devices in a mesh: rep: 4 (over z), dom: 8 (over y, x, core).
Axes of the slice: x: 2, y: 2, z: 4, core: 2. Of those that a mesh axis runs over, the one named last changes fastest.
Arguments:
- feats: bfloat16 [12288, 256], P(('rep', 'dom')), may hold values from -6 to 6
- cotangent: bfloat16 [12288, 256], P(('rep', 'dom')), may hold values from -6 to 6
- weight: bfloat16 [256, 256], replicated, may hold values from -0.375 to 0.375
- bias: float32 [256], replicated, may hold values from -3 to 3
- in_vals: bfloat16 [96, 4, 2, 128, 128], P(('rep', 'dom')), may hold values from -0.125 to 0.125
- in_cols: int32 [96, 4, 2], P(('rep', 'dom')), may hold values from 0 to 2, as said below
- off_vals: bfloat16 [96, 9, 128, 128], P(('rep', 'dom')), may hold values from -0.125 to 0.125
- off_ref: int32 [96, 9], P(('rep', 'dom')), may hold values from 0 to 7, as said below
- want: int32 [4, 8, 8, 1], P('rep', 'dom'), may hold values from 0 to 2, as said below
Outputs:
- activated: bfloat16 [12288, 256], P(('rep', 'dom'))
- grad_feats: bfloat16 [12288, 256], P(('rep', 'dom'))
- grad_weight: bfloat16 [256, 256], replicated
Inputs may be any that keep to these rules, and one draw needn't show every extreme that they name: in_cols[b, s, k] is a block of panel (s, e) of the row block's own domain e; the 2 entries in_cols[b, s, :] differ. want[q, e, f, c] is a block, numbered within panel (q, f), that panel (q, e) asks of panel (q, f); the 1 entries of one request differ. off_ref[b, k] = f + c names block want[q, e, f, c] for a row block b of panel (q, e); f is never e. For each cycle position q some domain f has all its 1 slots named by the tiles of every panel (q, e) with e other than f.
All inputs are finite; a program needn't handle non-finite values.
Results may differ from a plain program's by a relative error of at most 0.009.
Values may be sent and summed in bfloat16 or wider, within the bound.
No kernel may reach another device: no remote copies, remote signals or barrier semaphores. Data moves between devices by JAX's collectives and lax.ppermute only.
A program may use at most 128 MiB of HBM per device.

v0:
```python
import math

import jax
import jax.numpy as jnp
from jax import lax
from jax.sharding import PartitionSpec as P


def passed_along(value, axis, steps):
    count = lax.axis_size(axis)
    pairs = [(source, (source + steps) % count) for source in range(count)]
    return lax.ppermute(value, axis, pairs)


def local(feats, cotangent, weight, bias, in_vals, in_cols, off_vals, off_ref, want):
    cycle_size = lax.axis_size("rep")
    position = lax.axis_index("rep")
    blocks = in_vals.shape[0]
    block_edge = in_vals.shape[3]
    feature_width = feats.shape[1]
    panel_rows = feats.shape[0]
    panel = feats.reshape(blocks, block_edge, feature_width)
    requests = want.reshape(want.shape[2], want.shape[3])
    slot_total = requests.shape[0] * requests.shape[1]
    block_range = jnp.arange(blocks, dtype=jnp.int32)

    def panel_product(source_panel, source):
        tile_set = lax.dynamic_index_in_dim(in_vals, source, 1, keepdims=False)
        columns = lax.dynamic_index_in_dim(in_cols, source, 1, keepdims=False)
        picked = source_panel[columns]
        return jnp.einsum("ikab,ikbf->iaf", tile_set, picked, preferred_element_type=jnp.float32)

    def advance(hop_index, state_pair):
        moving, summed = state_pair
        moving = passed_along(moving, "rep", 1)
        source = (position - hop_index) % cycle_size
        return (moving, summed + panel_product(moving, source))

    opening = panel_product(panel, position)
    inner_part = lax.fori_loop(1, cycle_size, advance, (panel, opening))[1]
    fetch_served = lax.all_to_all(requests, "dom", split_axis=0, concat_axis=0, tiled=True)
    outbound = panel[fetch_served]
    arrived = lax.all_to_all(outbound, "dom", split_axis=0, concat_axis=0, tiled=True)
    served, arrived = (fetch_served, arrived.reshape(slot_total, block_edge, feature_width))
    outer_part = jnp.einsum(
        "ikab,ikbf->iaf", off_vals, arrived[off_ref], preferred_element_type=jnp.float32
    )
    aggregate = (inner_part + outer_part).astype(jnp.bfloat16)
    flat_agg = aggregate.reshape(panel_rows, feature_width)
    pre_act = jnp.dot(flat_agg, weight, preferred_element_type=jnp.float32) + bias
    activated = jax.nn.gelu(pre_act).astype(jnp.bfloat16)
    _, pullback = jax.vjp(jax.nn.gelu, pre_act)
    grad_pre = pullback(cotangent.astype(jnp.float32))[0].astype(jnp.bfloat16)
    local_weight = lax.dot_general(
        flat_agg, grad_pre, (((0,), (0,)), ((), ())), preferred_element_type=jnp.float32
    )
    grad_agg = lax.dot_general(
        grad_pre, weight, (((1,), (1,)), ((), ())), preferred_element_type=jnp.float32
    ).astype(jnp.bfloat16)
    grad_blocks = grad_agg.reshape(blocks, block_edge, feature_width)
    tile_set = in_vals
    columns = in_cols
    spread = jnp.einsum(
        "iqkab,iaf->iqkbf", tile_set, grad_blocks, preferred_element_type=jnp.float32
    )
    onehot = (columns[..., None] == block_range).astype(jnp.float32)
    term_rows = jnp.einsum("iqkj,iqkbf->qjbf", onehot, spread, precision=lax.Precision.HIGHEST)
    inner_back = lax.psum_scatter(
        term_rows.reshape(panel_rows * lax.axis_size("rep"), feature_width).astype(jnp.bfloat16),
        "rep",
        scatter_dimension=0,
        tiled=True,
    ).astype(jnp.float32)
    spread = jnp.einsum("ikab,iaf->ikbf", off_vals, grad_blocks, preferred_element_type=jnp.float32)
    summed = jax.ops.segment_sum(
        spread.reshape(-1, block_edge, feature_width), off_ref.reshape(-1), num_segments=slot_total
    )
    outbound = summed.astype(jnp.bfloat16).reshape(
        requests.shape[0], requests.shape[1], block_edge, feature_width
    )
    coming = lax.all_to_all(outbound, "dom", split_axis=0, concat_axis=0, tiled=True)
    onehot = (served[..., None] == block_range).astype(jnp.bfloat16)
    outer_back = jnp.einsum("scj,scbf->jbf", onehot, coming, preferred_element_type=jnp.float32)
    grad_total = inner_back.reshape(blocks, block_edge, feature_width) + outer_back
    grad_feats = grad_total.astype(jnp.bfloat16).reshape(panel_rows, feature_width)
    total_weight = lax.psum(local_weight, ("rep", "dom"))
    node_count = panel_rows * cycle_size * lax.axis_size("dom")
    grad_weight = (total_weight * (1.0 / math.sqrt(node_count))).astype(jnp.bfloat16)
    return (activated, grad_feats, grad_weight)


def solution(mesh):
    in_specs = (
        P(("rep", "dom"), None),
        P(("rep", "dom"), None),
        P(),
        P(),
        P(("rep", "dom"), None, None, None, None),
        P(("rep", "dom"), None, None),
        P(("rep", "dom"), None, None, None),
        P(("rep", "dom"), None),
        P("rep", "dom", None, None),
    )
    out_specs = (P(("rep", "dom"), None), P(("rep", "dom"), None), P())
    return jax.shard_map(local, mesh=mesh, in_specs=in_specs, out_specs=out_specs, check_vma=False)
```

profile of v0, /device:TPU:0, one launch (start us, length us, event | category | flops | bytes accessed | tf_op | source)
XLA Modules:
  0.0 214.2 jit_solution(9885268665804156996)
XLA Ops:
  8.0 1.0 copy.109
  9.0 1.3 copy.69
  10.3 5.2 %all-to-all-start = ((s32[8,1,1]{2,1,0:T(1,128)}), s32[8,1,1]{2,1,0:T(1,128)S(1)}, u32[]{:S(2)}, u32[]{:S(2)}) async-start(s32[8,1,1]{2,1,0:T(1,128)} %copy.69), calls=%async_computation | async-start | bytes 8192 | tf_op jit(solution)/shard_map/all_to_all | solution.py:41
  15.5 0.8 copy.68
  16.3 0.8 constant_dynamic-slice_fusion
  17.9 2.2 %all-to-all-done = s32[8,1,1]{2,1,0:T(1,128)S(1)} async-done(((s32[8,1,1]{2,1,0:T(1,128)}), s32[8,1,1]{2,1,0:T(1,128)S(1)}, u32[]{:S(2)}, u32[]{:S(2)}) %all-to-all-start) | async-done | bytes 64 | tf_op jit(solution)/shard_map/all_to_all | solution.py:41
  20.5 1.4 gather_fusion.2
  21.9 3.5 %all-to-all-start.1 = ((bf16[8,1,128,256]{3,2,1,0:T(8,128)(2,1)}), bf16[8,1,128,256]{3,2,1,0:T(8,128)(2,1)S(1)}, u32[]{:S(2)}, u32[]{:S(2)}) async-start(bf16[8,1,128,256]{3,2,1,0:T(8,128)(2,1)} %bitcast.12), calls=%async_computation.1 | async-start | bytes 1048576 | tf_op jit(solution)/shard_map/all_to_all | solution.py:43
  25.4 0.7 compare_select_fusion.2
  26.2 1.1 convolution_bitcast_fusion.3
  27.3 7.7 %all-to-all-done.1 = bf16[8,1,128,256]{3,2,1,0:T(8,128)(2,1)S(1)} async-done(((bf16[8,1,128,256]{3,2,1,0:T(8,128)(2,1)}), bf16[8,1,128,256]{3,2,1,0:T(8,128)(2,1)S(1)}, u32[]{:S(2)}, u32[]{:S(2)}) %all-to-all-start.1) | async-done | bytes 524320 | tf_op jit(solution)/shard_map/all_to_all | solution.py:43
  35.0 1.9 gather_fusion.3
  37.0 25.1 %while.17 = (s32[]{:T(128)}, bf16[3,128,256]{2,1,0:T(8,128)(2,1)S(1)}, f32[3,128,256]{2,1,0:T(8,128)S(1)}, s32[]{:T(128)}, bf16[3,4,2,128,128]{4,3,2,1,0:T(8,128...) while((s32[]{:T(128)}, bf16[3,128,256]{2,1,0:T(8,128)(2,1)S(1)}, ...), condition=%wide.region_1.2_spmd, body=%wide.region_0.1_spmd.sunk | while | flops 50431008 | bytes 3346928 | solution.py:40
  37.0 1.6 collective-permute-start
  38.8 5.7 %collective-permute-done = bf16[3,128,256]{2,1,0:T(8,128)(2,1)S(1)} collective-permute-done((bf16[3,128,256]{2,1,0:T(8,128)(2,1)S(1)}, bf16[3,128,256]{2,1,0:T(8,128)(2,1)S(1)}, u32[]{:S(2)}, u32[]{:S(2)}) %collective-permute-start) | collective-permute-done | bytes 196640 | tf_op jit(solution)/shard_map/while/body/eval_jaxpr/ppermute | solution.py:12
  45.7 7.2 %collective-permute-done = bf16[3,128,256]{2,1,0:T(8,128)(2,1)S(1)} collective-permute-done((bf16[3,128,256]{2,1,0:T(8,128)(2,1)S(1)}, bf16[3,128,256]{2,1,0:T(8,128)(2,1)S(1)}, u32[]{:S(2)}, u32[]{:S(2)}) %collective-permute-start) | collective-permute-done | bytes 196640 | tf_op jit(solution)/shard_map/while/body/eval_jaxpr/ppermute | solution.py:12
  54.0 7.2 %collective-permute-done = bf16[3,128,256]{2,1,0:T(8,128)(2,1)S(1)} collective-permute-done((bf16[3,128,256]{2,1,0:T(8,128)(2,1)S(1)}, bf16[3,128,256]{2,1,0:T(8,128)(2,1)S(1)}, u32[]{:S(2)}, u32[]{:S(2)}) %collective-permute-start) | collective-permute-done | bytes 196640 | tf_op jit(solution)/shard_map/while/body/eval_jaxpr/ppermute | solution.py:12
  62.1 2.0 fusion.5
  64.1 1.2 fusion.11
  65.5 1.0 fusion.32
  66.5 2.3 %convolution_bitcast_fusion.1 = f32[3,4,2,128,256]{3,4,2,1,0:T(8,128)} fusion(bf16[3,128,256,1,1]{2,1,4,3,0:T(8,128)(2,1)S(1)} %bitcast.112, bf16[3,4,2,128,128]{4,3,2,1,0:T(8,128)(2,1)S(1)} %get-tuple-element.277), kind=kOutput, calls=%fused_computation.13 | convolution fusion | flops 201326592 | bytes 4128768 | tf_op jit(solution)/shard_map/iqkab,iaf->iqkbf/dot_general | solution.py:63
  68.8 5.1 %copy.72 = f32[3,4,2,128,256]{4,0,2,3,1:T(4,128)} copy(f32[3,4,2,128,256]{3,4,2,1,0:T(8,128)} %convolution_bitcast_fusion.1) | data formatting | bytes 6291456 | tf_op jit(solution)/shard_map/iqkab,iaf->iqkbf/dot_general | solution.py:63
  73.9 6.3 %bitcast_convert_fusion = bf16[4,3,128,256]{3,1,2,0:T(4,128)(2,1)S(1)} fusion(f32[3,4,2,128,256]{4,0,2,3,1:T(4,128)} %copy.72, s32[3,4,2]{0,2,1:T(2,128)S(1)} %get-tuple-element.285), kind=kOutput, calls=%fused_computation.12 | convolution fusion | flops 28704840 | bytes 3932256 | tf_op jit(solution)/shard_map/iqkj,iqkbf->qjbf/dot_general | solution.py:67
  80.2 1.0 copy.73
  81.3 2.4 %fusion.31 = f32[3,256,9,128]{3,1,2,0:T(8,128)} fusion(bf16[3,128,256,1]{2,1,3,0:T(8,128)(2,1)S(1)} %bitcast.113, bf16[3,9,128,128]{3,2,1,0:T(8,128)(2,1)S(1)} %copy-done), kind=kOutput, calls=%fused_computation.60 | convolution fusion | flops 226492416 | bytes 4620288 | tf_op jit(solution)/shard_map/ikab,iaf->ikbf/dot_general | solution.py:74
  83.8 5.2 %copy.75 = f32[27,128,256]{2,1,0:T(8,128)} copy(f32[27,128,256]{1,2,0:T(8,128)} %bitcast.105) | data formatting | bytes 7077888 | tf_op jit(solution)/shard_map/reshape | solution.py:76
  89.0 6.2 %scatter_fusion = f32[8,128,256]{2,1,0:T(8,128)S(1)} fusion(f32[8,128,256]{2,1,0:T(8,128)S(1)} %broadcast_in_dim.8, s32[27]{0:T(128)S(1)} %reshape.215, f32[27,128,256]{2,1,0:T(8,128)} %copy.75), kind=kCustom, calls=%fused_computation.4 | custom fusion | flops 884736 | bytes 10616940 | tf_op jit(solution)/shard_map/scatter-add | solution.py:75
  95.3 0.8 convert_bitcast_fusion
  96.1 3.6 %all-to-all-start.2 = ((bf16[8,1,128,256]{3,2,1,0:T(8,128)(2,1)}), bf16[8,1,128,256]{3,2,1,0:T(8,128)(2,1)S(1)}, u32[]{:S(2)}, u32[]{:S(2)}) async-start(bf16[8,1,128,256]{3,2,1,0:T(8,128)(2,1)} %convert_bitcast_fusion), calls=%async_computation.3 | async-start | bytes 1048576 | tf_op jit(solution)/shard_map/all_to_all | solution.py:81
  99.7 103.3 %all-reduce.2.cloned.1.call-done = f32[256,256]{1,0:T(8,128)} async-done(((f32[256,256]{1,0:T(8,128)}), f32[256,256]{1,0:T(8,128)}) %all-reduce.2.cloned.1.call-update) | async-done | bytes 262160 | tf_op jit(solution)/shard_map/psum | solution.py:86
  203.1 1.6 multiply_convert_fusion.1
  205.1 1.7 fusion.19
  (55 shorter events, 5.5 us)
Async XLA Ops:
  8.0 54.1 %copy-start = (bf16[3,9,128,128]{3,2,1,0:T(8,128)(2,1)S(1)}, bf16[3,9,128,128]{3,2,1,0:T(8,128)(2,1)}, u32[]{:S(2)}) copy-start(bf16[3,9,128,128]{3,2,1,0:T(8,128)(2,1)} %param.17) | copy-start | bytes 2654212
  10.3 9.8 %all-to-all-start = ((s32[8,1,1]{2,1,0:T(1,128)}), s32[8,1,1]{2,1,0:T(1,128)S(1)}, u32[]{:S(2)}, u32[]{:S(2)}) async-start(s32[8,1,1]{2,1,0:T(1,128)} %copy.69), calls=%async_computation | async-start | bytes 8192 | tf_op jit(solution)/shard_map/all_to_all | solution.py:41
  17.3 19.6 %copy-start.1 = (bf16[3,4,2,128,128]{4,3,2,1,0:T(8,128)(2,1)S(1)}, bf16[3,4,2,128,128]{4,3,2,1,0:T(8,128)(2,1)}, u32[]{:S(2)}) copy-start(bf16[3,4,2,128,128]{4,3,2,1,0:T(8,128)(2,1)} %param.15) | copy-start | bytes 2359300
  21.9 13.2 %all-to-all-start.1 = ((bf16[8,1,128,256]{3,2,1,0:T(8,128)(2,1)}), bf16[8,1,128,256]{3,2,1,0:T(8,128)(2,1)S(1)}, u32[]{:S(2)}, u32[]{:S(2)}) async-start(bf16[8,1,128,256]{3,2,1,0:T(8,128)(2,1)} %bitcast.12), calls=%async_computation.1 | async-start | bytes 1048576 | tf_op jit(solution)/shard_map/all_to_all | solution.py:43
  25.4 177.7 %all-reduce.2.cloned.1.call-start = ((), (), s32[]{:S(2)}) async-start(), calls=%async_computation.5 | async-start | bytes 524288 | tf_op jit(solution)/shard_map/psum | solution.py:86
  37.0 27.1 %copy-start.2 = (bf16[256,256]{1,0:T(8,128)(2,1)S(1)}, bf16[256,256]{1,0:T(8,128)(2,1)}, u32[]{:S(2)}) copy-start(bf16[256,256]{1,0:T(8,128)(2,1)} %param.13) | copy-start | bytes 393220
  37.0 27.1 %copy-start.4 = (bf16[384,256]{1,0:T(8,128)(2,1)S(1)}, bf16[384,256]{1,0:T(8,128)(2,1)}, u32[]{:S(2)}) copy-start(bf16[384,256]{1,0:T(8,128)(2,1)} %param.12) | copy-start | bytes 589828
  37.0 27.1 %copy-start.5 = (f32[256]{0:T(256)S(1)}, f32[256]{0:T(256)}, u32[]{:S(2)}) copy-start(f32[256]{0:T(256)} %param.14) | copy-start | bytes 3076
  37.0 7.5 %collective-permute-start = (bf16[3,128,256]{2,1,0:T(8,128)(2,1)S(1)}, bf16[3,128,256]{2,1,0:T(8,128)(2,1)S(1)}, u32[]{:S(2)}, u32[]{:S(2)}) collective-permute-start(bf16[3,128,256]{2,1,0:T(8,128)(2,1)S(1)} %get-tuple-element.253), channel_id=1, source_target_pairs={{0,8},{8,16},{16,24},{24,0},{1,9},{9,17},{17,25},{25,1},{2,10},{10... | collective-permute-start | bytes 589832 | tf_op jit(solution)/shard_map/while/body/eval_jaxpr/ppermute | solution.py:12
  45.4 7.5 %collective-permute-start = (bf16[3,128,256]{2,1,0:T(8,128)(2,1)S(1)}, bf16[3,128,256]{2,1,0:T(8,128)(2,1)S(1)}, u32[]{:S(2)}, u32[]{:S(2)}) collective-permute-start(bf16[3,128,256]{2,1,0:T(8,128)(2,1)S(1)} %get-tuple-element.253), channel_id=1, source_target_pairs={{0,8},{8,16},{16,24},{24,0},{1,9},{9,17},{17,25},{25,1},{2,10},{10... | collective-permute-start | bytes 589832 | tf_op jit(solution)/shard_map/while/body/eval_jaxpr/ppermute | solution.py:12
  53.7 7.5 %collective-permute-start = (bf16[3,128,256]{2,1,0:T(8,128)(2,1)S(1)}, bf16[3,128,256]{2,1,0:T(8,128)(2,1)S(1)}, u32[]{:S(2)}, u32[]{:S(2)}) collective-permute-start(bf16[3,128,256]{2,1,0:T(8,128)(2,1)S(1)} %get-tuple-element.253), channel_id=1, source_target_pairs={{0,8},{8,16},{16,24},{24,0},{1,9},{9,17},{17,25},{25,1},{2,10},{10... | collective-permute-start | bytes 589832 | tf_op jit(solution)/shard_map/while/body/eval_jaxpr/ppermute | solution.py:12
  73.9 7.4 %copy-start.3 = (s32[3,9]{1,0:T(4,128)S(1)}, s32[3,9]{1,0:T(4,128)}, u32[]{:S(2)}) copy-start(s32[3,9]{1,0:T(4,128)} %param.18) | copy-start | bytes 328
  73.9 131.2 %reduce-scatter.2.cloned.1.call-start = ((), (), s32[]{:S(2)}) async-start(), calls=%async_computation.4 | async-start | bytes 983040 | tf_op jit(solution)/shard_map/reduce_scatter | solution.py:68
  96.1 108.5 %all-to-all-start.2 = ((bf16[8,1,128,256]{3,2,1,0:T(8,128)(2,1)}), bf16[8,1,128,256]{3,2,1,0:T(8,128)(2,1)S(1)}, u32[]{:S(2)}, u32[]{:S(2)}) async-start(bf16[8,1,128,256]{3,2,1,0:T(8,128)(2,1)} %convert_bitcast_fusion), calls=%async_computation.3 | async-start | bytes 1048576 | tf_op jit(solution)/shard_map/all_to_all | solution.py:81
Sparse Core Ops, SparseCore 0:
  74.0 128.9 all-reduce.1
Sparse Core Ops, SparseCore 1:
  81.3 21.5 reduce-scatter.1
where the time goes:
time: 215 us; the launch traced here: 214 us
  waiting for transfers between devices  133 us (62%)
  local copies, waits for them, and re-layouts  21.9 us (10%)
  matrix products  17.5 us (8%)
  between operations  15.6 us (7%)
  starting transfers between devices  14.1 us (7%)
  other arithmetic  11.5 us (5%)
    psum x1, waiting for transfers between devices, local(): total_weight = lax.psum(local_weight, ('rep', 'dom'))  103 us
    ppermute x3, waiting for transfers between devices, passed_along(): return lax.ppermute(value, axis, pairs)  20.1 us
    all_to_all x2, waiting for transfers between devices, local(): lax.all_to_all(outbound, 'dom', split_axis=0, concat_axis=0, tiled=True)  7.7 us
    all_to_all x2, starting transfers between devices, local(): lax.all_to_all(outbound, 'dom', split_axis=0, concat_axis=0, tiled=True)  7.06 us
    dot_general x1, matrix products, local(): jnp.einsum('iqkj,iqkbf->qjbf', onehot, spread, precision=lax.Precision.HI...  6.25 us
    scatter-add x1, other arithmetic, local(): jax.ops.segment_sum(spread.reshape(-1, block_edge, feature_width), off_re...  6.24 us
    reshape x1, local copies, waits for them, and re-layouts, local(): spread.reshape(-1, block_edge, feature_width)  5.19 us
    all_to_all x1, starting transfers between devices, local(): lax.all_to_all(requests, 'dom', split_axis=0, concat_axis=0, tiled=True)  5.17 us
  transfers between devices with their start and end apart: 8, of which 6 were waited for; matrix products, arithmetic and copies ran while one was open for 14% of the time, Pallas kernels for 0%

commit v1 on v0

v1 whole, which is shorter than its diff:
```python
import functools
import math

import jax
import jax.numpy as jnp
from jax import lax
from jax.experimental import pallas as pl
from jax.experimental.pallas import tpu as pltpu
from jax.sharding import PartitionSpec as P

F32, BF16 = jnp.float32, jnp.bfloat16
ROOT = math.sqrt(2.0 / math.pi)
CUBIC = 0.044715


def partners(count):
    if count & (count - 1) == 0:
        return [[(i, i ^ k) for i in range(count)] for k in range(1, count)]
    return [[(i, (i + k) % count) for i in range(count)] for k in range(1, count)]


def source_of(me, k, count):
    return me ^ k if count & (count - 1) == 0 else (me - k + count) % count


def call(body, outs, args, kinds, scratch=(), flops=0, name=None):
    spaces = {"s": pltpu.SMEM, "v": pltpu.VMEM}
    nbytes = sum(math.prod(a.shape) * a.dtype.itemsize for a in (*args, *outs))
    work = sum(math.prod(s.shape) * jnp.dtype(s.dtype).itemsize for s in scratch)
    return pl.pallas_call(
        body,
        out_shape=outs,
        in_specs=[pl.BlockSpec(memory_space=spaces[k]) for k in kinds],
        out_specs=[pl.BlockSpec(memory_space=pltpu.VMEM) for _ in outs],
        scratch_shapes=list(scratch),
        cost_estimate=pl.CostEstimate(flops=flops, bytes_accessed=nbytes, transcendentals=0),
        compiler_params=pltpu.CompilerParams(vmem_limit_bytes=nbytes + work + (8 << 20)),
        name=name,
    )(*args)


def arrange(count, order_ref, cols_ref, in_ref, off_ref, a_ref, at_ref, offt_ref):
    blocks, _, pairs, edge, _ = in_ref.shape
    rows = blocks * edge
    a_ref[...] = jnp.zeros_like(a_ref)
    at_ref[...] = jnp.zeros_like(at_ref)
    for n in range(count):
        s = order_ref[n]
        for b in range(blocks):
            for k in range(pairs):
                tile = in_ref[b, s, k]
                start = pl.multiple_of(n * rows + cols_ref[b, s, k] * edge, edge)
                a_ref[b * edge:(b + 1) * edge, pl.ds(start, edge)] = tile
                at_ref[pl.ds(start, edge), b * edge:(b + 1) * edge] = tile.T
    for b in range(blocks):
        for k in range(off_ref.shape[1]):
            offt_ref[b, k] = off_ref[b, k].T


def pick(edge, served_ref, panel_ref, out_ref):
    for slot in range(out_ref.shape[0]):
        out_ref[slot] = panel_ref[pl.ds(pl.multiple_of(served_ref[slot] * edge, edge), edge), :]


def layer(count, refs_ref, *args):
    panels = args[:count]
    (a_ref, off_ref, block_ref, weight_ref, bias_ref, cot_ref,
     act_ref, agg_ref, pre_ref, grad_ref) = args[count:]
    blocks, tiles, edge, _ = off_ref.shape
    rows = blocks * edge
    for b in range(blocks):
        part = slice(b * edge, (b + 1) * edge)
        total = jnp.zeros((edge, weight_ref.shape[0]), F32)
        for n in range(count):
            total += jnp.dot(a_ref[part, n * rows:(n + 1) * rows], panels[n][...], preferred_element_type=F32)
        for k in range(0, tiles, 2):
            ks = range(k, min(k + 2, tiles))
            left = jnp.concatenate([off_ref[b, i] for i in ks], axis=1)
            right = jnp.concatenate([block_ref[refs_ref[b, i]] for i in ks], axis=0)
            total += jnp.dot(left, right, preferred_element_type=F32)
        agg = total.astype(BF16)
        agg_ref[part, :] = agg
        v = jnp.dot(agg, weight_ref[...], preferred_element_type=F32) + bias_ref[...]
        t = jnp.tanh(ROOT * (v + CUBIC * (v * v * v)))
        act_ref[part, :] = (0.5 * v * (1.0 + t)).astype(BF16)
        slope = 0.5 * (1.0 + t) + 0.5 * v * (1.0 - t * t) * (ROOT * (1.0 + 3.0 * CUBIC * (v * v)))
        grad = (cot_ref[part, :].astype(F32) * slope).astype(BF16)
        pre_ref[part, :] = grad
        grad_ref[part, :] = lax.dot_general(
            grad, weight_ref[...], (((1,), (1,)), ((), ())), preferred_element_type=F32).astype(BF16)


def spread_inner(count, at_ref, grad_ref, *outs):
    rows = grad_ref.shape[0]
    for n in range(count):
        outs[n][...] = jnp.dot(at_ref[n * rows:(n + 1) * rows, :], grad_ref[...], preferred_element_type=F32).astype(BF16)


def spread_outer(refs_ref, offt_ref, grad_ref, agg_ref, pre_ref, out_ref, total_ref):
    blocks, tiles, edge, _ = offt_ref.shape
    slots, width = total_ref.shape[0], total_ref.shape[2]
    total_ref[...] = jnp.zeros_like(total_ref)
    for b in range(blocks):
        grad = grad_ref[b * edge:(b + 1) * edge, :]
        for k in range(tiles):
            slot = refs_ref[b, k]
            total_ref[slot] += jnp.dot(offt_ref[b, k], grad, preferred_element_type=F32)
    out_ref[:, :edge, :] = total_ref[...].astype(BF16)
    term = lax.dot_general(agg_ref[...], pre_ref[...], (((0,), (0,)), ((), ())), preferred_element_type=F32)
    out_ref[:, edge:, :] = term.astype(BF16).reshape(slots, width // slots, width)


def finish_weight(edge, coming_ref, out_ref):
    out_ref[...] = jnp.sum(coming_ref[:, edge:, :].astype(F32), axis=0).astype(BF16)


def finish(edge, served_ref, coming_ref, *args):
    terms, out_ref, total_ref = args[:-2], args[-2], args[-1]
    total = terms[0][...].astype(F32)
    for t in terms[1:]:
        total += t[...].astype(F32)
    total_ref[...] = total
    for slot in range(coming_ref.shape[0]):
        part = pl.ds(pl.multiple_of(served_ref[slot] * edge, edge), edge)
        total_ref[part, :] += coming_ref[slot, :edge, :].astype(F32)
    out_ref[...] = total_ref[...].astype(BF16)


def local(feats, cotangent, weight, bias, in_vals, in_cols, off_vals, off_ref, want):
    count, doms = lax.axis_size("rep"), lax.axis_size("dom")
    me = lax.axis_index("rep")
    blocks, _, _, edge, _ = in_vals.shape
    rows, width = feats.shape
    requests = want.reshape(want.shape[2], want.shape[3])
    slots = requests.size
    share = width // slots
    shape = jax.ShapeDtypeStruct
    perms = partners(count)

    panels = [feats] + [lax.ppermute(feats, "rep", p) for p in perms]
    order = jnp.stack([source_of(me, k, count) for k in range(count)]).astype(jnp.int32)
    served = lax.all_to_all(requests, "dom", split_axis=0, concat_axis=0, tiled=True).reshape(slots)
    picked = call(functools.partial(pick, edge), [shape((slots, edge, width), BF16)], (served, feats), "sv", name="pick")[0]
    arrived = lax.all_to_all(picked, "dom", split_axis=0, concat_axis=0, tiled=True)

    a, at, offt = call(
        functools.partial(arrange, count),
        [shape((rows, count * rows), BF16), shape((count * rows, rows), BF16), shape(off_vals.shape, BF16)],
        (order, in_cols, in_vals, off_vals), "ssvv", name="arrange")
    flat = shape((rows, width), BF16)
    activated, agg, grad_pre, grad_agg = call(
        functools.partial(layer, count), [flat] * 4,
        (off_ref, *panels, a, off_vals, arrived, weight, bias.reshape(1, width), cotangent),
        "s" + "v" * (count + 6), flops=10**9, name="layer")
    terms = call(functools.partial(spread_inner, count), [flat] * count, (at, grad_agg), "vv", flops=10**9, name="inner")
    got = [terms[0]] + [lax.ppermute(t, "rep", [(b, a) for a, b in p]) for t, p in zip(terms[1:], perms)]
    outer = call(
        spread_outer, [shape((slots, edge + share, width), BF16)], (off_ref, offt, grad_agg, agg, grad_pre), "svvvv",
        scratch=[pltpu.VMEM((slots, edge, width), F32)], flops=10**9, name="outer")[0]
    coming = lax.all_to_all(outer, "dom", split_axis=0, concat_axis=0, tiled=True)
    mine = call(functools.partial(finish_weight, edge), [shape((share, width), BF16)], (coming,), "v", name="weight")[0]
    shares = [mine] + [lax.ppermute(mine, "rep", p) for p in perms]
    scale = 1.0 / math.sqrt(rows * count * doms)
    whole = (sum(s.astype(F32) for s in shares) * scale).astype(BF16)
    grad_weight = lax.all_gather(whole, "dom", axis=0, tiled=True)
    grad_feats = call(
        functools.partial(finish, edge), [flat], (served, coming, *got), "sv" + "v" * count,
        scratch=[pltpu.VMEM((rows, width), F32)], name="finish")[0]
    return (activated, grad_feats, grad_weight)


def solution(mesh):
    in_specs = (
        P(("rep", "dom"), None),
        P(("rep", "dom"), None),
        P(),
        P(),
        P(("rep", "dom"), None, None, None, None),
        P(("rep", "dom"), None, None),
        P(("rep", "dom"), None, None, None),
        P(("rep", "dom"), None),
        P("rep", "dom", None, None),
    )
    out_specs = (P(("rep", "dom"), None), P(("rep", "dom"), None), P())
    return jax.shard_map(local, mesh=mesh, in_specs=in_specs, out_specs=out_specs, check_vma=False)
```

time: 215 us -> 85.6 us (0.40)
  waiting for transfers between devices: 133 us -> 25.3 us
  blocking collectives: 0 us -> 19 us
  matrix products: 17.5 us -> 0 us
  between operations: 15.6 us -> 0.76 us
  local copies, waits for them, and re-layouts: 21.9 us -> 7.96 us
  other arithmetic: 11.5 us -> 0.32 us
  Pallas kernels: 0 us -> 10.8 us
  starting transfers between devices: 14.1 us -> 21 us
    psum x1 -> x0, waiting for transfers between devices: 103 us -> none  [local(): total_weight = lax.psum(local_weight, ('rep', 'dom'))]
    dot_general x12 -> x0, matrix products: 17.5 us -> none  [the longest x1 6.25 us: local(): jnp.einsum('iqkj,iqkbf->qjbf', onehot, spread, precision=lax.Precision.HI...]
    ppermute x3 -> x9, starting transfers between devices: 1.75 us -> 13.4 us  [the longest x3 4.45 us: local(): shares = [mine] + [lax.ppermute(mine, 'rep', p) for p in perms]]
    pallas_call x0 -> x7, Pallas kernels: none -> 10.8 us  [call(): pl.pallas_call(body, out_shape=outs, in_specs=[pl.BlockSpec(memory_space=...]
    all_to_all x0 -> x1, blocking collectives: none -> 9.62 us  [local(): lax.all_to_all(requests, 'dom', split_axis=0, concat_axis=0, tiled=True)]
    all_gather x0 -> x1, blocking collectives: none -> 9.38 us  [local(): grad_weight = lax.all_gather(whole, 'dom', axis=0, tiled=True)]
    scatter-add x1 -> x0, other arithmetic: 6.24 us -> none  [local(): jax.ops.segment_sum(spread.reshape(-1, block_edge, feature_width), off_re...]
    unnamed x13 -> x32, local copies, waits for them, and re-layouts: 1.04 us -> 7.11 us
  transfers between devices with their start and end apart: 8 -> 11, of which waited for: 6 -> 5; matrix products, arithmetic and copies ran while one was open for 14% -> 0% of each run, Pallas kernels for 0% -> 4%
where the time goes in v1:
time: 85.6 us; the launch traced here: 85.2 us
  waiting for transfers between devices  25.3 us (30%)
  starting transfers between devices  21 us (25%)
  blocking collectives  19 us (22%)
  Pallas kernels  10.8 us (13%)
  local copies, waits for them, and re-layouts  7.96 us (9%)
    ppermute x3, waiting for transfers between devices, local(): panels = [feats] + [lax.ppermute(feats, 'rep', p) for p in perms]  13.2 us
    pallas_call x7, Pallas kernels, call(): pl.pallas_call(body, out_shape=outs, in_specs=[pl.BlockSpec(memory_space=...  10.8 us
    all_to_all x1, blocking collectives, local(): lax.all_to_all(requests, 'dom', split_axis=0, concat_axis=0, tiled=True)  9.62 us
    all_gather x1, blocking collectives, local(): grad_weight = lax.all_gather(whole, 'dom', axis=0, tiled=True)  9.38 us
    unnamed x32, local copies, waits for them, and re-layouts  7.11 us
    all_to_all x1, waiting for transfers between devices, local(): lax.all_to_all(outer, 'dom', split_axis=0, concat_axis=0, tiled=True)  5.19 us
    ppermute x3, starting transfers between devices, local(): shares = [mine] + [lax.ppermute(mine, 'rep', p) for p in perms]  4.45 us
    ppermute x3, starting transfers between devices, local(): panels = [feats] + [lax.ppermute(feats, 'rep', p) for p in perms]  4.45 us
  transfers between devices with their start and end apart: 11, of which 5 were waited for; matrix products, arithmetic and copies ran while one was open for 0% of the time, Pallas kernels for 4%

profile of v1, /device:TPU:0, one launch (start us, length us, event | category | flops | bytes accessed | tf_op | source)
XLA Modules:
  0.0 85.2 jit_solution(8019802118349636773)
XLA Ops:
  0.7 0.9 %copy.16 = s32[8,1,1]{2,1,0:T(1,128)S(1)} copy(s32[8,1,1]{0,2,1:T(1,128)} %bitcast.7) | data formatting | bytes 64 | tf_op jit(solution)/shard_map/all_to_all | solution.py:142
  1.5 9.6 %all_to_all.19 = s32[8,1,1]{2,1,0:T(1,128)S(1)} all-to-all(s32[8,1,1]{2,1,0:T(1,128)S(1)} %copy.16), channel_id=1, replica_groups=mesh['rep'=4,'dom'=8] {'dom'}, dimensions={0} | all-to-all | bytes 64 | tf_op jit(solution)/shard_map/all_to_all | solution.py:142
  11.1 0.2 reduce.served_ref
  11.4 0.9 %copy-done.2 = bf16[384,256]{1,0:T(8,128)(2,1)S(1)} copy-done((bf16[384,256]{1,0:T(8,128)(2,1)S(1)}, bf16[384,256]{1,0:T(8,128)(2,1)}, u32[]{:S(2)}) %copy-start.2) | copy-done | bytes 196632
  12.3 1.4 %pick.1 = bf16[8,128,256]{2,1,0:T(8,128)(2,1)} custom-call(s32[8]{0:T(128)S(1)} %reduce.served_ref, bf16[384,256]{1,0:T(8,128)(2,1)S(1)} %copy-done.2), custom_call_target="tpu_custom_call" | custom-call | bytes 720928 | tf_op jit(solution)/shard_map/pick/pallas_call | solution.py:30
  13.7 3.6 %all-to-all-start.1 = ((bf16[8,128,256]{2,1,0:T(8,128)(2,1)}), bf16[8,128,256]{2,1,0:T(8,128)(2,1)S(1)}, u32[]{:S(2)}, u32[]{:S(2)}) async-start(bf16[8,128,256]{2,1,0:T(8,128)(2,1)} %pick.1), calls=%async_computation.1 | async-start | bytes 1048576 | tf_op jit(solution)/shard_map/all_to_all | solution.py:144
  17.3 3.7 %collective-permute-start.2 = (bf16[384,256]{1,0:T(8,128)(2,1)}, bf16[384,256]{1,0:T(8,128)(2,1)}, u32[]{:S(2)}, u32[]{:S(2)}) collective-permute-start(bf16[384,256]{1,0:T(8,128)(2,1)} %args_0_.4), channel_id=1, source_target_pairs={{0,24},{8,16},{16,8},{24,0},{1,25},{9,17},{17,9},{25,1},{2,26},{10... | collective-permute-start | bytes 589832 | tf_op jit(solution)/shard_map/ppermute | solution.py:140
  21.0 0.8 collective-permute-start
  21.8 0.1 copy.15.cols_ref
  22.0 1.4 %arrange.1 = (bf16[384,1536]{1,0:T(8,128)(2,1)S(1)}, bf16[1536,384]{1,0:T(8,128)(2,1)S(1)}, bf16[3,9,128,128]{3,2,1,0:T(8,128)(2,1)S(1)}) custom-call(s32[4]{0:T(128)S(1)} %pad_add_fusion.order_ref, s32[3,4,2]{2,1,0:T(4,128)S(1)} %copy.15.cols_ref, bf16[3,4,2,128,128]{4,3,2,1,0:T(8,128)(2,1)S(1)} %copy-done.1, bf16[3,9,128,128]{3,2,1,0:T(8,128)(2,1)S(1)} %copy-done), custom_call_target="tpu_custom_call" | custom-call | bytes 4915312 | tf_op jit(solution)/shard_map/arrange/pallas_call | solution.py:30
  23.3 1.0 %copy-done.8 = bf16[1536,384]{1,0:T(8,128)(2,1)} copy-done((bf16[1536,384]{1,0:T(8,128)(2,1)}, bf16[1536,384]{1,0:T(8,128)(2,1)S(1)}, u32[]{:S(2)}) %copy-start.8) | copy-done | bytes 1179672
  24.4 0.9 %copy-done.10 = bf16[3,9,128,128]{3,2,1,0:T(8,128)(2,1)} copy-done((bf16[3,9,128,128]{3,2,1,0:T(8,128)(2,1)}, bf16[3,9,128,128]{3,2,1,0:T(8,128)(2,1)S(1)}, u32[]{:S(2)}) %copy-start.10) | copy-done | bytes 884760
  25.3 2.1 %collective-permute-done.2.args_3_ = bf16[384,256]{1,0:T(8,128)(2,1)} collective-permute-done((bf16[384,256]{1,0:T(8,128)(2,1)}, bf16[384,256]{1,0:T(8,128)(2,1)}, u32[]{:S(2)}, u32[]{:S(2)}) %collective-permute-start.2) | collective-permute-done | bytes 196640 | tf_op jit(solution)/shard_map/ppermute | solution.py:140
  27.4 11.1 %collective-permute-done.1.args_2_ = bf16[384,256]{1,0:T(8,128)(2,1)} collective-permute-done((bf16[384,256]{1,0:T(8,128)(2,1)}, bf16[384,256]{1,0:T(8,128)(2,1)}, u32[]{:S(2)}, u32[]{:S(2)}) %collective-permute-start.1) | collective-permute-done | bytes 196640 | tf_op jit(solution)/shard_map/ppermute | solution.py:140
  38.5 0.9 %copy-done.3 = bf16[384,256]{1,0:T(8,128)(2,1)S(1)} copy-done((bf16[384,256]{1,0:T(8,128)(2,1)S(1)}, bf16[384,256]{1,0:T(8,128)(2,1)}, u32[]{:S(2)}) %copy-start.3) | copy-done | bytes 196632
  39.5 0.9 %copy-done.4 = bf16[384,256]{1,0:T(8,128)(2,1)S(1)} copy-done((bf16[384,256]{1,0:T(8,128)(2,1)S(1)}, bf16[384,256]{1,0:T(8,128)(2,1)}, u32[]{:S(2)}) %copy-start.4) | copy-done | bytes 196632
  40.4 3.9 %layer.1 = (bf16[384,256]{1,0:T(8,128)(2,1)}, bf16[384,256]{1,0:T(8,128)(2,1)S(1)}, bf16[384,256]{1,0:T(8,128)(2,1)S(1)}, bf16[384,256]{1,0:T(8,128)(2,1)S(1)}) custom-call(s32[3,9]{1,0:T(4,128)S(1)} %copy-done.6, bf16[384,256]{1,0:T(8,128)(2,1)S(1)} %copy-done.3, bf16[384,256]{1,0:T(8,128)(2,1)} %collective-permute-done.args_1_, ...), custom_call_target="tpu_custom_call" | custom-call | flops 1000000000 | bytes 4490348 | tf_op jit(solution)/shard_map/layer/pallas_call | solution.py:30
  44.2 2.1 %outer.1 = bf16[8,160,256]{2,1,0:T(8,128)(2,1)} custom-call(s32[3,9]{1,0:T(4,128)S(1)} %copy-done.6, bf16[3,9,128,128]{3,2,1,0:T(8,128)(2,1)S(1)} %copy-done.11, bf16[384,256]{1,0:T(8,128)(2,1)S(1)} %get-tuple-element.17.grad_ref, bf16[384,256]{1,0:T(8,128)(2,1)S(1)} %get-tuple-element.18.agg_ref, bf16[384,256]{1,0:T(8,128)(2,1)S(1)} %get-tuple-element.19.pre_ref), custom_call_target="tpu_custom_call" | custom-call | flops 1000000000 | bytes 2130028 | tf_op jit(solution)/shard_map/outer/pallas_call | solution.py:30
  46.4 0.7 copy-done.12
  47.1 4.0 %all-to-all-start.2 = ((bf16[8,160,256]{2,1,0:T(8,128)(2,1)}), bf16[8,160,256]{2,1,0:T(8,128)(2,1)S(1)}, u32[]{:S(2)}, u32[]{:S(2)}) async-start(bf16[8,160,256]{2,1,0:T(8,128)(2,1)} %outer.1), calls=%async_computation.2 | async-start | bytes 1310720 | tf_op jit(solution)/shard_map/all_to_all | solution.py:160
  51.1 0.9 %copy-done.13 = bf16[384,256]{1,0:T(8,128)(2,1)S(1)} copy-done((bf16[384,256]{1,0:T(8,128)(2,1)S(1)}, bf16[384,256]{1,0:T(8,128)(2,1)}, u32[]{:S(2)}) %copy-start.13) | copy-done | bytes 196632
  52.0 0.6 inner.1
  52.7 3.0 %collective-permute-start.4 = (bf16[384,256]{1,0:T(8,128)(2,1)S(1)}, bf16[384,256]{1,0:T(8,128)(2,1)S(1)}, u32[]{:S(2)}, u32[]{:S(2)}) collective-permute-start(bf16[384,256]{1,0:T(8,128)(2,1)S(1)} %get-tuple-element.23), channel_id=1, source_target_pairs={{16,0},{24,8},{0,16},{8,24},{17,1},{25,9},{1,17},{9,25},{18,2},{26... | collective-permute-start | bytes 589832 | tf_op jit(solution)/shard_map/ppermute | solution.py:156
  55.7 1.3 %collective-permute-start.5 = (bf16[384,256]{1,0:T(8,128)(2,1)S(1)}, bf16[384,256]{1,0:T(8,128)(2,1)S(1)}, u32[]{:S(2)}, u32[]{:S(2)}) collective-permute-start(bf16[384,256]{1,0:T(8,128)(2,1)S(1)} %get-tuple-element.24), channel_id=1, source_target_pairs={{24,0},{16,8},{8,16},{0,24},{25,1},{17,9},{9,17},{1,25},{26,2},{18... | collective-permute-start | bytes 589832 | tf_op jit(solution)/shard_map/ppermute | solution.py:156
  57.0 5.2 %all-to-all-done.2.coming_ref = bf16[8,160,256]{2,1,0:T(8,128)(2,1)S(1)} async-done(((bf16[8,160,256]{2,1,0:T(8,128)(2,1)}), bf16[8,160,256]{2,1,0:T(8,128)(2,1)S(1)}, u32[]{:S(2)}, u32[]{:S(2)}) %all-to-all-start.2) | async-done | bytes 655392 | tf_op jit(solution)/shard_map/all_to_all | solution.py:160
  62.3 2.5 %collective-permute-start.8 = (bf16[32,256]{1,0:T(8,128)(2,1)S(1)}, bf16[32,256]{1,0:T(8,128)(2,1)S(1)}, u32[]{:S(2)}, u32[]{:S(2)}) collective-permute-start(bf16[32,256]{1,0:T(8,128)(2,1)S(1)} %weight.1), channel_id=1, source_target_pairs={{0,24},{8,16},{16,8},{24,0},{1,25},{9,17},{17,9},{25,1},{2,26},{10... | collective-permute-start | bytes 49160 | tf_op jit(solution)/shard_map/ppermute | solution.py:162
  64.8 1.9 %collective-permute-start.6 = (bf16[32,256]{1,0:T(8,128)(2,1)S(1)}, bf16[32,256]{1,0:T(8,128)(2,1)S(1)}, u32[]{:S(2)}, u32[]{:S(2)}) collective-permute-start(bf16[32,256]{1,0:T(8,128)(2,1)S(1)} %weight.1), channel_id=1, source_target_pairs={{0,8},{8,0},{16,24},{24,16},{1,9},{9,1},{17,25},{25,17},{2,10},{10... | collective-permute-start | bytes 49160 | tf_op jit(solution)/shard_map/ppermute | solution.py:162
  66.7 3.9 %collective-permute-done.4.args_2_ = bf16[384,256]{1,0:T(8,128)(2,1)S(1)} collective-permute-done((bf16[384,256]{1,0:T(8,128)(2,1)S(1)}, bf16[384,256]{1,0:T(8,128)(2,1)S(1)}, u32[]{:S(2)}, u32[]{:S(2)}) %collective-permute-start.4) | collective-permute-done | bytes 196640 | tf_op jit(solution)/shard_map/ppermute | solution.py:156
  70.6 1.5 %finish.1 = bf16[384,256]{1,0:T(8,128)(2,1)} custom-call(s32[8]{0:T(128)S(1)} %reduce.served_ref, bf16[8,160,256]{2,1,0:T(8,128)(2,1)S(1)} %all-to-all-done.2.coming_ref, bf16[384,256]{1,0:T(8,128)(2,1)S(1)} %get-tuple-element.21.args_0_, bf16[384,256]{1,0:T(8,128)(2,1)S(1)} %collective-permute-done.3.args_1_, ...), custom_call_target="tpu_custom_call" | custom-call | bytes 1638432 | tf_op jit(solution)/shard_map/finish/pallas_call | solution.py:30
  72.1 3.0 %collective-permute-done.7 = bf16[32,256]{1,0:T(8,128)(2,1)S(1)} collective-permute-done((bf16[32,256]{1,0:T(8,128)(2,1)S(1)}, bf16[32,256]{1,0:T(8,128)(2,1)S(1)}, u32[]{:S(2)}, u32[]{:S(2)}) %collective-permute-start.7) | collective-permute-done | bytes 16416 | tf_op jit(solution)/shard_map/ppermute | solution.py:162
  75.1 9.4 %all_gather.3 = bf16[256,256]{1,0:T(8,128)(2,1)S(1)} all-gather(bf16[32,256]{1,0:T(8,128)(2,1)S(1)} %multiply_convert_fusion), channel_id=1, replica_groups=mesh['rep'=4,'dom'=8] {'dom'}, dimensions={0}, use_global_device_ids=true | all-gather | bytes 147456 | tf_op jit(solution)/shard_map/all_gather | solution.py:165
  84.5 0.7 copy.18
  (35 shorter events, 0.3 us)
Async XLA Ops:
  0.6 21.3 %copy-start = (bf16[3,9,128,128]{3,2,1,0:T(8,128)(2,1)S(1)}, bf16[3,9,128,128]{3,2,1,0:T(8,128)(2,1)}, u32[]{:S(2)}) copy-start(bf16[3,9,128,128]{3,2,1,0:T(8,128)(2,1)} %args_5_.4) | copy-start | bytes 2654212
  0.6 21.3 %copy-start.1 = (bf16[3,4,2,128,128]{4,3,2,1,0:T(8,128)(2,1)S(1)}, bf16[3,4,2,128,128]{4,3,2,1,0:T(8,128)(2,1)}, u32[]{:S(2)}) copy-start(bf16[3,4,2,128,128]{4,3,2,1,0:T(8,128)(2,1)} %in_ref.1) | copy-start | bytes 2359300
  11.4 0.9 %copy-start.2 = (bf16[384,256]{1,0:T(8,128)(2,1)S(1)}, bf16[384,256]{1,0:T(8,128)(2,1)}, u32[]{:S(2)}) copy-start(bf16[384,256]{1,0:T(8,128)(2,1)} %args_0_.4) | copy-start | bytes 589828
  12.3 9.5 %copy-start.14 = (s32[3,4,2]{1,2,0:T(2,128)S(1)}, s32[3,4,2]{1,2,0:T(2,128)}, u32[]{:S(2)}) copy-start(s32[3,4,2]{1,2,0:T(2,128)} %param.14) | copy-start | bytes 292
  13.7 24.8 %copy-start.5 = (bf16[256,256]{1,0:T(8,128)(2,1)S(1)}, bf16[256,256]{1,0:T(8,128)(2,1)}, u32[]{:S(2)}) copy-start(bf16[256,256]{1,0:T(8,128)(2,1)} %args_7_.4) | copy-start | bytes 393220
  13.7 24.8 %copy-start.6 = (s32[3,9]{1,0:T(4,128)S(1)}, s32[3,9]{1,0:T(4,128)}, u32[]{:S(2)}) copy-start(s32[3,9]{1,0:T(4,128)} %refs_ref.3) | copy-start | bytes 328
  13.7 24.8 %copy-start.7 = (f32[256]{0:T(256)S(1)}, f32[256]{0:T(256)}, u32[]{:S(2)}) copy-start(f32[256]{0:T(256)} %param.12) | copy-start | bytes 3076
  13.7 24.8 %all-to-all-start.1 = ((bf16[8,128,256]{2,1,0:T(8,128)(2,1)}), bf16[8,128,256]{2,1,0:T(8,128)(2,1)S(1)}, u32[]{:S(2)}, u32[]{:S(2)}) async-start(bf16[8,128,256]{2,1,0:T(8,128)(2,1)} %pick.1), calls=%async_computation.1 | async-start | bytes 1048576 | tf_op jit(solution)/shard_map/all_to_all | solution.py:144
  17.3 10.0 %collective-permute-start.2 = (bf16[384,256]{1,0:T(8,128)(2,1)}, bf16[384,256]{1,0:T(8,128)(2,1)}, u32[]{:S(2)}, u32[]{:S(2)}) collective-permute-start(bf16[384,256]{1,0:T(8,128)(2,1)} %args_0_.4), channel_id=1, source_target_pairs={{0,24},{8,16},{16,8},{24,0},{1,25},{9,17},{17,9},{25,1},{2,26},{10... | collective-permute-start | bytes 589832 | tf_op jit(solution)/shard_map/ppermute | solution.py:140
  21.0 17.5 %collective-permute-start.1 = (bf16[384,256]{1,0:T(8,128)(2,1)}, bf16[384,256]{1,0:T(8,128)(2,1)}, u32[]{:S(2)}, u32[]{:S(2)}) collective-permute-start(bf16[384,256]{1,0:T(8,128)(2,1)} %args_0_.4), channel_id=1, source_target_pairs={{0,16},{8,24},{16,0},{24,8},{1,17},{9,25},{17,1},{25,9},{2,18},{10... | collective-permute-start | bytes 589832 | tf_op jit(solution)/shard_map/ppermute | solution.py:140
  21.0 17.5 %collective-permute-start = (bf16[384,256]{1,0:T(8,128)(2,1)}, bf16[384,256]{1,0:T(8,128)(2,1)}, u32[]{:S(2)}, u32[]{:S(2)}) collective-permute-start(bf16[384,256]{1,0:T(8,128)(2,1)} %args_0_.4), channel_id=1, source_target_pairs={{0,8},{8,0},{16,24},{24,16},{1,9},{9,1},{17,25},{25,17},{2,10},{10... | collective-permute-start | bytes 589832 | tf_op jit(solution)/shard_map/ppermute | solution.py:140
  23.3 1.0 %copy-start.8 = (bf16[1536,384]{1,0:T(8,128)(2,1)}, bf16[1536,384]{1,0:T(8,128)(2,1)S(1)}, u32[]{:S(2)}) copy-start(bf16[1536,384]{1,0:T(8,128)(2,1)S(1)} %get-tuple-element.20.at_ref) | copy-start | bytes 3538948
  24.4 0.9 %copy-start.10 = (bf16[3,9,128,128]{3,2,1,0:T(8,128)(2,1)}, bf16[3,9,128,128]{3,2,1,0:T(8,128)(2,1)S(1)}, u32[]{:S(2)}) copy-start(bf16[3,9,128,128]{3,2,1,0:T(8,128)(2,1)S(1)} %get-tuple-element.16.offt_ref) | copy-start | bytes 2654212
  38.5 0.9 %copy-start.3 = (bf16[384,256]{1,0:T(8,128)(2,1)S(1)}, bf16[384,256]{1,0:T(8,128)(2,1)}, u32[]{:S(2)}) copy-start(bf16[384,256]{1,0:T(8,128)(2,1)} %args_0_.4) | copy-start | bytes 589828
  39.5 0.9 %copy-start.4 = (bf16[384,256]{1,0:T(8,128)(2,1)S(1)}, bf16[384,256]{1,0:T(8,128)(2,1)}, u32[]{:S(2)}) copy-start(bf16[384,256]{1,0:T(8,128)(2,1)} %args_9_.1) | copy-start | bytes 589828
  40.4 3.9 %copy-start.11 = (bf16[3,9,128,128]{3,2,1,0:T(8,128)(2,1)S(1)}, bf16[3,9,128,128]{3,2,1,0:T(8,128)(2,1)}, u32[]{:S(2)}) copy-start(bf16[3,9,128,128]{3,2,1,0:T(8,128)(2,1)} %copy-done.10) | copy-start | bytes 2654212
  46.4 0.7 copy-start.12
  47.1 4.0 %copy-start.9 = (bf16[1536,384]{1,0:T(8,128)(2,1)S(1)}, bf16[1536,384]{1,0:T(8,128)(2,1)}, u32[]{:S(2)}) copy-start(bf16[1536,384]{1,0:T(8,128)(2,1)} %copy-done.8) | copy-start | bytes 3538948
  47.1 15.2 %all-to-all-start.2 = ((bf16[8,160,256]{2,1,0:T(8,128)(2,1)}), bf16[8,160,256]{2,1,0:T(8,128)(2,1)S(1)}, u32[]{:S(2)}, u32[]{:S(2)}) async-start(bf16[8,160,256]{2,1,0:T(8,128)(2,1)} %outer.1), calls=%async_computation.2 | async-start | bytes 1310720 | tf_op jit(solution)/shard_map/all_to_all | solution.py:160
  51.1 0.9 %copy-start.13 = (bf16[384,256]{1,0:T(8,128)(2,1)S(1)}, bf16[384,256]{1,0:T(8,128)(2,1)}, u32[]{:S(2)}) copy-start(bf16[384,256]{1,0:T(8,128)(2,1)} %copy-done.12) | copy-start | bytes 589828
  52.6 12.2 %collective-permute-start.3 = (bf16[384,256]{1,0:T(8,128)(2,1)S(1)}, bf16[384,256]{1,0:T(8,128)(2,1)S(1)}, u32[]{:S(2)}, u32[]{:S(2)}) collective-permute-start(bf16[384,256]{1,0:T(8,128)(2,1)S(1)} %get-tuple-element.22), channel_id=1, source_target_pairs={{8,0},{0,8},{24,16},{16,24},{9,1},{1,9},{25,17},{17,25},{10,2},{2,... | collective-permute-start | bytes 589832 | tf_op jit(solution)/shard_map/ppermute | solution.py:156
  52.7 17.9 %collective-permute-start.4 = (bf16[384,256]{1,0:T(8,128)(2,1)S(1)}, bf16[384,256]{1,0:T(8,128)(2,1)S(1)}, u32[]{:S(2)}, u32[]{:S(2)}) collective-permute-start(bf16[384,256]{1,0:T(8,128)(2,1)S(1)} %get-tuple-element.23), channel_id=1, source_target_pairs={{16,0},{24,8},{0,16},{8,24},{17,1},{25,9},{1,17},{9,25},{18,2},{26... | collective-permute-start | bytes 589832 | tf_op jit(solution)/shard_map/ppermute | solution.py:156
  55.7 14.9 %collective-permute-start.5 = (bf16[384,256]{1,0:T(8,128)(2,1)S(1)}, bf16[384,256]{1,0:T(8,128)(2,1)S(1)}, u32[]{:S(2)}, u32[]{:S(2)}) collective-permute-start(bf16[384,256]{1,0:T(8,128)(2,1)S(1)} %get-tuple-element.24), channel_id=1, source_target_pairs={{24,0},{16,8},{8,16},{0,24},{25,1},{17,9},{9,17},{1,25},{26,2},{18... | collective-permute-start | bytes 589832 | tf_op jit(solution)/shard_map/ppermute | solution.py:156
  62.3 9.8 %collective-permute-start.8 = (bf16[32,256]{1,0:T(8,128)(2,1)S(1)}, bf16[32,256]{1,0:T(8,128)(2,1)S(1)}, u32[]{:S(2)}, u32[]{:S(2)}) collective-permute-start(bf16[32,256]{1,0:T(8,128)(2,1)S(1)} %weight.1), channel_id=1, source_target_pairs={{0,24},{8,16},{16,8},{24,0},{1,25},{9,17},{17,9},{25,1},{2,26},{10... | collective-permute-start | bytes 49160 | tf_op jit(solution)/shard_map/ppermute | solution.py:162
  64.8 10.3 %collective-permute-start.7 = (bf16[32,256]{1,0:T(8,128)(2,1)S(1)}, bf16[32,256]{1,0:T(8,128)(2,1)S(1)}, u32[]{:S(2)}, u32[]{:S(2)}) collective-permute-start(bf16[32,256]{1,0:T(8,128)(2,1)S(1)} %weight.1), channel_id=1, source_target_pairs={{0,16},{8,24},{16,0},{24,8},{1,17},{9,25},{17,1},{25,9},{2,18},{10... | collective-permute-start | bytes 49160 | tf_op jit(solution)/shard_map/ppermute | solution.py:162
  64.8 10.3 %collective-permute-start.6 = (bf16[32,256]{1,0:T(8,128)(2,1)S(1)}, bf16[32,256]{1,0:T(8,128)(2,1)S(1)}, u32[]{:S(2)}, u32[]{:S(2)}) collective-permute-start(bf16[32,256]{1,0:T(8,128)(2,1)S(1)} %weight.1), channel_id=1, source_target_pairs={{0,8},{8,0},{16,24},{24,16},{1,9},{9,1},{17,25},{25,17},{2,10},{10... | collective-permute-start | bytes 49160 | tf_op jit(solution)/shard_map/ppermute | solution.py:162

commit v2 on v1

v2 whole, which is shorter than its diff:
```python
import functools
import math

import jax
import jax.numpy as jnp
from jax import lax
from jax.experimental import pallas as pl
from jax.experimental.pallas import tpu as pltpu
from jax.sharding import PartitionSpec as P

F32, BF16 = jnp.float32, jnp.bfloat16
ROOT = math.sqrt(2.0 / math.pi)
CUBIC = 0.044715


def swapped(value, axis, k):
    return lax.ppermute(value, axis, [(i, i ^ k) for i in range(lax.axis_size(axis))])


def after(value, other):
    return value if other is None else lax.optimization_barrier((value, other))[0]


def fenced(sure, body, *args):
    blank = lambda *args: jax.tree.map(lambda s: jnp.zeros(s.shape, s.dtype), jax.eval_shape(body, *args))
    return lax.cond(sure, body, blank, *args)


def call(body, outs, args, kinds, scratch=(), flops=0, name=None):
    spaces = {"s": pltpu.SMEM, "v": pltpu.VMEM, "h": pltpu.HBM}
    nbytes = sum(math.prod(a.shape) * a.dtype.itemsize for a in (*args, *outs))
    work = sum(math.prod(s.shape) * jnp.dtype(s.dtype).itemsize for s in scratch if s.memory_space == pltpu.VMEM)
    return pl.pallas_call(
        body,
        out_shape=outs,
        in_specs=[pl.BlockSpec(memory_space=spaces[k]) for k in kinds],
        out_specs=[pl.BlockSpec(memory_space=pltpu.VMEM) for _ in outs],
        scratch_shapes=list(scratch),
        cost_estimate=pl.CostEstimate(flops=flops, bytes_accessed=nbytes, transcendentals=0),
        compiler_params=pltpu.CompilerParams(vmem_limit_bytes=nbytes + work + (4 << 20)),
        name=name,
    )(*args)


def arrange(count, me_ref, cols_ref, in_hbm, off_hbm, a_ref, at_ref, offt_ref, in_ref, off_ref, in_sem, off_sem):
    blocks, _, pairs, edge, _ = in_ref.shape
    rows = blocks * edge
    in_copies = [pltpu.make_async_copy(in_hbm.at[b], in_ref.at[b], in_sem.at[b]) for b in range(blocks)]
    off_copies = [pltpu.make_async_copy(off_hbm.at[b], off_ref.at[b], off_sem.at[b]) for b in range(blocks)]
    for copy in in_copies + off_copies:
        copy.start()
    a_ref[...] = jnp.zeros_like(a_ref)
    at_ref[...] = jnp.zeros_like(at_ref)
    for b in range(blocks):
        in_copies[b].wait()
        for n in range(count):
            s = me_ref[0] ^ n
            for k in range(pairs):
                tile = in_ref[b, s, k]
                start = pl.multiple_of(n * rows + cols_ref[b, k, s] * edge, edge)
                a_ref[b * edge:(b + 1) * edge, pl.ds(start, edge)] = tile
                at_ref[pl.ds(start, edge), b * edge:(b + 1) * edge] = tile.T
    for b in range(blocks):
        off_copies[b].wait()
        for k in range(off_ref.shape[1]):
            offt_ref[b, k] = off_ref[b, k].T


def layer(count, doms, me_ref, want_ref, refs_ref, *args):
    panels, others = args[:count], args[count:count + doms - 1]
    (a_ref, at_ref, off_ref, weight_ref, bias_ref, cot_ref,
     act_ref, grad_ref, term_ref, *outs, agg_ref, pre_ref, block_ref) = args[count + doms - 1:]
    blocks, tiles, edge, _ = off_ref.shape
    rows, cap = blocks * edge, want_ref.shape[0]
    for n in range(1, doms):
        f = me_ref[1] ^ n
        for c in range(cap):
            block_ref[f * cap + c] = others[n - 1][pl.ds(pl.multiple_of(want_ref[c, f] * edge, edge), edge), :]
    for b in range(blocks):
        part = slice(b * edge, (b + 1) * edge)
        total = jnp.zeros((edge, weight_ref.shape[0]), F32)
        for n in range(count):
            total += jnp.dot(a_ref[part, n * rows:(n + 1) * rows], panels[n][...], preferred_element_type=F32)
        for k in range(0, tiles, 2):
            ks = range(k, min(k + 2, tiles))
            left = jnp.concatenate([off_ref[b, i] for i in ks], axis=1)
            right = jnp.concatenate([block_ref[refs_ref[b, i]] for i in ks], axis=0)
            total += jnp.dot(left, right, preferred_element_type=F32)
        agg = total.astype(BF16)
        agg_ref[part, :] = agg
        v = jnp.dot(agg, weight_ref[...], preferred_element_type=F32) + bias_ref[...]
        t = jnp.tanh(ROOT * (v + CUBIC * (v * v * v)))
        act_ref[part, :] = (0.5 * v * (1.0 + t)).astype(BF16)
        slope = 0.5 * (1.0 + t) + 0.5 * v * (1.0 - t * t) * (ROOT * (1.0 + 3.0 * CUBIC * (v * v)))
        grad = (cot_ref[part, :].astype(F32) * slope).astype(BF16)
        pre_ref[part, :] = grad
        grad_ref[part, :] = lax.dot_general(
            grad, weight_ref[...], (((1,), (1,)), ((), ())), preferred_element_type=F32).astype(BF16)

    term_ref[...] = lax.dot_general(
        agg_ref[...], pre_ref[...], (((0,), (0,)), ((), ())), preferred_element_type=F32).astype(BF16)
    for n in range(count):
        outs[n][...] = jnp.dot(at_ref[n * rows:(n + 1) * rows, :], grad_ref[...], preferred_element_type=F32).astype(BF16)


def spread_outer(want_ref, refs_ref, offt_ref, grad_ref, out_ref, total_ref):
    blocks, tiles, edge, _ = offt_ref.shape
    cap, doms = want_ref.shape
    total_ref[...] = jnp.zeros_like(total_ref)
    for b in range(blocks):
        grad = grad_ref[b * edge:(b + 1) * edge, :]
        for k in range(tiles):
            total_ref[refs_ref[b, k]] += jnp.dot(offt_ref[b, k], grad, preferred_element_type=F32)
    for f in range(doms):
        for c in range(cap):
            out_ref[f, c * edge:(c + 1) * edge, :] = total_ref[f * cap + c].astype(BF16)
            top = cap * edge + c * 16
            out_ref[f, top:top + 16, :] = jnp.full((16, out_ref.shape[2]), want_ref[c, f], jnp.int32).astype(BF16)


def joined(part, axis, k):
    return (part.astype(F32) + swapped(part, axis, k).astype(F32)).astype(BF16)


def finish(cap, edge, coming_ref, *args):
    terms, out_ref = args[:-1], args[-1]
    for j in range(out_ref.shape[0] // edge):
        part = slice(j * edge, (j + 1) * edge)
        total = terms[0][part, :].astype(F32)
        for ref in terms[1:]:
            total += ref[part, :].astype(F32)
        for f in range(coming_ref.shape[0]):
            for c in range(cap):
                top = cap * edge + c * 16
                place = coming_ref[f, top:top + 1, :].astype(F32)
                total += jnp.where(place == j, coming_ref[f, c * edge:(c + 1) * edge, :].astype(F32), 0.0)
        out_ref[part, :] = total.astype(BF16)


def local(feats, cotangent, weight, bias, in_vals, in_cols, off_vals, off_ref, want):
    count, doms = lax.axis_size("rep"), lax.axis_size("dom")
    me = jnp.stack([lax.axis_index("rep"), lax.axis_index("dom")]).astype(jnp.int32)
    blocks, _, _, edge, _ = in_vals.shape
    rows, width = feats.shape
    requests = want.transpose(0, 1, 3, 2).reshape(want.shape[3], want.shape[2])
    cap = requests.shape[0]
    share = width // doms
    shape = jax.ShapeDtypeStruct
    flat = shape((rows, width), BF16)

    slots = doms * cap
    piece = shape((share, width), BF16)
    sure = requests[0, 0] >= 0
    scale = 1.0 / math.sqrt(rows * count * doms)

    def exchange(outer, term):
        coming = lax.all_to_all(outer, "dom", split_axis=0, concat_axis=0, tiled=True)
        k = 1
        while k < doms:
            term, k = joined(term, "dom", k), 2 * k
        k = 1
        while 2 * k < count:
            term, k = joined(term, "rep", k), 2 * k
        return coming, term

    panels = [feats] + [swapped(feats, "rep", k) for k in range(1, count)]
    even = [feats] + [swapped(feats, "dom", k) for k in range(2, doms, 2)]
    dma = pltpu.SemaphoreType.DMA((blocks,))
    a, at, offt = call(
        functools.partial(arrange, count),
        [shape((rows, count * rows), BF16), shape((count * rows, rows), BF16), shape(off_vals.shape, BF16)],
        (after(me, even[2]), in_cols.transpose(0, 2, 1), in_vals, off_vals), "sshh",
        scratch=[pltpu.VMEM(in_vals.shape, BF16), pltpu.VMEM(off_vals.shape, BF16), dma, dma], name="arrange")
    odd = [swapped(after(value, offt), "dom", 1) for value in even]
    others = [value for pair in zip(even, odd) for value in pair][1:]
    activated, grad_agg, term, *terms = call(
        functools.partial(layer, count, doms), [flat] * 2 + [shape((width, width), BF16)] + [flat] * count,
        (me, requests, off_ref, *panels, *others, a, at, off_vals, weight, bias.reshape(1, width), cotangent),
        "sss" + "v" * (count + doms + 5),
        scratch=[pltpu.VMEM((rows, width), BF16)] * 2 + [pltpu.VMEM((slots, edge, width), BF16)],
        flops=10**9, name="layer")
    got = [terms[0]] + [swapped(terms[k], "rep", k) for k in range(1, count)]
    outer = call(
        spread_outer, [shape((doms, cap * (edge + 16), width), BF16)], (requests, off_ref, offt, grad_agg), "ssvv",
        scratch=[pltpu.VMEM((slots, edge, width), F32)], flops=10**9, name="outer")[0]
    coming, term = fenced(sure, exchange, outer, term)
    term, *got = lax.optimization_barrier((term, *got))
    grad_weight = ((term.astype(F32) + swapped(term, "rep", count // 2).astype(F32)) * scale).astype(BF16)
    grad_feats = call(functools.partial(finish, cap, edge), [flat], (coming, *got), "v" * (count + 1), name="finish")[0]
    return (activated, grad_feats, grad_weight)


def solution(mesh):
    in_specs = (
        P(("rep", "dom"), None),
        P(("rep", "dom"), None),
        P(),
        P(),
        P(("rep", "dom"), None, None, None, None),
        P(("rep", "dom"), None, None),
        P(("rep", "dom"), None, None, None),
        P(("rep", "dom"), None),
        P("rep", "dom", None, None),
    )
    out_specs = (P(("rep", "dom"), None), P(("rep", "dom"), None), P())
    return jax.shard_map(local, mesh=mesh, in_specs=in_specs, out_specs=out_specs, check_vma=False)
```

time: 85.6 us -> 68.1 us (0.80)
  blocking collectives: 19 us -> 0 us
  starting transfers between devices: 21 us -> 26.4 us
  local copies, waits for them, and re-layouts: 7.96 us -> 3.01 us
  waiting for transfers between devices: 25.3 us -> 26.3 us
    all_to_all x1 -> x0, blocking collectives: 9.62 us -> none  [local(): lax.all_to_all(requests, 'dom', split_axis=0, concat_axis=0, tiled=True)]
    all_gather x1 -> x0, blocking collectives: 9.38 us -> none  [local(): grad_weight = lax.all_gather(whole, 'dom', axis=0, tiled=True)]
    ppermute x9 -> x18, starting transfers between devices: 13.4 us -> 22.2 us  [swapped(): lax.ppermute(value, axis, [(i, i ^ k) for i in range(lax.axis_size(axis))])]
    unnamed x32 -> x20, local copies, waits for them, and re-layouts: 7.11 us -> 3.01 us
    all_to_all x2 -> x1, starting transfers between devices: 7.63 us -> 4.19 us  [exchange(): lax.all_to_all(outer, 'dom', split_axis=0, concat_axis=0, tiled=True)]
    ppermute x9 -> x18, waiting for transfers between devices: 20.1 us -> 21.8 us  [swapped(): lax.ppermute(value, axis, [(i, i ^ k) for i in range(lax.axis_size(axis))])]
    all_to_all x2 -> x1, waiting for transfers between devices: 5.19 us -> 4.53 us  [exchange(): lax.all_to_all(outer, 'dom', split_axis=0, concat_axis=0, tiled=True)]
    pallas_call x7 -> x4, Pallas kernels: 10.8 us -> 10.3 us  [call(): pl.pallas_call(body, out_shape=outs, in_specs=[pl.BlockSpec(memory_space=...]
  transfers between devices with their start and end apart: 11 -> 19, of which waited for: 5 -> 7; matrix products, arithmetic and copies ran while one was open for 0% -> 0% of each run, Pallas kernels for 4% -> 9%
where the time goes in v2:
time: 68.1 us; the launch traced here: 67.7 us
  starting transfers between devices  26.4 us (39%)
  waiting for transfers between devices  26.3 us (39%)
  Pallas kernels  10.3 us (15%)
  local copies, waits for them, and re-layouts  3.01 us (4%)
  other arithmetic  0.91 us (1%)
  between operations  0.81 us (1%)
    ppermute x18, starting transfers between devices, swapped(): lax.ppermute(value, axis, [(i, i ^ k) for i in range(lax.axis_size(axis))])  22.2 us
    ppermute x18, waiting for transfers between devices, swapped(): lax.ppermute(value, axis, [(i, i ^ k) for i in range(lax.axis_size(axis))])  21.8 us
    pallas_call x4, Pallas kernels, call(): pl.pallas_call(body, out_shape=outs, in_specs=[pl.BlockSpec(memory_space=...  10.3 us
    all_to_all x1, waiting for transfers between devices, exchange(): lax.all_to_all(outer, 'dom', split_axis=0, concat_axis=0, tiled=True)  4.53 us
    all_to_all x1, starting transfers between devices, exchange(): lax.all_to_all(outer, 'dom', split_axis=0, concat_axis=0, tiled=True)  4.19 us
    unnamed x20, local copies, waits for them, and re-layouts  3.01 us
  transfers between devices with their start and end apart: 19, of which 7 were waited for; matrix products, arithmetic and copies ran while one was open for 0% of the time, Pallas kernels for 9%

profile of v2, /device:TPU:0, one launch (start us, length us, event | category | flops | bytes accessed | tf_op | source)
XLA Modules:
  0.0 67.7 jit_solution(1229770178661006779)
XLA Ops:
  0.7 3.0 %collective-permute-start.7 = (bf16[384,256]{1,0:T(8,128)(2,1)}, bf16[384,256]{1,0:T(8,128)(2,1)S(1)}, u32[]{:S(2)}, u32[]{:S(2)}) collective-permute-start(bf16[384,256]{1,0:T(8,128)(2,1)} %args_0_.4), channel_id=1, source_target_pairs={{0,4},{1,5},{2,6},{3,7},{4,0},{5,1},{6,2},{7,3},{8,12},{9,13},{10,... | collective-permute-start | bytes 589832 | tf_op jit(solution)/shard_map/ppermute | solution.py:17
  3.7 1.5 %collective-permute-start.9 = (bf16[384,256]{1,0:T(8,128)(2,1)}, bf16[384,256]{1,0:T(8,128)(2,1)S(1)}, u32[]{:S(2)}, u32[]{:S(2)}) collective-permute-start(bf16[384,256]{1,0:T(8,128)(2,1)} %args_0_.4), channel_id=1, source_target_pairs={{0,2},{1,3},{2,0},{3,1},{4,6},{5,7},{6,4},{7,5},{8,10},{9,11},{10,... | collective-permute-start | bytes 589832 | tf_op jit(solution)/shard_map/ppermute | solution.py:17
  5.2 2.0 %collective-permute-start.4 = (bf16[384,256]{1,0:T(8,128)(2,1)}, bf16[384,256]{1,0:T(8,128)(2,1)S(1)}, u32[]{:S(2)}, u32[]{:S(2)}) collective-permute-start(bf16[384,256]{1,0:T(8,128)(2,1)} %args_0_.4), channel_id=1, source_target_pairs={{0,8},{8,0},{16,24},{24,16},{1,9},{9,1},{17,25},{25,17},{2,10},{10... | collective-permute-start | bytes 589832 | tf_op jit(solution)/shard_map/ppermute | solution.py:17
  7.2 2.6 %collective-permute-start.5 = (bf16[384,256]{1,0:T(8,128)(2,1)}, bf16[384,256]{1,0:T(8,128)(2,1)S(1)}, u32[]{:S(2)}, u32[]{:S(2)}) collective-permute-start(bf16[384,256]{1,0:T(8,128)(2,1)} %args_0_.4), channel_id=1, source_target_pairs={{0,16},{8,24},{16,0},{24,8},{1,17},{9,25},{17,1},{25,9},{2,18},{10... | collective-permute-start | bytes 589832 | tf_op jit(solution)/shard_map/ppermute | solution.py:17
  9.8 0.1 pad_add_fusion.me_ref
  9.9 3.0 %collective-permute-start.6 = (bf16[384,256]{1,0:T(8,128)(2,1)}, bf16[384,256]{1,0:T(8,128)(2,1)S(1)}, u32[]{:S(2)}, u32[]{:S(2)}) collective-permute-start(bf16[384,256]{1,0:T(8,128)(2,1)} %args_0_.4), channel_id=1, source_target_pairs={{0,24},{8,16},{16,8},{24,0},{1,25},{9,17},{17,9},{25,1},{2,26},{10... | collective-permute-start | bytes 589832 | tf_op jit(solution)/shard_map/ppermute | solution.py:17
  12.9 1.2 %copy-done = bf16[3,9,128,128]{3,2,1,0:T(8,128)(2,1)S(1)} copy-done((bf16[3,9,128,128]{3,2,1,0:T(8,128)(2,1)S(1)}, bf16[3,9,128,128]{3,2,1,0:T(8,128)(2,1)}, u32[]{:S(2)}) %copy-start) | copy-done | bytes 884760
  14.1 1.1 %copy-done.2 = bf16[3,4,2,128,128]{4,3,2,1,0:T(8,128)(2,1)S(1)} copy-done((bf16[3,4,2,128,128]{4,3,2,1,0:T(8,128)(2,1)S(1)}, bf16[3,4,2,128,128]{4,3,2,1,0:T(8,128)(2,1)}, u32[]{:S(2)}) %copy-start.2) | copy-done | bytes 786456
  15.2 0.7 %copy-done.6 = s32[3,4,2]{1,2,0:T(2,128)S(1)} copy-done((s32[3,4,2]{1,2,0:T(2,128)S(1)}, s32[3,4,2]{1,2,0:T(2,128)}, u32[]{:S(2)}) %copy-start.6) | copy-done | bytes 120
  15.9 1.9 %arrange.1 = (bf16[384,1536]{1,0:T(8,128)(2,1)S(1)}, bf16[1536,384]{1,0:T(8,128)(2,1)S(1)}, bf16[3,9,128,128]{3,2,1,0:T(8,128)(2,1)S(1)}) custom-call(s32[2]{0:T(128)S(1)} %pad_add_fusion.me_ref, s32[3,2,4]{2,1,0:T(2,128)S(1)} %bitcast.7, bf16[3,4,2,128,128]{4,3,2,1,0:T(8,128)(2,1)S(1)} %copy-done.2, bf16[3,9,128,128]{3,2,1,0:T(8,128)(2,1)S(1)} %copy-done), custom_call_target="tpu_custom_call" | custom-call | bytes 4915304 | tf_op jit(solution)/shard_map/arrange/pallas_call | solution.py:33
  17.9 0.5 collective-permute-start.10
  18.4 0.1 collective-permute-start.13
  18.5 6.0 %collective-permute-done.5.args_2_ = bf16[384,256]{1,0:T(8,128)(2,1)S(1)} collective-permute-done((bf16[384,256]{1,0:T(8,128)(2,1)}, bf16[384,256]{1,0:T(8,128)(2,1)S(1)}, u32[]{:S(2)}, u32[]{:S(2)}) %collective-permute-start.5) | collective-permute-done | bytes 196640 | tf_op jit(solution)/shard_map/ppermute | solution.py:17
  24.5 1.4 %collective-permute-done.8.args_4_ = bf16[384,256]{1,0:T(8,128)(2,1)S(1)} collective-permute-done((bf16[384,256]{1,0:T(8,128)(2,1)S(1)}, bf16[384,256]{1,0:T(8,128)(2,1)S(1)}, u32[]{:S(2)}, u32[]{:S(2)}) %collective-permute-start.8) | collective-permute-done | bytes 196640 | tf_op jit(solution)/shard_map/ppermute | solution.py:17
  26.0 4.1 %layer.1 = (bf16[384,256]{1,0:T(8,128)(2,1)}, bf16[384,256]{1,0:T(8,128)(2,1)S(1)}, bf16[256,256]{1,0:T(8,128)(2,1)S(1)}, bf16[384,256]{1,0:T(8,128)(2,1)S(1)}, ...) custom-call(s32[2]{0:T(128)S(1)} %pad_add_fusion.me_ref, ...), custom_call_target="tpu_custom_call" | custom-call | flops 1000000000 | bytes 7046292 | tf_op jit(solution)/shard_map/layer/pallas_call | solution.py:33
  30.1 1.3 %collective-permute-start.14 = (bf16[384,256]{1,0:T(8,128)(2,1)S(1)}, bf16[384,256]{1,0:T(8,128)(2,1)S(1)}, u32[]{:S(2)}, u32[]{:S(2)}) collective-permute-start(bf16[384,256]{1,0:T(8,128)(2,1)S(1)} %get-tuple-element.45), channel_id=1, source_target_pairs={{0,8},{8,0},{16,24},{24,16},{1,9},{9,1},{17,25},{25,17},{2,10},{10... | collective-permute-start | bytes 589832 | tf_op jit(solution)/shard_map/ppermute | solution.py:17
  31.3 1.3 %collective-permute-start.15 = (bf16[384,256]{1,0:T(8,128)(2,1)S(1)}, bf16[384,256]{1,0:T(8,128)(2,1)S(1)}, u32[]{:S(2)}, u32[]{:S(2)}) collective-permute-start(bf16[384,256]{1,0:T(8,128)(2,1)S(1)} %get-tuple-element.46), channel_id=1, source_target_pairs={{0,16},{8,24},{16,0},{24,8},{1,17},{9,25},{17,1},{25,9},{2,18},{10... | collective-permute-start | bytes 589832 | tf_op jit(solution)/shard_map/ppermute | solution.py:17
  32.6 1.8 %collective-permute-start.16 = (bf16[384,256]{1,0:T(8,128)(2,1)S(1)}, bf16[384,256]{1,0:T(8,128)(2,1)S(1)}, u32[]{:S(2)}, u32[]{:S(2)}) collective-permute-start(bf16[384,256]{1,0:T(8,128)(2,1)S(1)} %get-tuple-element.47), channel_id=1, source_target_pairs={{0,24},{8,16},{16,8},{24,0},{1,25},{9,17},{17,9},{25,1},{2,26},{10... | collective-permute-start | bytes 589832 | tf_op jit(solution)/shard_map/ppermute | solution.py:17
  34.5 2.1 %outer.1 = bf16[8,144,256]{2,1,0:T(8,128)(2,1)} custom-call(s32[1,8]{1,0:T(1,128)S(1)} %bitcast.11, s32[3,9]{1,0:T(4,128)S(1)} %copy-done.7, bf16[3,9,128,128]{3,2,1,0:T(8,128)(2,1)S(1)} %get-tuple-element.32.offt_ref, bf16[384,256]{1,0:T(8,128)(2,1)S(1)} %get-tuple-element.40.grad_ref), custom_call_target="tpu_custom_call" | custom-call | flops 1000000000 | bytes 1671308 | tf_op jit(solution)/shard_map/outer/pallas_call | solution.py:33
  36.6 23.3 %conditional.1 = (bf16[8,144,256]{2,1,0:T(8,128)(2,1)}, bf16[256,256]{1,0:T(8,128)(2,1)S(1)}) conditional(s32[]{:T(128)} %bitcast.5, () %tuple.27, (bf16[8,144,256]{2,1,0:T(8,128)(2,1)}, bf16[256,256]{1,0:T(8,128)(2,1)S(1)}) %tuple.28), branch_computations={%region_0.0_spmd, %region_1.0_spmd} | conditional | flops 1048576 | bytes 5439696 | solution.py:26
  36.6 1.3 %collective-permute-done = bf16[256,256]{1,0:T(8,128)(2,1)S(1)} collective-permute-done((bf16[256,256]{1,0:T(8,128)(2,1)S(1)}, bf16[256,256]{1,0:T(8,128)(2,1)S(1)}, u32[]{:S(2)}, u32[]{:S(2)}) %collective-permute-start) | collective-permute-done | bytes 131104 | tf_op jit(solution)/shard_map/cond/branch_1_fun/ppermute | solution.py:17
  38.0 1.6 %collective-permute-start.1 = (bf16[256,256]{1,0:T(8,128)(2,1)S(1)}, bf16[256,256]{1,0:T(8,128)(2,1)S(1)}, u32[]{:S(2)}, u32[]{:S(2)}) collective-permute-start(bf16[256,256]{1,0:T(8,128)(2,1)S(1)} %add_convert_fusion.3), channel_id=1, source_target_pairs={{0,2},{1,3},{2,0},{3,1},{4,6},{5,7},{6,4},{7,5},{8,10},{9,11},{10,... | collective-permute-start | bytes 393224 | tf_op jit(solution)/shard_map/cond/branch_1_fun/ppermute | solution.py:17
  39.6 4.1 %collective-permute-done.1 = bf16[256,256]{1,0:T(8,128)(2,1)S(1)} collective-permute-done((bf16[256,256]{1,0:T(8,128)(2,1)S(1)}, bf16[256,256]{1,0:T(8,128)(2,1)S(1)}, u32[]{:S(2)}, u32[]{:S(2)}) %collective-permute-start.1) | collective-permute-done | bytes 131104 | tf_op jit(solution)/shard_map/cond/branch_1_fun/ppermute | solution.py:17
  43.7 1.6 %collective-permute-start.2 = (bf16[256,256]{1,0:T(8,128)(2,1)S(1)}, bf16[256,256]{1,0:T(8,128)(2,1)S(1)}, u32[]{:S(2)}, u32[]{:S(2)}) collective-permute-start(bf16[256,256]{1,0:T(8,128)(2,1)S(1)} %add_convert_fusion.2), channel_id=1, source_target_pairs={{0,4},{1,5},{2,6},{3,7},{4,0},{5,1},{6,2},{7,3},{8,12},{9,13},{10,... | collective-permute-start | bytes 393224 | tf_op jit(solution)/shard_map/cond/branch_1_fun/ppermute | solution.py:17
  45.2 4.2 %all-to-all-start = ((bf16[8,144,256]{2,1,0:T(8,128)(2,1)}), bf16[8,144,256]{2,1,0:T(8,128)(2,1)}, u32[]{:S(2)}, u32[]{:S(2)}) async-start(bf16[8,144,256]{2,1,0:T(8,128)(2,1)} %get-tuple-element.4), calls=%async_computation | async-start | bytes 1179648 | tf_op jit(solution)/shard_map/cond/branch_1_fun/all_to_all | solution.py:157
  49.5 0.4 collective-permute-start.3
  49.9 5.4 %collective-permute-done.3 = bf16[256,256]{1,0:T(8,128)(2,1)S(1)} collective-permute-done((bf16[256,256]{1,0:T(8,128)(2,1)S(1)}, bf16[256,256]{1,0:T(8,128)(2,1)S(1)}, u32[]{:S(2)}, u32[]{:S(2)}) %collective-permute-start.3) | collective-permute-done | bytes 131104 | tf_op jit(solution)/shard_map/cond/branch_1_fun/ppermute | solution.py:17
  55.4 4.5 %all-to-all-done = bf16[8,144,256]{2,1,0:T(8,128)(2,1)} async-done(((bf16[8,144,256]{2,1,0:T(8,128)(2,1)}), bf16[8,144,256]{2,1,0:T(8,128)(2,1)}, u32[]{:S(2)}, u32[]{:S(2)}) %all-to-all-start) | async-done | bytes 589856 | tf_op jit(solution)/shard_map/cond/branch_1_fun/all_to_all | solution.py:157
  59.9 1.4 %collective-permute-start.17 = (bf16[256,256]{1,0:T(8,128)(2,1)S(1)}, bf16[256,256]{1,0:T(8,128)(2,1)S(1)}, u32[]{:S(2)}, u32[]{:S(2)}) collective-permute-start(bf16[256,256]{1,0:T(8,128)(2,1)S(1)} %get-tuple-element.52), channel_id=1, source_target_pairs={{0,16},{8,24},{16,0},{24,8},{1,17},{9,25},{17,1},{25,9},{2,18},{10... | collective-permute-start | bytes 393224 | tf_op jit(solution)/shard_map/ppermute | solution.py:17
  61.3 2.2 %finish.1 = bf16[384,256]{1,0:T(8,128)(2,1)} custom-call(bf16[8,144,256]{2,1,0:T(8,128)(2,1)} %get-tuple-element.42.coming_ref, bf16[384,256]{1,0:T(8,128)(2,1)S(1)} %get-tuple-element.48.args_0_, bf16[384,256]{1,0:T(8,128)(2,1)S(1)} %collective-permute-done.14.args_1_, bf16[384,256]{1,0:T(8,128)(2,1)S(1)} %collective-permute-done.15.args_2_, ...), custom_call_target="tpu_custom_call" | custom-call | bytes 1572864 | tf_op jit(solution)/shard_map/finish/pallas_call | solution.py:33
  63.5 3.5 %collective-permute-done.17 = bf16[256,256]{1,0:T(8,128)(2,1)S(1)} collective-permute-done((bf16[256,256]{1,0:T(8,128)(2,1)S(1)}, bf16[256,256]{1,0:T(8,128)(2,1)S(1)}, u32[]{:S(2)}, u32[]{:S(2)}) %collective-permute-start.17) | collective-permute-done | bytes 131104 | tf_op jit(solution)/shard_map/ppermute | solution.py:17
  67.0 0.7 %multiply_convert_fusion = bf16[256,256]{1,0:T(8,128)(2,1)} fusion(bf16[256,256]{1,0:T(8,128)(2,1)S(1)} %collective-permute-done.17, bf16[256,256]{1,0:T(8,128)(2,1)S(1)} %get-tuple-element.52), kind=kLoop, calls=%fused_computation.4 | loop fusion | flops 327680 | bytes 393216 | tf_op jit(solution)/shard_map/convert_element_type | solution.py:188
  (37 shorter events, 0.3 us)
Async XLA Ops:
  0.6 25.3 %copy-start.9 = (s32[1,1,8,1]{2,3,1,0:T(1,128)S(1)}, s32[1,1,8,1]{2,3,1,0:T(1,128)}, u32[]{:S(2)}) copy-start(s32[1,1,8,1]{2,3,1,0:T(1,128)} %param.19) | copy-start | bytes 100
  0.6 25.3 %copy-start.8 = (f32[256]{0:T(256)S(1)}, f32[256]{0:T(256)}, u32[]{:S(2)}) copy-start(f32[256]{0:T(256)} %param.14) | copy-start | bytes 3076
  0.7 25.3 %copy-start.7 = (s32[3,9]{1,0:T(4,128)S(1)}, s32[3,9]{1,0:T(4,128)}, u32[]{:S(2)}) copy-start(s32[3,9]{1,0:T(4,128)} %refs_ref.3) | copy-start | bytes 328
  0.7 9.2 %collective-permute-start.7 = (bf16[384,256]{1,0:T(8,128)(2,1)}, bf16[384,256]{1,0:T(8,128)(2,1)S(1)}, u32[]{:S(2)}, u32[]{:S(2)}) collective-permute-start(bf16[384,256]{1,0:T(8,128)(2,1)} %args_0_.4), channel_id=1, source_target_pairs={{0,4},{1,5},{2,6},{3,7},{4,0},{5,1},{6,2},{7,3},{8,12},{9,13},{10,... | collective-permute-start | bytes 589832 | tf_op jit(solution)/shard_map/ppermute | solution.py:17
  3.7 14.1 %collective-permute-start.9 = (bf16[384,256]{1,0:T(8,128)(2,1)}, bf16[384,256]{1,0:T(8,128)(2,1)S(1)}, u32[]{:S(2)}, u32[]{:S(2)}) collective-permute-start(bf16[384,256]{1,0:T(8,128)(2,1)} %args_0_.4), channel_id=1, source_target_pairs={{0,2},{1,3},{2,0},{3,1},{4,6},{5,7},{6,4},{7,5},{8,10},{9,11},{10,... | collective-permute-start | bytes 589832 | tf_op jit(solution)/shard_map/ppermute | solution.py:17
  5.2 12.7 %collective-permute-start.12 = (bf16[384,256]{1,0:T(8,128)(2,1)}, bf16[384,256]{1,0:T(8,128)(2,1)S(1)}, u32[]{:S(2)}, u32[]{:S(2)}) collective-permute-start(bf16[384,256]{1,0:T(8,128)(2,1)} %args_0_.4), channel_id=1, source_target_pairs={{0,6},{1,7},{2,4},{3,5},{4,2},{5,3},{6,0},{7,1},{8,14},{9,15},{10,... | collective-permute-start | bytes 589832 | tf_op jit(solution)/shard_map/ppermute | solution.py:17
  5.2 13.1 %collective-permute-start.4 = (bf16[384,256]{1,0:T(8,128)(2,1)}, bf16[384,256]{1,0:T(8,128)(2,1)S(1)}, u32[]{:S(2)}, u32[]{:S(2)}) collective-permute-start(bf16[384,256]{1,0:T(8,128)(2,1)} %args_0_.4), channel_id=1, source_target_pairs={{0,8},{8,0},{16,24},{24,16},{1,9},{9,1},{17,25},{25,17},{2,10},{10... | collective-permute-start | bytes 589832 | tf_op jit(solution)/shard_map/ppermute | solution.py:17
  7.2 17.2 %collective-permute-start.5 = (bf16[384,256]{1,0:T(8,128)(2,1)}, bf16[384,256]{1,0:T(8,128)(2,1)S(1)}, u32[]{:S(2)}, u32[]{:S(2)}) collective-permute-start(bf16[384,256]{1,0:T(8,128)(2,1)} %args_0_.4), channel_id=1, source_target_pairs={{0,16},{8,24},{16,0},{24,8},{1,17},{9,25},{17,1},{25,9},{2,18},{10... | collective-permute-start | bytes 589832 | tf_op jit(solution)/shard_map/ppermute | solution.py:17
  9.9 14.6 %collective-permute-start.6 = (bf16[384,256]{1,0:T(8,128)(2,1)}, bf16[384,256]{1,0:T(8,128)(2,1)S(1)}, u32[]{:S(2)}, u32[]{:S(2)}) collective-permute-start(bf16[384,256]{1,0:T(8,128)(2,1)} %args_0_.4), channel_id=1, source_target_pairs={{0,24},{8,16},{16,8},{24,0},{1,25},{9,17},{17,9},{25,1},{2,26},{10... | collective-permute-start | bytes 589832 | tf_op jit(solution)/shard_map/ppermute | solution.py:17
  12.9 1.2 %copy-start = (bf16[3,9,128,128]{3,2,1,0:T(8,128)(2,1)S(1)}, bf16[3,9,128,128]{3,2,1,0:T(8,128)(2,1)}, u32[]{:S(2)}) copy-start(bf16[3,9,128,128]{3,2,1,0:T(8,128)(2,1)} %args_13_.1) | copy-start | bytes 2654212
  14.1 1.1 %copy-start.2 = (bf16[3,4,2,128,128]{4,3,2,1,0:T(8,128)(2,1)S(1)}, bf16[3,4,2,128,128]{4,3,2,1,0:T(8,128)(2,1)}, u32[]{:S(2)}) copy-start(bf16[3,4,2,128,128]{4,3,2,1,0:T(8,128)(2,1)} %in_hbm.1) | copy-start | bytes 2359300
  15.2 0.7 %copy-start.6 = (s32[3,4,2]{1,2,0:T(2,128)S(1)}, s32[3,4,2]{1,2,0:T(2,128)}, u32[]{:S(2)}) copy-start(s32[3,4,2]{1,2,0:T(2,128)} %param.16) | copy-start | bytes 292
  15.9 8.6 %copy-start.3 = (bf16[384,256]{1,0:T(8,128)(2,1)S(1)}, bf16[384,256]{1,0:T(8,128)(2,1)}, u32[]{:S(2)}) copy-start(bf16[384,256]{1,0:T(8,128)(2,1)} %args_0_.4) | copy-start | bytes 589828
  15.9 10.0 %copy-start.1 = (bf16[3,9,128,128]{3,2,1,0:T(8,128)(2,1)S(1)}, bf16[3,9,128,128]{3,2,1,0:T(8,128)(2,1)}, u32[]{:S(2)}) copy-start(bf16[3,9,128,128]{3,2,1,0:T(8,128)(2,1)} %args_13_.1) | copy-start | bytes 2654212
  15.9 10.0 %copy-start.4 = (bf16[384,256]{1,0:T(8,128)(2,1)S(1)}, bf16[384,256]{1,0:T(8,128)(2,1)}, u32[]{:S(2)}) copy-start(bf16[384,256]{1,0:T(8,128)(2,1)} %args_16_.1) | copy-start | bytes 589828
  15.9 10.0 %copy-start.5 = (bf16[256,256]{1,0:T(8,128)(2,1)S(1)}, bf16[256,256]{1,0:T(8,128)(2,1)}, u32[]{:S(2)}) copy-start(bf16[256,256]{1,0:T(8,128)(2,1)} %args_14_.1) | copy-start | bytes 393220
  17.8 6.7 %collective-permute-start.11 = (bf16[384,256]{1,0:T(8,128)(2,1)S(1)}, bf16[384,256]{1,0:T(8,128)(2,1)S(1)}, u32[]{:S(2)}, u32[]{:S(2)}) collective-permute-start(bf16[384,256]{1,0:T(8,128)(2,1)S(1)} %collective-permute-done.7.args_7_), channel_id=1, source_target_pairs={{0,1},{1,0},{2,3},{3,2},{4,5},{5,4},{6,7},{7,6},{8,9},{9,8},{10,11... | collective-permute-start | bytes 589832 | tf_op jit(solution)/shard_map/ppermute | solution.py:17
  17.9 6.6 %collective-permute-start.10 = (bf16[384,256]{1,0:T(8,128)(2,1)S(1)}, bf16[384,256]{1,0:T(8,128)(2,1)S(1)}, u32[]{:S(2)}, u32[]{:S(2)}) collective-permute-start(bf16[384,256]{1,0:T(8,128)(2,1)S(1)} %collective-permute-done.9.args_5_), channel_id=1, source_target_pairs={{0,1},{1,0},{2,3},{3,2},{4,5},{5,4},{6,7},{7,6},{8,9},{9,8},{10,11... | collective-permute-start | bytes 589832 | tf_op jit(solution)/shard_map/ppermute | solution.py:17
  18.4 6.1 %collective-permute-start.13 = (bf16[384,256]{1,0:T(8,128)(2,1)S(1)}, bf16[384,256]{1,0:T(8,128)(2,1)S(1)}, u32[]{:S(2)}, u32[]{:S(2)}) collective-permute-start(bf16[384,256]{1,0:T(8,128)(2,1)S(1)} %collective-permute-done.12.args_9_), channel_id=1, source_target_pairs={{0,1},{1,0},{2,3},{3,2},{4,5},{5,4},{6,7},{7,6},{8,9},{9,8},{10,11... | collective-permute-start | bytes 589832 | tf_op jit(solution)/shard_map/ppermute | solution.py:17
  24.5 1.4 %collective-permute-start.8 = (bf16[384,256]{1,0:T(8,128)(2,1)S(1)}, bf16[384,256]{1,0:T(8,128)(2,1)S(1)}, u32[]{:S(2)}, u32[]{:S(2)}) collective-permute-start(bf16[384,256]{1,0:T(8,128)(2,1)S(1)} %copy-done.3), channel_id=1, source_target_pairs={{0,1},{1,0},{2,3},{3,2},{4,5},{5,4},{6,7},{7,6},{8,9},{9,8},{10,11... | collective-permute-start | bytes 589832 | tf_op jit(solution)/shard_map/ppermute | solution.py:17
  30.1 29.8 %collective-permute-start.14 = (bf16[384,256]{1,0:T(8,128)(2,1)S(1)}, bf16[384,256]{1,0:T(8,128)(2,1)S(1)}, u32[]{:S(2)}, u32[]{:S(2)}) collective-permute-start(bf16[384,256]{1,0:T(8,128)(2,1)S(1)} %get-tuple-element.45), channel_id=1, source_target_pairs={{0,8},{8,0},{16,24},{24,16},{1,9},{9,1},{17,25},{25,17},{2,10},{10... | collective-permute-start | bytes 589832 | tf_op jit(solution)/shard_map/ppermute | solution.py:17
  31.3 28.6 %collective-permute-start.15 = (bf16[384,256]{1,0:T(8,128)(2,1)S(1)}, bf16[384,256]{1,0:T(8,128)(2,1)S(1)}, u32[]{:S(2)}, u32[]{:S(2)}) collective-permute-start(bf16[384,256]{1,0:T(8,128)(2,1)S(1)} %get-tuple-element.46), channel_id=1, source_target_pairs={{0,16},{8,24},{16,0},{24,8},{1,17},{9,25},{17,1},{25,9},{2,18},{10... | collective-permute-start | bytes 589832 | tf_op jit(solution)/shard_map/ppermute | solution.py:17
  32.6 27.3 %collective-permute-start.16 = (bf16[384,256]{1,0:T(8,128)(2,1)S(1)}, bf16[384,256]{1,0:T(8,128)(2,1)S(1)}, u32[]{:S(2)}, u32[]{:S(2)}) collective-permute-start(bf16[384,256]{1,0:T(8,128)(2,1)S(1)} %get-tuple-element.47), channel_id=1, source_target_pairs={{0,24},{8,16},{16,8},{24,0},{1,25},{9,17},{17,9},{25,1},{2,26},{10... | collective-permute-start | bytes 589832 | tf_op jit(solution)/shard_map/ppermute | solution.py:17
  36.6 1.3 %collective-permute-start = (bf16[256,256]{1,0:T(8,128)(2,1)S(1)}, bf16[256,256]{1,0:T(8,128)(2,1)S(1)}, u32[]{:S(2)}, u32[]{:S(2)}) collective-permute-start(bf16[256,256]{1,0:T(8,128)(2,1)S(1)} %get-tuple-element.5), channel_id=1, source_target_pairs={{0,1},{1,0},{2,3},{3,2},{4,5},{5,4},{6,7},{7,6},{8,9},{9,8},{10,11... | collective-permute-start | bytes 393224 | tf_op jit(solution)/shard_map/cond/branch_1_fun/ppermute | solution.py:17
  38.0 5.6 %collective-permute-start.1 = (bf16[256,256]{1,0:T(8,128)(2,1)S(1)}, bf16[256,256]{1,0:T(8,128)(2,1)S(1)}, u32[]{:S(2)}, u32[]{:S(2)}) collective-permute-start(bf16[256,256]{1,0:T(8,128)(2,1)S(1)} %add_convert_fusion.3), channel_id=1, source_target_pairs={{0,2},{1,3},{2,0},{3,1},{4,6},{5,7},{6,4},{7,5},{8,10},{9,11},{10,... | collective-permute-start | bytes 393224 | tf_op jit(solution)/shard_map/cond/branch_1_fun/ppermute | solution.py:17
  43.7 5.8 %collective-permute-start.2 = (bf16[256,256]{1,0:T(8,128)(2,1)S(1)}, bf16[256,256]{1,0:T(8,128)(2,1)S(1)}, u32[]{:S(2)}, u32[]{:S(2)}) collective-permute-start(bf16[256,256]{1,0:T(8,128)(2,1)S(1)} %add_convert_fusion.2), channel_id=1, source_target_pairs={{0,4},{1,5},{2,6},{3,7},{4,0},{5,1},{6,2},{7,3},{8,12},{9,13},{10,... | collective-permute-start | bytes 393224 | tf_op jit(solution)/shard_map/cond/branch_1_fun/ppermute | solution.py:17
  45.2 14.7 %all-to-all-start = ((bf16[8,144,256]{2,1,0:T(8,128)(2,1)}), bf16[8,144,256]{2,1,0:T(8,128)(2,1)}, u32[]{:S(2)}, u32[]{:S(2)}) async-start(bf16[8,144,256]{2,1,0:T(8,128)(2,1)} %get-tuple-element.4), calls=%async_computation | async-start | bytes 1179648 | tf_op jit(solution)/shard_map/cond/branch_1_fun/all_to_all | solution.py:157
  49.5 5.8 %collective-permute-start.3 = (bf16[256,256]{1,0:T(8,128)(2,1)S(1)}, bf16[256,256]{1,0:T(8,128)(2,1)S(1)}, u32[]{:S(2)}, u32[]{:S(2)}) collective-permute-start(bf16[256,256]{1,0:T(8,128)(2,1)S(1)} %add_convert_fusion.1), channel_id=1, source_target_pairs={{0,8},{8,0},{16,24},{24,16},{1,9},{9,1},{17,25},{25,17},{2,10},{10... | collective-permute-start | bytes 393224 | tf_op jit(solution)/shard_map/cond/branch_1_fun/ppermute | solution.py:17
  59.9 7.1 %collective-permute-start.17 = (bf16[256,256]{1,0:T(8,128)(2,1)S(1)}, bf16[256,256]{1,0:T(8,128)(2,1)S(1)}, u32[]{:S(2)}, u32[]{:S(2)}) collective-permute-start(bf16[256,256]{1,0:T(8,128)(2,1)S(1)} %get-tuple-element.52), channel_id=1, source_target_pairs={{0,16},{8,24},{16,0},{24,8},{1,17},{9,25},{17,1},{25,9},{2,18},{10... | collective-permute-start | bytes 393224 | tf_op jit(solution)/shard_map/ppermute | solution.py:17

commit v3 on v2

v3 whole, which is shorter than its diff:
```python
import functools
import math

import jax
import jax.numpy as jnp
from jax import lax
from jax.experimental import pallas as pl
from jax.experimental.pallas import tpu as pltpu
from jax.sharding import PartitionSpec as P

F32, BF16 = jnp.float32, jnp.bfloat16
ROOT = math.sqrt(2.0 / math.pi)
CUBIC = 0.044715


def swapped(value, axis, k):
    return lax.ppermute(value, axis, [(i, i ^ k) for i in range(lax.axis_size(axis))])


def after(value, other):
    return value if other is None else lax.optimization_barrier((value, other))[0]


def fenced(sure, body, *args):
    blank = lambda *args: jax.tree.map(lambda s: jnp.zeros(s.shape, s.dtype), jax.eval_shape(body, *args))
    return lax.cond(sure, body, blank, *args)


def call(body, outs, args, kinds, scratch=(), flops=0, name=None):
    spaces = {"s": pltpu.SMEM, "v": pltpu.VMEM, "h": pltpu.HBM}
    nbytes = sum(math.prod(a.shape) * a.dtype.itemsize for a in (*args, *outs))
    work = sum(math.prod(s.shape) * jnp.dtype(s.dtype).itemsize for s in scratch if s.memory_space == pltpu.VMEM)
    return pl.pallas_call(
        body,
        out_shape=outs,
        in_specs=[pl.BlockSpec(memory_space=spaces[k]) for k in kinds],
        out_specs=[pl.BlockSpec(memory_space=pltpu.VMEM) for _ in outs],
        scratch_shapes=list(scratch),
        cost_estimate=pl.CostEstimate(flops=flops, bytes_accessed=nbytes, transcendentals=0),
        compiler_params=pltpu.CompilerParams(vmem_limit_bytes=nbytes + work + (4 << 20)),
        name=name,
    )(*args)


def arrange(count, me_ref, cols_ref, in_hbm, a_ref, in_ref, in_sem):
    blocks, _, pairs, edge, _ = in_ref.shape
    rows = blocks * edge
    copies = [pltpu.make_async_copy(in_hbm.at[b], in_ref.at[b], in_sem.at[b]) for b in range(blocks)]
    for copy in copies:
        copy.start()
    a_ref[...] = jnp.zeros_like(a_ref)
    for b in range(blocks):
        copies[b].wait()
        for n in range(count):
            s = me_ref[0] ^ ((count - n) % count)
            for k in range(pairs):
                start = pl.multiple_of(n * rows + cols_ref[b, k, s] * edge, edge)
                a_ref[b * edge:(b + 1) * edge, pl.ds(start, edge)] = in_ref[b, s, k]


def dot(left, right):
    return jnp.dot(left, right, preferred_element_type=F32)


def dot_t(left, right):
    return lax.dot_general(left, right, (((0,), (0,)), ((), ())), preferred_element_type=F32)


def layer(count, doms, me_ref, want_ref, refs_ref, *args):
    panels, others = args[:count], args[count:count + doms - 1]
    (a_ref, off_ref, weight_ref, bias_ref, cot_ref,
     act_ref, keep_ref, give_ref, *rest) = args[count + doms - 1:]
    outs, (grad_ref, term_ref, block_ref) = rest[:count], rest[count:]
    blocks, tiles, edge, _ = off_ref.shape
    rows, cap = blocks * edge, want_ref.shape[0]
    for n in range(1, doms):
        f = me_ref[1] ^ n
        for c in range(cap):
            block_ref[f * cap + c] = others[n - 1][pl.ds(pl.multiple_of(want_ref[c, f] * edge, edge), edge), :]
    inner = dot(a_ref[...], jnp.concatenate([ref[...] for ref in panels], axis=0))
    sums = []
    for b in range(blocks):
        left = jnp.concatenate([off_ref[b, k] for k in range(tiles)], axis=1)
        right = jnp.concatenate([block_ref[refs_ref[b, k]] for k in range(tiles)], axis=0)
        sums.append(inner[b * edge:(b + 1) * edge] + dot(left, right))
    agg = jnp.concatenate(sums, axis=0).astype(BF16)
    v = dot(agg, weight_ref[...]) + bias_ref[...]
    t = jnp.tanh(ROOT * (v + CUBIC * (v * v * v)))
    act_ref[...] = (0.5 * v * (1.0 + t)).astype(BF16)
    slope = 0.5 * (1.0 + t) + 0.5 * v * (1.0 - t * t) * (ROOT * (1.0 + 3.0 * CUBIC * (v * v)))
    grad_pre = (cot_ref[...].astype(F32) * slope).astype(BF16)
    grad_agg = lax.dot_general(
        grad_pre, weight_ref[...], (((1,), (1,)), ((), ())), preferred_element_type=F32).astype(BF16)
    grad_ref[...] = grad_agg
    for n in range(count):
        outs[n][...] = dot_t(a_ref[:, n * rows:(n + 1) * rows], grad_agg).astype(BF16)
    term_ref[...] = dot_t(agg, grad_pre)
    half, core = keep_ref.shape[0], me_ref[1] & 1
    keep_ref[...] = term_ref[pl.ds(pl.multiple_of(core * half, half), half), :].astype(BF16)
    give_ref[...] = term_ref[pl.ds(pl.multiple_of((1 - core) * half, half), half), :].astype(BF16)


def spread_outer(want_ref, refs_ref, off_ref, grad_ref, out_ref, total_ref):
    blocks, tiles, edge, _ = off_ref.shape
    cap, doms = want_ref.shape
    grad_agg = grad_ref[...]
    total_ref[...] = jnp.zeros_like(total_ref)
    for b in range(blocks):
        grad_b = grad_agg[b * edge:(b + 1) * edge]
        for k in range(tiles):
            total_ref[refs_ref[b, k]] += dot_t(off_ref[b, k], grad_b)
    for f in range(doms):
        for c in range(cap):
            out_ref[f, c * edge:(c + 1) * edge, :] = total_ref[f * cap + c].astype(BF16)
            top = cap * edge + c * 16
            out_ref[f, top:top + 16, :] = jnp.full((16, out_ref.shape[2]), want_ref[c, f], jnp.int32).astype(BF16)


def joined(part, axis, k):
    return (part.astype(F32) + swapped(part, axis, k).astype(F32)).astype(BF16)


def finish(cap, edge, scale, me_ref, part_ref, other_ref, coming_ref, *args):
    terms, (out_ref, weight_ref) = args[:-2], args[-2:]
    half, core = part_ref.shape[0], me_ref[1] & 1
    weight_ref[pl.ds(pl.multiple_of(core * half, half), half), :] = (part_ref[...].astype(F32) * scale).astype(BF16)
    weight_ref[pl.ds(pl.multiple_of((1 - core) * half, half), half), :] = (other_ref[...].astype(F32) * scale).astype(BF16)
    for j in range(out_ref.shape[0] // edge):
        part = slice(j * edge, (j + 1) * edge)
        total = terms[0][part, :].astype(F32)
        for ref in terms[1:]:
            total += ref[part, :].astype(F32)
        for f in range(coming_ref.shape[0]):
            for c in range(cap):
                top = cap * edge + c * 16
                place = coming_ref[f, top:top + 1, :].astype(F32)
                total += jnp.where(place == j, coming_ref[f, c * edge:(c + 1) * edge, :].astype(F32), 0.0)
        out_ref[part, :] = total.astype(BF16)


def local(feats, cotangent, weight, bias, in_vals, in_cols, off_vals, off_ref, want):
    count, doms = lax.axis_size("rep"), lax.axis_size("dom")
    me = jnp.stack([lax.axis_index("rep"), lax.axis_index("dom")]).astype(jnp.int32)
    blocks, _, _, edge, _ = in_vals.shape
    rows, width = feats.shape
    requests = want.transpose(0, 1, 3, 2).reshape(want.shape[3], want.shape[2])
    cap = requests.shape[0]
    shape = jax.ShapeDtypeStruct
    flat = shape((rows, width), BF16)

    slots = doms * cap
    sure = requests[0, 0] >= 0
    scale = 1.0 / math.sqrt(rows * count * doms)

    def exchange(outer, part):
        coming = lax.all_to_all(outer, "dom", split_axis=0, concat_axis=0, tiled=True)
        for axis, k, size in (("dom", 4, doms), ("rep", 1, count)):
            while k < size:
                part, k = joined(part, axis, k), 2 * k
        return coming, part, swapped(part, "dom", 1)

    near = swapped(feats, "dom", 1)
    even = [feats] + [swapped(feats, "dom", k) for k in range(2, doms, 2)]
    panels = [feats] + [swapped(feats, "rep", k) for k in range(count - 1, 0, -1)]
    a = call(
        functools.partial(arrange, count), [shape((rows, count * rows), BF16)],
        (after(after(me, near), even[2]), in_cols.transpose(0, 2, 1), in_vals), "ssh",
        scratch=[pltpu.VMEM(in_vals.shape, BF16), pltpu.SemaphoreType.DMA((blocks,))], name="arrange")[0]
    odd = [near] + [swapped(after(after(value, a), panels[1]), "dom", 1) for n, value in enumerate(even) if n]
    others = [value for pair in zip(even, odd) for value in pair][1:]
    activated, keep, give, *terms, grad_agg = call(
        functools.partial(layer, count, doms),
        [flat] + [shape((width // 2, width), BF16)] * 2 + [flat] * (count + 1),
        (me, requests, off_ref, *panels, *others, a, off_vals, weight, bias.reshape(1, width), cotangent),
        "sss" + "v" * (count + doms + 4),
        scratch=[pltpu.VMEM((width, width), F32), pltpu.VMEM((slots, edge, width), BF16)],
        flops=10**9, name="layer")
    part = (keep.astype(F32) + swapped(give, "dom", 1).astype(F32)).astype(BF16)
    part = joined(part, "dom", 2)
    got = [terms[0]] + [swapped(terms[count - k], "rep", k) for k in range(count - 1, 0, -1)]
    outer = call(
        spread_outer, [shape((doms, cap * (edge + 16), width), BF16)], (requests, off_ref, off_vals, grad_agg), "ssvv",
        scratch=[pltpu.VMEM((slots, edge, width), F32)], flops=10**9, name="outer")[0]
    coming, part, other = fenced(sure, exchange, outer, part)
    grad_feats, grad_weight = call(
        functools.partial(finish, cap, edge, scale), [flat, shape((width, width), BF16)],
        (me, part, other, coming, *got), "s" + "v" * (count + 3), name="finish")
    return (activated, grad_feats, grad_weight)


def solution(mesh):
    in_specs = (
        P(("rep", "dom"), None),
        P(("rep", "dom"), None),
        P(),
        P(),
        P(("rep", "dom"), None, None, None, None),
        P(("rep", "dom"), None, None),
        P(("rep", "dom"), None, None, None),
        P(("rep", "dom"), None),
        P("rep", "dom", None, None),
    )
    out_specs = (P(("rep", "dom"), None), P(("rep", "dom"), None), P())
    return jax.shard_map(local, mesh=mesh, in_specs=in_specs, out_specs=out_specs, check_vma=False)
```

time: 68.1 us -> 59.1 us (0.87)
  starting transfers between devices: 26.4 us -> 22.2 us
  waiting for transfers between devices: 26.3 us -> 24 us
  Pallas kernels: 10.3 us -> 9.04 us
  local copies, waits for them, and re-layouts: 3.01 us -> 1.85 us
    ppermute x18 -> x19, starting transfers between devices: 22.2 us -> 18 us  [swapped(): lax.ppermute(value, axis, [(i, i ^ k) for i in range(lax.axis_size(axis))])]
    all_to_all x1, waiting for transfers between devices: 4.53 us -> 0.64 us  [exchange(): lax.all_to_all(outer, 'dom', split_axis=0, concat_axis=0, tiled=True)]
    ppermute x18 -> x19, waiting for transfers between devices: 21.8 us -> 23.4 us  [swapped(): lax.ppermute(value, axis, [(i, i ^ k) for i in range(lax.axis_size(axis))])]
    pallas_call x4, Pallas kernels: 10.3 us -> 9.04 us  [call(): pl.pallas_call(body, out_shape=outs, in_specs=[pl.BlockSpec(memory_space=...]
    unnamed x20 -> x18, local copies, waits for them, and re-layouts: 3.01 us -> 1.85 us
  transfers between devices with their start and end apart: 19 -> 20, of which waited for: 7 -> 9; matrix products, arithmetic and copies ran while one was open for 0% -> 1% of each run, Pallas kernels for 9% -> 5%
where the time goes in v3:
time: 59.1 us; the launch traced here: 58.8 us
  waiting for transfers between devices  24 us (41%)
  starting transfers between devices  22.2 us (38%)
  Pallas kernels  9.04 us (15%)
  local copies, waits for them, and re-layouts  1.85 us (3%)
  between operations  0.83 us (1%)
  other arithmetic  0.79 us (1%)
    ppermute x19, waiting for transfers between devices, swapped(): lax.ppermute(value, axis, [(i, i ^ k) for i in range(lax.axis_size(axis))])  23.4 us
    ppermute x19, starting transfers between devices, swapped(): lax.ppermute(value, axis, [(i, i ^ k) for i in range(lax.axis_size(axis))])  18 us
    pallas_call x4, Pallas kernels, call(): pl.pallas_call(body, out_shape=outs, in_specs=[pl.BlockSpec(memory_space=...  9.04 us
    all_to_all x1, starting transfers between devices, exchange(): lax.all_to_all(outer, 'dom', split_axis=0, concat_axis=0, tiled=True)  4.19 us
    unnamed x18, local copies, waits for them, and re-layouts  1.85 us
  transfers between devices with their start and end apart: 20, of which 9 were waited for; matrix products, arithmetic and copies ran while one was open for 1% of the time, Pallas kernels for 5%

profile of v3, /device:TPU:0, one launch (start us, length us, event | category | flops | bytes accessed | tf_op | source)
XLA Modules:
  0.0 58.8 jit_solution(8719880300468327313)
XLA Ops:
  0.6 0.5 collective-permute-start.7
  1.2 2.6 %collective-permute-start.9 = (bf16[384,256]{1,0:T(8,128)(2,1)}, bf16[384,256]{1,0:T(8,128)(2,1)S(1)}, u32[]{:S(2)}, u32[]{:S(2)}) collective-permute-start(bf16[384,256]{1,0:T(8,128)(2,1)} %args_0_.4), channel_id=1, source_target_pairs={{0,4},{1,5},{2,6},{3,7},{4,0},{5,1},{6,2},{7,3},{8,12},{9,13},{10,... | collective-permute-start | bytes 589832 | tf_op jit(solution)/shard_map/ppermute | solution.py:17
  3.8 3.6 %collective-permute-start.4 = (bf16[384,256]{1,0:T(8,128)(2,1)}, bf16[384,256]{1,0:T(8,128)(2,1)S(1)}, u32[]{:S(2)}, u32[]{:S(2)}) collective-permute-start(bf16[384,256]{1,0:T(8,128)(2,1)} %args_0_.4), channel_id=1, source_target_pairs={{0,24},{8,16},{16,8},{24,0},{1,25},{9,17},{17,9},{25,1},{2,26},{10... | collective-permute-start | bytes 589832 | tf_op jit(solution)/shard_map/ppermute | solution.py:17
  7.4 1.5 %collective-permute-start.8 = (bf16[384,256]{1,0:T(8,128)(2,1)}, bf16[384,256]{1,0:T(8,128)(2,1)S(1)}, u32[]{:S(2)}, u32[]{:S(2)}) collective-permute-start(bf16[384,256]{1,0:T(8,128)(2,1)} %args_0_.4), channel_id=1, source_target_pairs={{0,2},{1,3},{2,0},{3,1},{4,6},{5,7},{6,4},{7,5},{8,10},{9,11},{10,... | collective-permute-start | bytes 589832 | tf_op jit(solution)/shard_map/ppermute | solution.py:17
  8.8 0.5 collective-permute-start.12
  9.3 0.1 pad_add_fusion.me_ref
  9.5 1.8 %collective-permute-start.6 = (bf16[384,256]{1,0:T(8,128)(2,1)}, bf16[384,256]{1,0:T(8,128)(2,1)S(1)}, u32[]{:S(2)}, u32[]{:S(2)}) collective-permute-start(bf16[384,256]{1,0:T(8,128)(2,1)} %args_0_.4), channel_id=1, source_target_pairs={{0,8},{8,0},{16,24},{24,16},{1,9},{9,1},{17,25},{25,17},{2,10},{10... | collective-permute-start | bytes 589832 | tf_op jit(solution)/shard_map/ppermute | solution.py:17
  11.3 1.1 %copy-done.1 = bf16[3,4,2,128,128]{4,3,2,1,0:T(8,128)(2,1)S(1)} copy-done((bf16[3,4,2,128,128]{4,3,2,1,0:T(8,128)(2,1)S(1)}, bf16[3,4,2,128,128]{4,3,2,1,0:T(8,128)(2,1)}, u32[]{:S(2)}) %copy-start.1) | copy-done | bytes 786456
  12.4 0.7 %copy-done.5 = s32[3,4,2]{1,2,0:T(2,128)S(1)} copy-done((s32[3,4,2]{1,2,0:T(2,128)S(1)}, s32[3,4,2]{1,2,0:T(2,128)}, u32[]{:S(2)}) %copy-start.5) | copy-done | bytes 120
  13.1 0.9 %arrange.1.args_11_ = bf16[384,1536]{1,0:T(8,128)(2,1)S(1)} custom-call(s32[2]{0:T(128)S(1)} %pad_add_fusion.me_ref, s32[3,2,4]{2,1,0:T(2,128)S(1)} %bitcast.7, bf16[3,4,2,128,128]{4,3,2,1,0:T(8,128)(2,1)S(1)} %copy-done.1), custom_call_target="tpu_custom_call" | custom-call | bytes 1966184 | tf_op jit(solution)/shard_map/arrange/pallas_call | solution.py:33
  14.1 0.1 collective-permute-start.11
  14.1 1.2 %collective-permute-done.8.args_5_ = bf16[384,256]{1,0:T(8,128)(2,1)S(1)} collective-permute-done((bf16[384,256]{1,0:T(8,128)(2,1)}, bf16[384,256]{1,0:T(8,128)(2,1)S(1)}, u32[]{:S(2)}, u32[]{:S(2)}) %collective-permute-start.8) | collective-permute-done | bytes 196640 | tf_op jit(solution)/shard_map/ppermute | solution.py:17
  15.4 3.1 %collective-permute-done.12.args_9_ = bf16[384,256]{1,0:T(8,128)(2,1)S(1)} collective-permute-done((bf16[384,256]{1,0:T(8,128)(2,1)}, bf16[384,256]{1,0:T(8,128)(2,1)S(1)}, u32[]{:S(2)}, u32[]{:S(2)}) %collective-permute-start.12) | collective-permute-done | bytes 196640 | tf_op jit(solution)/shard_map/ppermute | solution.py:17
  18.4 6.2 %collective-permute-done.5.args_2_ = bf16[384,256]{1,0:T(8,128)(2,1)S(1)} collective-permute-done((bf16[384,256]{1,0:T(8,128)(2,1)}, bf16[384,256]{1,0:T(8,128)(2,1)S(1)}, u32[]{:S(2)}, u32[]{:S(2)}) %collective-permute-start.5) | collective-permute-done | bytes 196640 | tf_op jit(solution)/shard_map/ppermute | solution.py:17
  24.7 3.7 %layer.1 = (bf16[384,256]{1,0:T(8,128)(2,1)}, bf16[128,256]{1,0:T(8,128)(2,1)S(1)}, bf16[128,256]{1,0:T(8,128)(2,1)S(1)}, bf16[384,256]{1,0:T(8,128)(2,1)S(1)}, ...) custom-call(s32[2]{0:T(128)S(1)} %pad_add_fusion.me_ref, ...), custom_call_target="tpu_custom_call" | custom-call | flops 1000000000 | bytes 5866644 | tf_op jit(solution)/shard_map/layer/pallas_call | solution.py:33
  28.4 2.5 %collective-permute-start.16 = (bf16[384,256]{1,0:T(8,128)(2,1)S(1)}, bf16[384,256]{1,0:T(8,128)(2,1)S(1)}, u32[]{:S(2)}, u32[]{:S(2)}) collective-permute-start(bf16[384,256]{1,0:T(8,128)(2,1)S(1)} %get-tuple-element.46), channel_id=1, source_target_pairs={{0,24},{8,16},{16,8},{24,0},{1,25},{9,17},{17,9},{25,1},{2,26},{10... | collective-permute-start | bytes 589832 | tf_op jit(solution)/shard_map/ppermute | solution.py:17
  31.0 1.9 %collective-permute-start.18 = (bf16[384,256]{1,0:T(8,128)(2,1)S(1)}, bf16[384,256]{1,0:T(8,128)(2,1)S(1)}, u32[]{:S(2)}, u32[]{:S(2)}) collective-permute-start(bf16[384,256]{1,0:T(8,128)(2,1)S(1)} %get-tuple-element.48), channel_id=1, source_target_pairs={{0,8},{8,0},{16,24},{24,16},{1,9},{9,1},{17,25},{25,17},{2,10},{10... | collective-permute-start | bytes 589832 | tf_op jit(solution)/shard_map/ppermute | solution.py:17
  32.9 1.6 %collective-permute-start.15 = (bf16[128,256]{1,0:T(8,128)(2,1)S(1)}, bf16[128,256]{1,0:T(8,128)(2,1)S(1)}, u32[]{:S(2)}, u32[]{:S(2)}) collective-permute-start(bf16[128,256]{1,0:T(8,128)(2,1)S(1)} %add_convert_fusion.4), channel_id=1, source_target_pairs={{0,2},{1,3},{2,0},{3,1},{4,6},{5,7},{6,4},{7,5},{8,10},{9,11},{10,... | collective-permute-start | bytes 196616 | tf_op jit(solution)/shard_map/ppermute | solution.py:17
  34.5 2.1 %outer.1 = bf16[8,144,256]{2,1,0:T(8,128)(2,1)} custom-call(s32[1,8]{1,0:T(1,128)S(1)} %bitcast.11, s32[3,9]{1,0:T(4,128)S(1)} %copy-done.6, bf16[3,9,128,128]{3,2,1,0:T(8,128)(2,1)S(1)} %copy-done, bf16[384,256]{1,0:T(8,128)(2,1)S(1)} %get-tuple-element.39.grad_ref), custom_call_target="tpu_custom_call" | custom-call | flops 1000000000 | bytes 1671308 | tf_op jit(solution)/shard_map/outer/pallas_call | solution.py:33
  36.6 0.7 %collective-permute-done.15 = bf16[128,256]{1,0:T(8,128)(2,1)S(1)} collective-permute-done((bf16[128,256]{1,0:T(8,128)(2,1)S(1)}, bf16[128,256]{1,0:T(8,128)(2,1)S(1)}, u32[]{:S(2)}, u32[]{:S(2)}) %collective-permute-start.15) | collective-permute-done | bytes 65568 | tf_op jit(solution)/shard_map/ppermute | solution.py:17
  37.3 19.2 %conditional.1 = (bf16[8,144,256]{2,1,0:T(8,128)(2,1)}, bf16[128,256]{1,0:T(8,128)(2,1)}, bf16[128,256]{1,0:T(8,128)(2,1)}) conditional(s32[]{:T(128)} %bitcast.5, () %tuple.32, (bf16[8,144,256]{2,1,0:T(8,128)(2,1)}, bf16[128,256]{1,0:T(8,128)(2,1)S(1)}) %tuple.33), branch_computations={%region_0.0_spmd, %region_1.0_spmd} | conditional | flops 393216 | bytes 3408088 | solution.py:26
  37.3 0.6 collective-permute-start
  37.9 3.8 %collective-permute-done = bf16[128,256]{1,0:T(8,128)(2,1)S(1)} collective-permute-done((bf16[128,256]{1,0:T(8,128)(2,1)S(1)}, bf16[128,256]{1,0:T(8,128)(2,1)S(1)}, u32[]{:S(2)}, u32[]{:S(2)}) %collective-permute-start) | collective-permute-done | bytes 65568 | tf_op jit(solution)/shard_map/cond/branch_1_fun/ppermute | solution.py:17
  41.7 0.2 collective-permute-start.1
  41.8 4.2 %all-to-all-start = ((bf16[8,144,256]{2,1,0:T(8,128)(2,1)}), bf16[8,144,256]{2,1,0:T(8,128)(2,1)}, u32[]{:S(2)}, u32[]{:S(2)}) async-start(bf16[8,144,256]{2,1,0:T(8,128)(2,1)} %get-tuple-element.4), calls=%async_computation | async-start | bytes 1179648 | tf_op jit(solution)/shard_map/cond/branch_1_fun/all_to_all | solution.py:156
  46.0 2.3 %collective-permute-done.1 = bf16[128,256]{1,0:T(8,128)(2,1)S(1)} collective-permute-done((bf16[128,256]{1,0:T(8,128)(2,1)S(1)}, bf16[128,256]{1,0:T(8,128)(2,1)S(1)}, u32[]{:S(2)}, u32[]{:S(2)}) %collective-permute-start.1) | collective-permute-done | bytes 65568 | tf_op jit(solution)/shard_map/cond/branch_1_fun/ppermute | solution.py:17
  48.4 0.7 %collective-permute-start.2 = (bf16[128,256]{1,0:T(8,128)(2,1)S(1)}, bf16[128,256]{1,0:T(8,128)(2,1)S(1)}, u32[]{:S(2)}, u32[]{:S(2)}) collective-permute-start(bf16[128,256]{1,0:T(8,128)(2,1)S(1)} %add_convert_fusion.1), channel_id=1, source_target_pairs={{0,16},{8,24},{16,0},{24,8},{1,17},{9,25},{17,1},{25,9},{2,18},{10... | collective-permute-start | bytes 196616 | tf_op jit(solution)/shard_map/cond/branch_1_fun/ppermute | solution.py:17
  49.1 4.5 %collective-permute-done.2 = bf16[128,256]{1,0:T(8,128)(2,1)S(1)} collective-permute-done((bf16[128,256]{1,0:T(8,128)(2,1)S(1)}, bf16[128,256]{1,0:T(8,128)(2,1)S(1)}, u32[]{:S(2)}, u32[]{:S(2)}) %collective-permute-start.2) | collective-permute-done | bytes 65568 | tf_op jit(solution)/shard_map/cond/branch_1_fun/ppermute | solution.py:17
  53.6 0.6 %add_convert_fusion = bf16[128,256]{1,0:T(8,128)(2,1)} fusion(bf16[128,256]{1,0:T(8,128)(2,1)S(1)} %collective-permute-done.2, bf16[128,256]{1,0:T(8,128)(2,1)S(1)} %add_convert_fusion.1), kind=kLoop, calls=%fused_computation | loop fusion | flops 131072 | bytes 196608 | tf_op jit(solution)/shard_map/cond/branch_1_fun/convert_element_type | solution.py:120
  54.3 1.6 %collective-permute-done.3 = bf16[128,256]{1,0:T(8,128)(2,1)} collective-permute-done((bf16[128,256]{1,0:T(8,128)(2,1)}, bf16[128,256]{1,0:T(8,128)(2,1)}, u32[]{:S(2)}, u32[]{:S(2)}) %collective-permute-start.3) | collective-permute-done | bytes 65568 | tf_op jit(solution)/shard_map/cond/branch_1_fun/ppermute | solution.py:17
  55.9 0.6 %all-to-all-done = bf16[8,144,256]{2,1,0:T(8,128)(2,1)} async-done(((bf16[8,144,256]{2,1,0:T(8,128)(2,1)}), bf16[8,144,256]{2,1,0:T(8,128)(2,1)}, u32[]{:S(2)}, u32[]{:S(2)}) %all-to-all-start) | async-done | bytes 589856 | tf_op jit(solution)/shard_map/cond/branch_1_fun/all_to_all | solution.py:156
  56.5 2.3 %finish.1 = (bf16[384,256]{1,0:T(8,128)(2,1)}, bf16[256,256]{1,0:T(8,128)(2,1)}) custom-call(s32[2]{0:T(128)S(1)} %pad_add_fusion.me_ref, bf16[128,256]{1,0:T(8,128)(2,1)} %get-tuple-element.42.part_ref, bf16[128,256]{1,0:T(8,128)(2,1)} %get-tuple-element.43.other_ref, bf16[8,144,256]{2,1,0:T(8,128)(2,1)} %get-tuple-element.44.coming_ref, ...), custom_call_target="tpu_custom_call" | custom-call | bytes 1835016 | tf_op jit(solution)/shard_map/finish/pallas_call | solution.py:33
  (37 shorter events, 0.2 us)
Async XLA Ops:
  0.6 24.0 %copy-start = (bf16[3,9,128,128]{3,2,1,0:T(8,128)(2,1)S(1)}, bf16[3,9,128,128]{3,2,1,0:T(8,128)(2,1)}, u32[]{:S(2)}) copy-start(bf16[3,9,128,128]{3,2,1,0:T(8,128)(2,1)} %off_ref.1) | copy-start | bytes 2654212
  0.6 8.8 %collective-permute-start.7 = (bf16[384,256]{1,0:T(8,128)(2,1)}, bf16[384,256]{1,0:T(8,128)(2,1)S(1)}, u32[]{:S(2)}, u32[]{:S(2)}) collective-permute-start(bf16[384,256]{1,0:T(8,128)(2,1)} %args_0_.4), channel_id=1, source_target_pairs={{0,1},{1,0},{2,3},{3,2},{4,5},{5,4},{6,7},{7,6},{8,9},{9,8},{10,11... | collective-permute-start | bytes 589832 | tf_op jit(solution)/shard_map/ppermute | solution.py:17
  1.2 8.3 %collective-permute-start.9 = (bf16[384,256]{1,0:T(8,128)(2,1)}, bf16[384,256]{1,0:T(8,128)(2,1)S(1)}, u32[]{:S(2)}, u32[]{:S(2)}) collective-permute-start(bf16[384,256]{1,0:T(8,128)(2,1)} %args_0_.4), channel_id=1, source_target_pairs={{0,4},{1,5},{2,6},{3,7},{4,0},{5,1},{6,2},{7,3},{8,12},{9,13},{10,... | collective-permute-start | bytes 589832 | tf_op jit(solution)/shard_map/ppermute | solution.py:17
  3.8 10.3 %collective-permute-start.4 = (bf16[384,256]{1,0:T(8,128)(2,1)}, bf16[384,256]{1,0:T(8,128)(2,1)S(1)}, u32[]{:S(2)}, u32[]{:S(2)}) collective-permute-start(bf16[384,256]{1,0:T(8,128)(2,1)} %args_0_.4), channel_id=1, source_target_pairs={{0,24},{8,16},{16,8},{24,0},{1,25},{9,17},{17,9},{25,1},{2,26},{10... | collective-permute-start | bytes 589832 | tf_op jit(solution)/shard_map/ppermute | solution.py:17
  7.4 8.0 %collective-permute-start.8 = (bf16[384,256]{1,0:T(8,128)(2,1)}, bf16[384,256]{1,0:T(8,128)(2,1)S(1)}, u32[]{:S(2)}, u32[]{:S(2)}) collective-permute-start(bf16[384,256]{1,0:T(8,128)(2,1)} %args_0_.4), channel_id=1, source_target_pairs={{0,2},{1,3},{2,0},{3,1},{4,6},{5,7},{6,4},{7,5},{8,10},{9,11},{10,... | collective-permute-start | bytes 589832 | tf_op jit(solution)/shard_map/ppermute | solution.py:17
  8.8 9.6 %collective-permute-start.12 = (bf16[384,256]{1,0:T(8,128)(2,1)}, bf16[384,256]{1,0:T(8,128)(2,1)S(1)}, u32[]{:S(2)}, u32[]{:S(2)}) collective-permute-start(bf16[384,256]{1,0:T(8,128)(2,1)} %args_0_.4), channel_id=1, source_target_pairs={{0,6},{1,7},{2,4},{3,5},{4,2},{5,3},{6,0},{7,1},{8,14},{9,15},{10,... | collective-permute-start | bytes 589832 | tf_op jit(solution)/shard_map/ppermute | solution.py:17
  9.4 15.2 %collective-permute-start.5 = (bf16[384,256]{1,0:T(8,128)(2,1)}, bf16[384,256]{1,0:T(8,128)(2,1)S(1)}, u32[]{:S(2)}, u32[]{:S(2)}) collective-permute-start(bf16[384,256]{1,0:T(8,128)(2,1)} %args_0_.4), channel_id=1, source_target_pairs={{0,16},{8,24},{16,0},{24,8},{1,17},{9,25},{17,1},{25,9},{2,18},{10... | collective-permute-start | bytes 589832 | tf_op jit(solution)/shard_map/ppermute | solution.py:17
  9.5 15.1 %collective-permute-start.6 = (bf16[384,256]{1,0:T(8,128)(2,1)}, bf16[384,256]{1,0:T(8,128)(2,1)S(1)}, u32[]{:S(2)}, u32[]{:S(2)}) collective-permute-start(bf16[384,256]{1,0:T(8,128)(2,1)} %args_0_.4), channel_id=1, source_target_pairs={{0,8},{8,0},{16,24},{24,16},{1,9},{9,1},{17,25},{25,17},{2,10},{10... | collective-permute-start | bytes 589832 | tf_op jit(solution)/shard_map/ppermute | solution.py:17
  11.3 1.1 %copy-start.1 = (bf16[3,4,2,128,128]{4,3,2,1,0:T(8,128)(2,1)S(1)}, bf16[3,4,2,128,128]{4,3,2,1,0:T(8,128)(2,1)}, u32[]{:S(2)}) copy-start(bf16[3,4,2,128,128]{4,3,2,1,0:T(8,128)(2,1)} %in_hbm.1) | copy-start | bytes 2359300
  12.4 0.7 %copy-start.5 = (s32[3,4,2]{1,2,0:T(2,128)S(1)}, s32[3,4,2]{1,2,0:T(2,128)}, u32[]{:S(2)}) copy-start(s32[3,4,2]{1,2,0:T(2,128)} %param.16) | copy-start | bytes 292
  13.1 11.5 %copy-start.2 = (bf16[384,256]{1,0:T(8,128)(2,1)S(1)}, bf16[384,256]{1,0:T(8,128)(2,1)}, u32[]{:S(2)}) copy-start(bf16[384,256]{1,0:T(8,128)(2,1)} %args_0_.4) | copy-start | bytes 589828
  13.1 11.5 %copy-start.3 = (bf16[384,256]{1,0:T(8,128)(2,1)S(1)}, bf16[384,256]{1,0:T(8,128)(2,1)}, u32[]{:S(2)}) copy-start(bf16[384,256]{1,0:T(8,128)(2,1)} %args_15_.1) | copy-start | bytes 589828
  13.1 11.5 %copy-start.4 = (bf16[256,256]{1,0:T(8,128)(2,1)S(1)}, bf16[256,256]{1,0:T(8,128)(2,1)}, u32[]{:S(2)}) copy-start(bf16[256,256]{1,0:T(8,128)(2,1)} %args_13_.1) | copy-start | bytes 393220
  13.1 11.6 %copy-start.6 = (s32[3,9]{1,0:T(4,128)S(1)}, s32[3,9]{1,0:T(4,128)}, u32[]{:S(2)}) copy-start(s32[3,9]{1,0:T(4,128)} %refs_ref.3) | copy-start | bytes 328
  13.1 11.6 %copy-start.7 = (f32[256]{0:T(256)S(1)}, f32[256]{0:T(256)}, u32[]{:S(2)}) copy-start(f32[256]{0:T(256)} %param.14) | copy-start | bytes 3076
  13.1 11.6 %copy-start.8 = (s32[1,1,8,1]{2,3,1,0:T(1,128)S(1)}, s32[1,1,8,1]{2,3,1,0:T(1,128)}, u32[]{:S(2)}) copy-start(s32[1,1,8,1]{2,3,1,0:T(1,128)} %param.19) | copy-start | bytes 100
  14.1 10.5 %collective-permute-start.11 = (bf16[384,256]{1,0:T(8,128)(2,1)S(1)}, bf16[384,256]{1,0:T(8,128)(2,1)S(1)}, u32[]{:S(2)}, u32[]{:S(2)}) collective-permute-start(bf16[384,256]{1,0:T(8,128)(2,1)S(1)} %collective-permute-done.9.args_7_), channel_id=1, source_target_pairs={{0,1},{1,0},{2,3},{3,2},{4,5},{5,4},{6,7},{7,6},{8,9},{9,8},{10,11... | collective-permute-start | bytes 589832 | tf_op jit(solution)/shard_map/ppermute | solution.py:17
  15.4 9.2 %collective-permute-start.10 = (bf16[384,256]{1,0:T(8,128)(2,1)S(1)}, bf16[384,256]{1,0:T(8,128)(2,1)S(1)}, u32[]{:S(2)}, u32[]{:S(2)}) collective-permute-start(bf16[384,256]{1,0:T(8,128)(2,1)S(1)} %collective-permute-done.8.args_5_), channel_id=1, source_target_pairs={{0,1},{1,0},{2,3},{3,2},{4,5},{5,4},{6,7},{7,6},{8,9},{9,8},{10,11... | collective-permute-start | bytes 589832 | tf_op jit(solution)/shard_map/ppermute | solution.py:17
  18.4 6.2 %collective-permute-start.13 = (bf16[384,256]{1,0:T(8,128)(2,1)S(1)}, bf16[384,256]{1,0:T(8,128)(2,1)S(1)}, u32[]{:S(2)}, u32[]{:S(2)}) collective-permute-start(bf16[384,256]{1,0:T(8,128)(2,1)S(1)} %collective-permute-done.12.args_9_), channel_id=1, source_target_pairs={{0,1},{1,0},{2,3},{3,2},{4,5},{5,4},{6,7},{7,6},{8,9},{9,8},{10,11... | collective-permute-start | bytes 589832 | tf_op jit(solution)/shard_map/ppermute | solution.py:17
  28.4 4.5 %collective-permute-start.14 = (bf16[128,256]{1,0:T(8,128)(2,1)S(1)}, bf16[128,256]{1,0:T(8,128)(2,1)S(1)}, u32[]{:S(2)}, u32[]{:S(2)}) collective-permute-start(bf16[128,256]{1,0:T(8,128)(2,1)S(1)} %get-tuple-element.41), channel_id=1, source_target_pairs={{0,1},{1,0},{2,3},{3,2},{4,5},{5,4},{6,7},{7,6},{8,9},{9,8},{10,11... | collective-permute-start | bytes 196616 | tf_op jit(solution)/shard_map/ppermute | solution.py:17
  28.4 28.0 %collective-permute-start.16 = (bf16[384,256]{1,0:T(8,128)(2,1)S(1)}, bf16[384,256]{1,0:T(8,128)(2,1)S(1)}, u32[]{:S(2)}, u32[]{:S(2)}) collective-permute-start(bf16[384,256]{1,0:T(8,128)(2,1)S(1)} %get-tuple-element.46), channel_id=1, source_target_pairs={{0,24},{8,16},{16,8},{24,0},{1,25},{9,17},{17,9},{25,1},{2,26},{10... | collective-permute-start | bytes 589832 | tf_op jit(solution)/shard_map/ppermute | solution.py:17
  31.0 25.5 %collective-permute-start.17 = (bf16[384,256]{1,0:T(8,128)(2,1)S(1)}, bf16[384,256]{1,0:T(8,128)(2,1)S(1)}, u32[]{:S(2)}, u32[]{:S(2)}) collective-permute-start(bf16[384,256]{1,0:T(8,128)(2,1)S(1)} %get-tuple-element.47), channel_id=1, source_target_pairs={{0,16},{8,24},{16,0},{24,8},{1,17},{9,25},{17,1},{25,9},{2,18},{10... | collective-permute-start | bytes 589832 | tf_op jit(solution)/shard_map/ppermute | solution.py:17
  31.0 25.5 %collective-permute-start.18 = (bf16[384,256]{1,0:T(8,128)(2,1)S(1)}, bf16[384,256]{1,0:T(8,128)(2,1)S(1)}, u32[]{:S(2)}, u32[]{:S(2)}) collective-permute-start(bf16[384,256]{1,0:T(8,128)(2,1)S(1)} %get-tuple-element.48), channel_id=1, source_target_pairs={{0,8},{8,0},{16,24},{24,16},{1,9},{9,1},{17,25},{25,17},{2,10},{10... | collective-permute-start | bytes 589832 | tf_op jit(solution)/shard_map/ppermute | solution.py:17
  32.9 4.3 %collective-permute-start.15 = (bf16[128,256]{1,0:T(8,128)(2,1)S(1)}, bf16[128,256]{1,0:T(8,128)(2,1)S(1)}, u32[]{:S(2)}, u32[]{:S(2)}) collective-permute-start(bf16[128,256]{1,0:T(8,128)(2,1)S(1)} %add_convert_fusion.4), channel_id=1, source_target_pairs={{0,2},{1,3},{2,0},{3,1},{4,6},{5,7},{6,4},{7,5},{8,10},{9,11},{10,... | collective-permute-start | bytes 196616 | tf_op jit(solution)/shard_map/ppermute | solution.py:17
  37.3 4.3 %collective-permute-start = (bf16[128,256]{1,0:T(8,128)(2,1)S(1)}, bf16[128,256]{1,0:T(8,128)(2,1)S(1)}, u32[]{:S(2)}, u32[]{:S(2)}) collective-permute-start(bf16[128,256]{1,0:T(8,128)(2,1)S(1)} %get-tuple-element.5), channel_id=1, source_target_pairs={{0,4},{1,5},{2,6},{3,7},{4,0},{5,1},{6,2},{7,3},{8,12},{9,13},{10,... | collective-permute-start | bytes 196616 | tf_op jit(solution)/shard_map/cond/branch_1_fun/ppermute | solution.py:17
  41.7 6.7 %collective-permute-start.1 = (bf16[128,256]{1,0:T(8,128)(2,1)S(1)}, bf16[128,256]{1,0:T(8,128)(2,1)S(1)}, u32[]{:S(2)}, u32[]{:S(2)}) collective-permute-start(bf16[128,256]{1,0:T(8,128)(2,1)S(1)} %add_convert_fusion.2), channel_id=1, source_target_pairs={{0,8},{8,0},{16,24},{24,16},{1,9},{9,1},{17,25},{25,17},{2,10},{10... | collective-permute-start | bytes 196616 | tf_op jit(solution)/shard_map/cond/branch_1_fun/ppermute | solution.py:17
  41.8 14.7 %all-to-all-start = ((bf16[8,144,256]{2,1,0:T(8,128)(2,1)}), bf16[8,144,256]{2,1,0:T(8,128)(2,1)}, u32[]{:S(2)}, u32[]{:S(2)}) async-start(bf16[8,144,256]{2,1,0:T(8,128)(2,1)} %get-tuple-element.4), calls=%async_computation | async-start | bytes 1179648 | tf_op jit(solution)/shard_map/cond/branch_1_fun/all_to_all | solution.py:156
  48.4 5.2 %collective-permute-start.2 = (bf16[128,256]{1,0:T(8,128)(2,1)S(1)}, bf16[128,256]{1,0:T(8,128)(2,1)S(1)}, u32[]{:S(2)}, u32[]{:S(2)}) collective-permute-start(bf16[128,256]{1,0:T(8,128)(2,1)S(1)} %add_convert_fusion.1), channel_id=1, source_target_pairs={{0,16},{8,24},{16,0},{24,8},{1,17},{9,25},{17,1},{25,9},{2,18},{10... | collective-permute-start | bytes 196616 | tf_op jit(solution)/shard_map/cond/branch_1_fun/ppermute | solution.py:17
  54.3 1.6 %collective-permute-start.3 = (bf16[128,256]{1,0:T(8,128)(2,1)}, bf16[128,256]{1,0:T(8,128)(2,1)}, u32[]{:S(2)}, u32[]{:S(2)}) collective-permute-start(bf16[128,256]{1,0:T(8,128)(2,1)} %add_convert_fusion), channel_id=1, source_target_pairs={{0,1},{1,0},{2,3},{3,2},{4,5},{5,4},{6,7},{7,6},{8,9},{9,8},{10,11... | collective-permute-start | bytes 196616 | tf_op jit(solution)/shard_map/cond/branch_1_fun/ppermute | solution.py:17

commit v4 on v3

--- a/solution.py
+++ b/solution.py
@@ -15,6 +15,11 @@
 
 def swapped(value, axis, k):
     return lax.ppermute(value, axis, [(i, i ^ k) for i in range(lax.axis_size(axis))])
+
+
+def relayed(value, turns):
+    pairs = [(0, 1), (1, 3), (3, 2), (2, 0)]
+    return lax.ppermute(value, "rep", [pair[::turns] for pair in pairs])
 
 
 def after(value, other):
@@ -160,13 +165,18 @@
         return coming, part, swapped(part, "dom", 1)
 
     near = swapped(feats, "dom", 1)
-    even = [feats] + [swapped(feats, "dom", k) for k in range(2, doms, 2)]
-    panels = [feats] + [swapped(feats, "rep", k) for k in range(count - 1, 0, -1)]
+    even = [feats] + [swapped(feats if k == 4 else after(feats, near), "dom", k) for k in range(2, doms, 2)]
+    inside = (lax.axis_index("rep") == 1) | (lax.axis_index("rep") == 2)
+    if count == 4:
+        far = swapped(feats, "rep", 3)
+        panels = [feats, far, relayed(jnp.where(inside, far, feats), -1), swapped(feats, "rep", 1)]
+    else:
+        panels = [feats] + [swapped(feats, "rep", k) for k in range(count - 1, 0, -1)]
     a = call(
         functools.partial(arrange, count), [shape((rows, count * rows), BF16)],
         (after(after(me, near), even[2]), in_cols.transpose(0, 2, 1), in_vals), "ssh",
         scratch=[pltpu.VMEM(in_vals.shape, BF16), pltpu.SemaphoreType.DMA((blocks,))], name="arrange")[0]
-    odd = [near] + [swapped(after(after(value, a), panels[1]), "dom", 1) for n, value in enumerate(even) if n]
+    odd = [near] + [swapped(after(value, a), "dom", 1) for n, value in enumerate(even) if n]
     others = [value for pair in zip(even, odd) for value in pair][1:]
     activated, keep, give, *terms, grad_agg = call(
         functools.partial(layer, count, doms),
@@ -176,8 +186,9 @@
         scratch=[pltpu.VMEM((width, width), F32), pltpu.VMEM((slots, edge, width), BF16)],
         flops=10**9, name="layer")
     part = (keep.astype(F32) + swapped(give, "dom", 1).astype(F32)).astype(BF16)
+    first = part
     part = joined(part, "dom", 2)
-    got = [terms[0]] + [swapped(terms[count - k], "rep", k) for k in range(count - 1, 0, -1)]
+    got = [terms[0]] + [swapped(after(terms[count - k], first if k == 1 else None), "rep", k) for k in range(count - 1, 0, -1)]
     outer = call(
         spread_outer, [shape((doms, cap * (edge + 16), width), BF16)], (requests, off_ref, off_vals, grad_agg), "ssvv",
         scratch=[pltpu.VMEM((slots, edge, width), F32)], flops=10**9, name="outer")[0]

time: 59.1 us -> 56.6 us (0.958)
  waiting for transfers between devices: 24 us -> 16.8 us
  starting transfers between devices: 22.2 us -> 27 us
    ppermute x19 -> x18, waiting for transfers between devices: 23.4 us -> 12.4 us  [swapped(): lax.ppermute(value, axis, [(i, i ^ k) for i in range(lax.axis_size(axis))])]
    ppermute x0 -> x1, starting transfers between devices: none -> 4.25 us  [relayed(): return lax.ppermute(value, 'rep', [pair[::turns] for pair in pairs])]
    ppermute x0 -> x1, waiting for transfers between devices: none -> 2.97 us  [relayed(): return lax.ppermute(value, 'rep', [pair[::turns] for pair in pairs])]
    all_to_all x1, waiting for transfers between devices: 0.64 us -> 1.45 us  [exchange(): lax.all_to_all(outer, 'dom', split_axis=0, concat_axis=0, tiled=True)]
    ppermute x19 -> x18, starting transfers between devices: 18 us -> 18.5 us  [swapped(): lax.ppermute(value, axis, [(i, i ^ k) for i in range(lax.axis_size(axis))])]
  transfers between devices with their start and end apart: 20 -> 20, of which waited for: 9 -> 8; matrix products, arithmetic and copies ran while one was open for 1% -> 1% of each run, Pallas kernels for 5% -> 5%
where the time goes in v4:
time: 56.6 us; the launch traced here: 56.4 us
  starting transfers between devices  27 us (48%)
  waiting for transfers between devices  16.8 us (30%)
  Pallas kernels  9.05 us (16%)
  local copies, waits for them, and re-layouts  1.85 us (3%)
  other arithmetic  0.82 us (1%)
  between operations  0.8 us (1%)
    ppermute x18, starting transfers between devices, swapped(): lax.ppermute(value, axis, [(i, i ^ k) for i in range(lax.axis_size(axis))])  18.5 us
    ppermute x18, waiting for transfers between devices, swapped(): lax.ppermute(value, axis, [(i, i ^ k) for i in range(lax.axis_size(axis))])  12.4 us
    pallas_call x4, Pallas kernels, call(): pl.pallas_call(body, out_shape=outs, in_specs=[pl.BlockSpec(memory_space=...  9.05 us
    ppermute x1, starting transfers between devices, relayed(): return lax.ppermute(value, 'rep', [pair[::turns] for pair in pairs])  4.25 us
    all_to_all x1, starting transfers between devices, exchange(): lax.all_to_all(outer, 'dom', split_axis=0, concat_axis=0, tiled=True)  4.19 us
    ppermute x1, waiting for transfers between devices, relayed(): return lax.ppermute(value, 'rep', [pair[::turns] for pair in pairs])  2.97 us
    unnamed x18, local copies, waits for them, and re-layouts  1.85 us
    all_to_all x1, waiting for transfers between devices, exchange(): lax.all_to_all(outer, 'dom', split_axis=0, concat_axis=0, tiled=True)  1.45 us
  transfers between devices with their start and end apart: 20, of which 8 were waited for; matrix products, arithmetic and copies ran while one was open for 1% of the time, Pallas kernels for 5%

profile of v4, /device:TPU:0, one launch (start us, length us, event | category | flops | bytes accessed | tf_op | source)
XLA Modules:
  0.0 56.4 jit_solution(11321654394526252856)
XLA Ops:
  0.6 0.5 collective-permute-start.7
  1.1 2.6 %collective-permute-start.9 = (bf16[384,256]{1,0:T(8,128)(2,1)}, bf16[384,256]{1,0:T(8,128)(2,1)S(1)}, u32[]{:S(2)}, u32[]{:S(2)}) collective-permute-start(bf16[384,256]{1,0:T(8,128)(2,1)} %args_0_.4), channel_id=1, source_target_pairs={{0,4},{1,5},{2,6},{3,7},{4,0},{5,1},{6,2},{7,3},{8,12},{9,13},{10,... | collective-permute-start | bytes 589832 | tf_op jit(solution)/shard_map/ppermute | solution.py:17
  3.7 3.6 %collective-permute-start.4 = (bf16[384,256]{1,0:T(8,128)(2,1)}, bf16[384,256]{1,0:T(8,128)(2,1)S(1)}, u32[]{:S(2)}, u32[]{:S(2)}) collective-permute-start(bf16[384,256]{1,0:T(8,128)(2,1)} %args_0_.4), channel_id=1, source_target_pairs={{0,24},{8,16},{16,8},{24,0},{1,25},{9,17},{17,9},{25,1},{2,26},{10... | collective-permute-start | bytes 589832 | tf_op jit(solution)/shard_map/ppermute | solution.py:17
  7.3 0.1 pad_add_fusion.me_ref
  7.4 1.5 %collective-permute-start.8 = (bf16[384,256]{1,0:T(8,128)(2,1)}, bf16[384,256]{1,0:T(8,128)(2,1)S(1)}, u32[]{:S(2)}, u32[]{:S(2)}) collective-permute-start(bf16[384,256]{1,0:T(8,128)(2,1)} %args_0_.4), channel_id=1, source_target_pairs={{0,2},{1,3},{2,0},{3,1},{4,6},{5,7},{6,4},{7,5},{8,10},{9,11},{10,... | collective-permute-start | bytes 589832 | tf_op jit(solution)/shard_map/ppermute | solution.py:17
  8.9 0.5 collective-permute-start.12
  9.4 1.1 %copy-done.1 = bf16[3,4,2,128,128]{4,3,2,1,0:T(8,128)(2,1)S(1)} copy-done((bf16[3,4,2,128,128]{4,3,2,1,0:T(8,128)(2,1)S(1)}, bf16[3,4,2,128,128]{4,3,2,1,0:T(8,128)(2,1)}, u32[]{:S(2)}) %copy-start.1) | copy-done | bytes 786456
  10.6 0.7 %copy-done.5 = s32[3,4,2]{1,2,0:T(2,128)S(1)} copy-done((s32[3,4,2]{1,2,0:T(2,128)S(1)}, s32[3,4,2]{1,2,0:T(2,128)}, u32[]{:S(2)}) %copy-start.5) | copy-done | bytes 120
  11.3 0.9 %arrange.1.args_11_ = bf16[384,1536]{1,0:T(8,128)(2,1)S(1)} custom-call(s32[2]{0:T(128)S(1)} %pad_add_fusion.me_ref, s32[3,2,4]{2,1,0:T(2,128)S(1)} %bitcast.7, bf16[3,4,2,128,128]{4,3,2,1,0:T(8,128)(2,1)S(1)} %copy-done.1), custom_call_target="tpu_custom_call" | custom-call | bytes 1966184 | tf_op jit(solution)/shard_map/arrange/pallas_call | solution.py:38
  12.2 0.1 collective-permute-start.11
  12.3 1.2 %collective-permute-done.4.args_1_ = bf16[384,256]{1,0:T(8,128)(2,1)S(1)} collective-permute-done((bf16[384,256]{1,0:T(8,128)(2,1)}, bf16[384,256]{1,0:T(8,128)(2,1)S(1)}, u32[]{:S(2)}, u32[]{:S(2)}) %collective-permute-start.4) | collective-permute-done | bytes 196640 | tf_op jit(solution)/shard_map/ppermute | solution.py:17
  13.6 4.3 %collective-permute-start.5 = (bf16[384,256]{1,0:T(8,128)(2,1)S(1)}, bf16[384,256]{1,0:T(8,128)(2,1)S(1)}, u32[]{:S(2)}, u32[]{:S(2)}) collective-permute-start(bf16[384,256]{1,0:T(8,128)(2,1)S(1)} %broadcast_select_fusion), channel_id=1, source_target_pairs={{8,0},{24,8},{16,24},{0,16},{9,1},{25,9},{17,25},{1,17},{10,2},{26... | collective-permute-start | bytes 589832 | tf_op jit(solution)/shard_map/ppermute | solution.py:22
  17.8 0.7 %collective-permute-done.12.args_9_ = bf16[384,256]{1,0:T(8,128)(2,1)S(1)} collective-permute-done((bf16[384,256]{1,0:T(8,128)(2,1)}, bf16[384,256]{1,0:T(8,128)(2,1)S(1)}, u32[]{:S(2)}, u32[]{:S(2)}) %collective-permute-start.12) | collective-permute-done | bytes 196640 | tf_op jit(solution)/shard_map/ppermute | solution.py:17
  18.5 3.0 %collective-permute-done.5.args_2_ = bf16[384,256]{1,0:T(8,128)(2,1)S(1)} collective-permute-done((bf16[384,256]{1,0:T(8,128)(2,1)S(1)}, bf16[384,256]{1,0:T(8,128)(2,1)S(1)}, u32[]{:S(2)}, u32[]{:S(2)}) %collective-permute-start.5) | collective-permute-done | bytes 196640 | tf_op jit(solution)/shard_map/ppermute | solution.py:22
  21.5 3.7 %layer.1 = (bf16[384,256]{1,0:T(8,128)(2,1)}, bf16[128,256]{1,0:T(8,128)(2,1)S(1)}, bf16[128,256]{1,0:T(8,128)(2,1)S(1)}, bf16[384,256]{1,0:T(8,128)(2,1)S(1)}, ...) custom-call(s32[2]{0:T(128)S(1)} %pad_add_fusion.me_ref, ...), custom_call_target="tpu_custom_call" | custom-call | flops 1000000000 | bytes 5866644 | tf_op jit(solution)/shard_map/layer/pallas_call | solution.py:38
  25.3 2.3 %collective-permute-start.16 = (bf16[384,256]{1,0:T(8,128)(2,1)S(1)}, bf16[384,256]{1,0:T(8,128)(2,1)S(1)}, u32[]{:S(2)}, u32[]{:S(2)}) collective-permute-start(bf16[384,256]{1,0:T(8,128)(2,1)S(1)} %get-tuple-element.43), channel_id=1, source_target_pairs={{0,24},{8,16},{16,8},{24,0},{1,25},{9,17},{17,9},{25,1},{2,26},{10... | collective-permute-start | bytes 589832 | tf_op jit(solution)/shard_map/ppermute | solution.py:17
  27.6 1.6 %collective-permute-start.17 = (bf16[384,256]{1,0:T(8,128)(2,1)S(1)}, bf16[384,256]{1,0:T(8,128)(2,1)S(1)}, u32[]{:S(2)}, u32[]{:S(2)}) collective-permute-start(bf16[384,256]{1,0:T(8,128)(2,1)S(1)} %get-tuple-element.44), channel_id=1, source_target_pairs={{0,16},{8,24},{16,0},{24,8},{1,17},{9,25},{17,1},{25,9},{2,18},{10... | collective-permute-start | bytes 589832 | tf_op jit(solution)/shard_map/ppermute | solution.py:17
  29.2 1.6 %collective-permute-start.15 = (bf16[128,256]{1,0:T(8,128)(2,1)S(1)}, bf16[128,256]{1,0:T(8,128)(2,1)S(1)}, u32[]{:S(2)}, u32[]{:S(2)}) collective-permute-start(bf16[128,256]{1,0:T(8,128)(2,1)S(1)} %add_convert_fusion.4), channel_id=1, source_target_pairs={{0,2},{1,3},{2,0},{3,1},{4,6},{5,7},{6,4},{7,5},{8,10},{9,11},{10,... | collective-permute-start | bytes 196616 | tf_op jit(solution)/shard_map/ppermute | solution.py:17
  30.8 2.1 %outer.1 = bf16[8,144,256]{2,1,0:T(8,128)(2,1)} custom-call(s32[1,8]{1,0:T(1,128)S(1)} %bitcast.11, s32[3,9]{1,0:T(4,128)S(1)} %copy-done.6, bf16[3,9,128,128]{3,2,1,0:T(8,128)(2,1)S(1)} %copy-done, bf16[384,256]{1,0:T(8,128)(2,1)S(1)} %get-tuple-element.36.grad_ref), custom_call_target="tpu_custom_call" | custom-call | flops 1000000000 | bytes 1671308 | tf_op jit(solution)/shard_map/outer/pallas_call | solution.py:38
  32.9 0.6 collective-permute-start.18
  33.5 0.1 collective-permute-done.15
  33.6 20.5 %conditional.1 = (bf16[8,144,256]{2,1,0:T(8,128)(2,1)}, bf16[128,256]{1,0:T(8,128)(2,1)}, bf16[128,256]{1,0:T(8,128)(2,1)}) conditional(s32[]{:T(128)} %bitcast.5, () %tuple.29, (bf16[8,144,256]{2,1,0:T(8,128)(2,1)}, bf16[128,256]{1,0:T(8,128)(2,1)S(1)}) %tuple.30), branch_computations={%region_0.1_spmd, %region_1.2_spmd} | conditional | flops 393216 | bytes 3408088 | solution.py:31
  33.6 0.6 %collective-permute-start = (bf16[128,256]{1,0:T(8,128)(2,1)S(1)}, bf16[128,256]{1,0:T(8,128)(2,1)S(1)}, u32[]{:S(2)}, u32[]{:S(2)}) collective-permute-start(bf16[128,256]{1,0:T(8,128)(2,1)S(1)} %get-tuple-element.5), channel_id=1, source_target_pairs={{0,4},{1,5},{2,6},{3,7},{4,0},{5,1},{6,2},{7,3},{8,12},{9,13},{10,... | collective-permute-start | bytes 196616 | tf_op jit(solution)/shard_map/cond/branch_1_fun/ppermute | solution.py:17
  34.2 3.8 %collective-permute-done = bf16[128,256]{1,0:T(8,128)(2,1)S(1)} collective-permute-done((bf16[128,256]{1,0:T(8,128)(2,1)S(1)}, bf16[128,256]{1,0:T(8,128)(2,1)S(1)}, u32[]{:S(2)}, u32[]{:S(2)}) %collective-permute-start) | collective-permute-done | bytes 65568 | tf_op jit(solution)/shard_map/cond/branch_1_fun/ppermute | solution.py:17
  38.0 1.4 %collective-permute-start.1 = (bf16[128,256]{1,0:T(8,128)(2,1)S(1)}, bf16[128,256]{1,0:T(8,128)(2,1)S(1)}, u32[]{:S(2)}, u32[]{:S(2)}) collective-permute-start(bf16[128,256]{1,0:T(8,128)(2,1)S(1)} %add_convert_fusion.2), channel_id=1, source_target_pairs={{0,8},{8,0},{16,24},{24,16},{1,9},{9,1},{17,25},{25,17},{2,10},{10... | collective-permute-start | bytes 196616 | tf_op jit(solution)/shard_map/cond/branch_1_fun/ppermute | solution.py:17
  39.4 4.2 %all-to-all-start = ((bf16[8,144,256]{2,1,0:T(8,128)(2,1)}), bf16[8,144,256]{2,1,0:T(8,128)(2,1)}, u32[]{:S(2)}, u32[]{:S(2)}) async-start(bf16[8,144,256]{2,1,0:T(8,128)(2,1)} %get-tuple-element.4), calls=%async_computation | async-start | bytes 1179648 | tf_op jit(solution)/shard_map/cond/branch_1_fun/all_to_all | solution.py:161
  43.6 1.7 %collective-permute-start.2 = (bf16[128,256]{1,0:T(8,128)(2,1)S(1)}, bf16[128,256]{1,0:T(8,128)(2,1)S(1)}, u32[]{:S(2)}, u32[]{:S(2)}) collective-permute-start(bf16[128,256]{1,0:T(8,128)(2,1)S(1)} %add_convert_fusion.1), channel_id=1, source_target_pairs={{0,16},{8,24},{16,0},{24,8},{1,17},{9,25},{17,1},{25,9},{2,18},{10... | collective-permute-start | bytes 196616 | tf_op jit(solution)/shard_map/cond/branch_1_fun/ppermute | solution.py:17
  45.4 5.0 %collective-permute-done.2 = bf16[128,256]{1,0:T(8,128)(2,1)S(1)} collective-permute-done((bf16[128,256]{1,0:T(8,128)(2,1)S(1)}, bf16[128,256]{1,0:T(8,128)(2,1)S(1)}, u32[]{:S(2)}, u32[]{:S(2)}) %collective-permute-start.2) | collective-permute-done | bytes 65568 | tf_op jit(solution)/shard_map/cond/branch_1_fun/ppermute | solution.py:17
  50.4 0.6 %add_convert_fusion = bf16[128,256]{1,0:T(8,128)(2,1)} fusion(bf16[128,256]{1,0:T(8,128)(2,1)S(1)} %collective-permute-done.2, bf16[128,256]{1,0:T(8,128)(2,1)S(1)} %add_convert_fusion.1), kind=kLoop, calls=%fused_computation | loop fusion | flops 131072 | bytes 196608 | tf_op jit(solution)/shard_map/cond/branch_1_fun/convert_element_type | solution.py:125
  51.0 1.6 %collective-permute-done.3 = bf16[128,256]{1,0:T(8,128)(2,1)} collective-permute-done((bf16[128,256]{1,0:T(8,128)(2,1)}, bf16[128,256]{1,0:T(8,128)(2,1)}, u32[]{:S(2)}, u32[]{:S(2)}) %collective-permute-start.3) | collective-permute-done | bytes 65568 | tf_op jit(solution)/shard_map/cond/branch_1_fun/ppermute | solution.py:17
  52.6 1.4 %all-to-all-done = bf16[8,144,256]{2,1,0:T(8,128)(2,1)} async-done(((bf16[8,144,256]{2,1,0:T(8,128)(2,1)}), bf16[8,144,256]{2,1,0:T(8,128)(2,1)}, u32[]{:S(2)}, u32[]{:S(2)}) %all-to-all-start) | async-done | bytes 589856 | tf_op jit(solution)/shard_map/cond/branch_1_fun/all_to_all | solution.py:161
  54.1 2.3 %finish.1 = (bf16[384,256]{1,0:T(8,128)(2,1)}, bf16[256,256]{1,0:T(8,128)(2,1)}) custom-call(s32[2]{0:T(128)S(1)} %pad_add_fusion.me_ref, bf16[128,256]{1,0:T(8,128)(2,1)} %get-tuple-element.39.part_ref, bf16[128,256]{1,0:T(8,128)(2,1)} %get-tuple-element.40.other_ref, bf16[8,144,256]{2,1,0:T(8,128)(2,1)} %get-tuple-element.41.coming_ref, ...), custom_call_target="tpu_custom_call" | custom-call | bytes 1835016 | tf_op jit(solution)/shard_map/finish/pallas_call | solution.py:38
  (38 shorter events, 0.2 us)
Async XLA Ops:
  0.6 6.8 %collective-permute-start.7 = (bf16[384,256]{1,0:T(8,128)(2,1)}, bf16[384,256]{1,0:T(8,128)(2,1)S(1)}, u32[]{:S(2)}, u32[]{:S(2)}) collective-permute-start(bf16[384,256]{1,0:T(8,128)(2,1)} %args_0_.4), channel_id=1, source_target_pairs={{0,1},{1,0},{2,3},{3,2},{4,5},{5,4},{6,7},{7,6},{8,9},{9,8},{10,11... | collective-permute-start | bytes 589832 | tf_op jit(solution)/shard_map/ppermute | solution.py:17
  1.1 8.3 %collective-permute-start.9 = (bf16[384,256]{1,0:T(8,128)(2,1)}, bf16[384,256]{1,0:T(8,128)(2,1)S(1)}, u32[]{:S(2)}, u32[]{:S(2)}) collective-permute-start(bf16[384,256]{1,0:T(8,128)(2,1)} %args_0_.4), channel_id=1, source_target_pairs={{0,4},{1,5},{2,6},{3,7},{4,0},{5,1},{6,2},{7,3},{8,12},{9,13},{10,... | collective-permute-start | bytes 589832 | tf_op jit(solution)/shard_map/ppermute | solution.py:17
  3.7 9.8 %collective-permute-start.4 = (bf16[384,256]{1,0:T(8,128)(2,1)}, bf16[384,256]{1,0:T(8,128)(2,1)S(1)}, u32[]{:S(2)}, u32[]{:S(2)}) collective-permute-start(bf16[384,256]{1,0:T(8,128)(2,1)} %args_0_.4), channel_id=1, source_target_pairs={{0,24},{8,16},{16,8},{24,0},{1,25},{9,17},{17,9},{25,1},{2,26},{10... | collective-permute-start | bytes 589832 | tf_op jit(solution)/shard_map/ppermute | solution.py:17
  7.3 11.2 %collective-permute-start.6 = (bf16[384,256]{1,0:T(8,128)(2,1)}, bf16[384,256]{1,0:T(8,128)(2,1)S(1)}, u32[]{:S(2)}, u32[]{:S(2)}) collective-permute-start(bf16[384,256]{1,0:T(8,128)(2,1)} %args_0_.4), channel_id=1, source_target_pairs={{0,8},{8,0},{16,24},{24,16},{1,9},{9,1},{17,25},{25,17},{2,10},{10... | collective-permute-start | bytes 589832 | tf_op jit(solution)/shard_map/ppermute | solution.py:17
  7.4 10.4 %collective-permute-start.8 = (bf16[384,256]{1,0:T(8,128)(2,1)}, bf16[384,256]{1,0:T(8,128)(2,1)S(1)}, u32[]{:S(2)}, u32[]{:S(2)}) collective-permute-start(bf16[384,256]{1,0:T(8,128)(2,1)} %args_0_.4), channel_id=1, source_target_pairs={{0,2},{1,3},{2,0},{3,1},{4,6},{5,7},{6,4},{7,5},{8,10},{9,11},{10,... | collective-permute-start | bytes 589832 | tf_op jit(solution)/shard_map/ppermute | solution.py:17
  8.9 9.6 %collective-permute-start.12 = (bf16[384,256]{1,0:T(8,128)(2,1)}, bf16[384,256]{1,0:T(8,128)(2,1)S(1)}, u32[]{:S(2)}, u32[]{:S(2)}) collective-permute-start(bf16[384,256]{1,0:T(8,128)(2,1)} %args_0_.4), channel_id=1, source_target_pairs={{0,6},{1,7},{2,4},{3,5},{4,2},{5,3},{6,0},{7,1},{8,14},{9,15},{10,... | collective-permute-start | bytes 589832 | tf_op jit(solution)/shard_map/ppermute | solution.py:17
  9.4 1.1 %copy-start.1 = (bf16[3,4,2,128,128]{4,3,2,1,0:T(8,128)(2,1)S(1)}, bf16[3,4,2,128,128]{4,3,2,1,0:T(8,128)(2,1)}, u32[]{:S(2)}) copy-start(bf16[3,4,2,128,128]{4,3,2,1,0:T(8,128)(2,1)} %in_hbm.1) | copy-start | bytes 2359300
  10.6 0.7 %copy-start.5 = (s32[3,4,2]{1,2,0:T(2,128)S(1)}, s32[3,4,2]{1,2,0:T(2,128)}, u32[]{:S(2)}) copy-start(s32[3,4,2]{1,2,0:T(2,128)} %param.16) | copy-start | bytes 292
  11.3 2.3 %copy-start.2 = (bf16[384,256]{1,0:T(8,128)(2,1)S(1)}, bf16[384,256]{1,0:T(8,128)(2,1)}, u32[]{:S(2)}) copy-start(bf16[384,256]{1,0:T(8,128)(2,1)} %args_0_.4) | copy-start | bytes 589828
  11.3 10.2 %copy-start = (bf16[3,9,128,128]{3,2,1,0:T(8,128)(2,1)S(1)}, bf16[3,9,128,128]{3,2,1,0:T(8,128)(2,1)}, u32[]{:S(2)}) copy-start(bf16[3,9,128,128]{3,2,1,0:T(8,128)(2,1)} %off_ref.1) | copy-start | bytes 2654212
  11.3 10.2 %copy-start.3 = (bf16[384,256]{1,0:T(8,128)(2,1)S(1)}, bf16[384,256]{1,0:T(8,128)(2,1)}, u32[]{:S(2)}) copy-start(bf16[384,256]{1,0:T(8,128)(2,1)} %args_15_.1) | copy-start | bytes 589828
  11.3 10.2 %copy-start.4 = (bf16[256,256]{1,0:T(8,128)(2,1)S(1)}, bf16[256,256]{1,0:T(8,128)(2,1)}, u32[]{:S(2)}) copy-start(bf16[256,256]{1,0:T(8,128)(2,1)} %args_13_.1) | copy-start | bytes 393220
  11.3 10.2 %copy-start.6 = (s32[3,9]{1,0:T(4,128)S(1)}, s32[3,9]{1,0:T(4,128)}, u32[]{:S(2)}) copy-start(s32[3,9]{1,0:T(4,128)} %refs_ref.3) | copy-start | bytes 328
  11.3 10.2 %copy-start.7 = (f32[256]{0:T(256)S(1)}, f32[256]{0:T(256)}, u32[]{:S(2)}) copy-start(f32[256]{0:T(256)} %param.14) | copy-start | bytes 3076
  11.3 10.2 %copy-start.8 = (s32[1,1,8,1]{2,3,1,0:T(1,128)S(1)}, s32[1,1,8,1]{2,3,1,0:T(1,128)}, u32[]{:S(2)}) copy-start(s32[1,1,8,1]{2,3,1,0:T(1,128)} %param.19) | copy-start | bytes 100
  12.2 6.3 %collective-permute-start.11 = (bf16[384,256]{1,0:T(8,128)(2,1)S(1)}, bf16[384,256]{1,0:T(8,128)(2,1)S(1)}, u32[]{:S(2)}, u32[]{:S(2)}) collective-permute-start(bf16[384,256]{1,0:T(8,128)(2,1)S(1)} %collective-permute-done.9.args_7_), channel_id=1, source_target_pairs={{0,1},{1,0},{2,3},{3,2},{4,5},{5,4},{6,7},{7,6},{8,9},{9,8},{10,11... | collective-permute-start | bytes 589832 | tf_op jit(solution)/shard_map/ppermute | solution.py:17
  13.6 7.9 %collective-permute-start.5 = (bf16[384,256]{1,0:T(8,128)(2,1)S(1)}, bf16[384,256]{1,0:T(8,128)(2,1)S(1)}, u32[]{:S(2)}, u32[]{:S(2)}) collective-permute-start(bf16[384,256]{1,0:T(8,128)(2,1)S(1)} %broadcast_select_fusion), channel_id=1, source_target_pairs={{8,0},{24,8},{16,24},{0,16},{9,1},{25,9},{17,25},{1,17},{10,2},{26... | collective-permute-start | bytes 589832 | tf_op jit(solution)/shard_map/ppermute | solution.py:22
  17.8 3.7 %collective-permute-start.10 = (bf16[384,256]{1,0:T(8,128)(2,1)S(1)}, bf16[384,256]{1,0:T(8,128)(2,1)S(1)}, u32[]{:S(2)}, u32[]{:S(2)}) collective-permute-start(bf16[384,256]{1,0:T(8,128)(2,1)S(1)} %collective-permute-done.8.args_5_), channel_id=1, source_target_pairs={{0,1},{1,0},{2,3},{3,2},{4,5},{5,4},{6,7},{7,6},{8,9},{9,8},{10,11... | collective-permute-start | bytes 589832 | tf_op jit(solution)/shard_map/ppermute | solution.py:17
  18.5 3.0 %collective-permute-start.13 = (bf16[384,256]{1,0:T(8,128)(2,1)S(1)}, bf16[384,256]{1,0:T(8,128)(2,1)S(1)}, u32[]{:S(2)}, u32[]{:S(2)}) collective-permute-start(bf16[384,256]{1,0:T(8,128)(2,1)S(1)} %collective-permute-done.12.args_9_), channel_id=1, source_target_pairs={{0,1},{1,0},{2,3},{3,2},{4,5},{5,4},{6,7},{7,6},{8,9},{9,8},{10,11... | collective-permute-start | bytes 589832 | tf_op jit(solution)/shard_map/ppermute | solution.py:17
  25.3 3.9 %collective-permute-start.14 = (bf16[128,256]{1,0:T(8,128)(2,1)S(1)}, bf16[128,256]{1,0:T(8,128)(2,1)S(1)}, u32[]{:S(2)}, u32[]{:S(2)}) collective-permute-start(bf16[128,256]{1,0:T(8,128)(2,1)S(1)} %get-tuple-element.38), channel_id=1, source_target_pairs={{0,1},{1,0},{2,3},{3,2},{4,5},{5,4},{6,7},{7,6},{8,9},{9,8},{10,11... | collective-permute-start | bytes 196616 | tf_op jit(solution)/shard_map/ppermute | solution.py:17
  25.3 28.7 %collective-permute-start.16 = (bf16[384,256]{1,0:T(8,128)(2,1)S(1)}, bf16[384,256]{1,0:T(8,128)(2,1)S(1)}, u32[]{:S(2)}, u32[]{:S(2)}) collective-permute-start(bf16[384,256]{1,0:T(8,128)(2,1)S(1)} %get-tuple-element.43), channel_id=1, source_target_pairs={{0,24},{8,16},{16,8},{24,0},{1,25},{9,17},{17,9},{25,1},{2,26},{10... | collective-permute-start | bytes 589832 | tf_op jit(solution)/shard_map/ppermute | solution.py:17
  27.6 26.5 %collective-permute-start.17 = (bf16[384,256]{1,0:T(8,128)(2,1)S(1)}, bf16[384,256]{1,0:T(8,128)(2,1)S(1)}, u32[]{:S(2)}, u32[]{:S(2)}) collective-permute-start(bf16[384,256]{1,0:T(8,128)(2,1)S(1)} %get-tuple-element.44), channel_id=1, source_target_pairs={{0,16},{8,24},{16,0},{24,8},{1,17},{9,25},{17,1},{25,9},{2,18},{10... | collective-permute-start | bytes 589832 | tf_op jit(solution)/shard_map/ppermute | solution.py:17
  29.2 4.3 %collective-permute-start.15 = (bf16[128,256]{1,0:T(8,128)(2,1)S(1)}, bf16[128,256]{1,0:T(8,128)(2,1)S(1)}, u32[]{:S(2)}, u32[]{:S(2)}) collective-permute-start(bf16[128,256]{1,0:T(8,128)(2,1)S(1)} %add_convert_fusion.4), channel_id=1, source_target_pairs={{0,2},{1,3},{2,0},{3,1},{4,6},{5,7},{6,4},{7,5},{8,10},{9,11},{10,... | collective-permute-start | bytes 196616 | tf_op jit(solution)/shard_map/ppermute | solution.py:17
  32.9 21.2 %collective-permute-start.18 = (bf16[384,256]{1,0:T(8,128)(2,1)S(1)}, bf16[384,256]{1,0:T(8,128)(2,1)S(1)}, u32[]{:S(2)}, u32[]{:S(2)}) collective-permute-start(bf16[384,256]{1,0:T(8,128)(2,1)S(1)} %get-tuple-element.46), channel_id=1, source_target_pairs={{0,8},{8,0},{16,24},{24,16},{1,9},{9,1},{17,25},{25,17},{2,10},{10... | collective-permute-start | bytes 589832 | tf_op jit(solution)/shard_map/ppermute | solution.py:17
  33.6 4.3 %collective-permute-start = (bf16[128,256]{1,0:T(8,128)(2,1)S(1)}, bf16[128,256]{1,0:T(8,128)(2,1)S(1)}, u32[]{:S(2)}, u32[]{:S(2)}) collective-permute-start(bf16[128,256]{1,0:T(8,128)(2,1)S(1)} %get-tuple-element.5), channel_id=1, source_target_pairs={{0,4},{1,5},{2,6},{3,7},{4,0},{5,1},{6,2},{7,3},{8,12},{9,13},{10,... | collective-permute-start | bytes 196616 | tf_op jit(solution)/shard_map/cond/branch_1_fun/ppermute | solution.py:17
  38.0 5.6 %collective-permute-start.1 = (bf16[128,256]{1,0:T(8,128)(2,1)S(1)}, bf16[128,256]{1,0:T(8,128)(2,1)S(1)}, u32[]{:S(2)}, u32[]{:S(2)}) collective-permute-start(bf16[128,256]{1,0:T(8,128)(2,1)S(1)} %add_convert_fusion.2), channel_id=1, source_target_pairs={{0,8},{8,0},{16,24},{24,16},{1,9},{9,1},{17,25},{25,17},{2,10},{10... | collective-permute-start | bytes 196616 | tf_op jit(solution)/shard_map/cond/branch_1_fun/ppermute | solution.py:17
  39.4 14.7 %all-to-all-start = ((bf16[8,144,256]{2,1,0:T(8,128)(2,1)}), bf16[8,144,256]{2,1,0:T(8,128)(2,1)}, u32[]{:S(2)}, u32[]{:S(2)}) async-start(bf16[8,144,256]{2,1,0:T(8,128)(2,1)} %get-tuple-element.4), calls=%async_computation | async-start | bytes 1179648 | tf_op jit(solution)/shard_map/cond/branch_1_fun/all_to_all | solution.py:161
  43.6 6.7 %collective-permute-start.2 = (bf16[128,256]{1,0:T(8,128)(2,1)S(1)}, bf16[128,256]{1,0:T(8,128)(2,1)S(1)}, u32[]{:S(2)}, u32[]{:S(2)}) collective-permute-start(bf16[128,256]{1,0:T(8,128)(2,1)S(1)} %add_convert_fusion.1), channel_id=1, source_target_pairs={{0,16},{8,24},{16,0},{24,8},{1,17},{9,25},{17,1},{25,9},{2,18},{10... | collective-permute-start | bytes 196616 | tf_op jit(solution)/shard_map/cond/branch_1_fun/ppermute | solution.py:17
  51.0 1.6 %collective-permute-start.3 = (bf16[128,256]{1,0:T(8,128)(2,1)}, bf16[128,256]{1,0:T(8,128)(2,1)}, u32[]{:S(2)}, u32[]{:S(2)}) collective-permute-start(bf16[128,256]{1,0:T(8,128)(2,1)} %add_convert_fusion), channel_id=1, source_target_pairs={{0,1},{1,0},{2,3},{3,2},{4,5},{5,4},{6,7},{7,6},{8,9},{9,8},{10,11... | collective-permute-start | bytes 196616 | tf_op jit(solution)/shard_map/cond/branch_1_fun/ppermute | solution.py:17

commit v5 on v4

--- a/solution.py
+++ b/solution.py
@@ -125,11 +125,14 @@
     return (part.astype(F32) + swapped(part, axis, k).astype(F32)).astype(BF16)
 
 
-def finish(cap, edge, scale, me_ref, part_ref, other_ref, coming_ref, *args):
-    terms, (out_ref, weight_ref) = args[:-2], args[-2:]
+def join(scale, me_ref, part_ref, other_ref, out_ref):
     half, core = part_ref.shape[0], me_ref[1] & 1
-    weight_ref[pl.ds(pl.multiple_of(core * half, half), half), :] = (part_ref[...].astype(F32) * scale).astype(BF16)
-    weight_ref[pl.ds(pl.multiple_of((1 - core) * half, half), half), :] = (other_ref[...].astype(F32) * scale).astype(BF16)
+    out_ref[pl.ds(pl.multiple_of(core * half, half), half), :] = (part_ref[...].astype(F32) * scale).astype(BF16)
+    out_ref[pl.ds(pl.multiple_of((1 - core) * half, half), half), :] = (other_ref[...].astype(F32) * scale).astype(BF16)
+
+
+def finish(cap, edge, coming_ref, *args):
+    terms, out_ref = args[:-1], args[-1]
     for j in range(out_ref.shape[0] // edge):
         part = slice(j * edge, (j + 1) * edge)
         total = terms[0][part, :].astype(F32)
@@ -159,10 +162,10 @@
 
     def exchange(outer, part):
         coming = lax.all_to_all(outer, "dom", split_axis=0, concat_axis=0, tiled=True)
-        for axis, k, size in (("dom", 4, doms), ("rep", 1, count)):
+        for axis, k, size in (("dom", 2, 4), ("rep", 1, count)):
             while k < size:
                 part, k = joined(part, axis, k), 2 * k
-        return coming, part, swapped(part, "dom", 1)
+        return coming, call(functools.partial(join, scale), [shape((width, width), BF16)], (me, part, swapped(part, "dom", 1)), "svv", name="join")[0]
 
     near = swapped(feats, "dom", 1)
     even = [feats] + [swapped(feats if k == 4 else after(feats, near), "dom", k) for k in range(2, doms, 2)]
@@ -187,15 +190,13 @@
         flops=10**9, name="layer")
     part = (keep.astype(F32) + swapped(give, "dom", 1).astype(F32)).astype(BF16)
     first = part
-    part = joined(part, "dom", 2)
+    part = joined(part, "dom", 4)
     got = [terms[0]] + [swapped(after(terms[count - k], first if k == 1 else None), "rep", k) for k in range(count - 1, 0, -1)]
     outer = call(
         spread_outer, [shape((doms, cap * (edge + 16), width), BF16)], (requests, off_ref, off_vals, grad_agg), "ssvv",
         scratch=[pltpu.VMEM((slots, edge, width), F32)], flops=10**9, name="outer")[0]
-    coming, part, other = fenced(sure, exchange, outer, part)
-    grad_feats, grad_weight = call(
-        functools.partial(finish, cap, edge, scale), [flat, shape((width, width), BF16)],
-        (me, part, other, coming, *got), "s" + "v" * (count + 3), name="finish")
+    coming, grad_weight = fenced(sure, exchange, outer, part)
+    grad_feats = call(functools.partial(finish, cap, edge), [flat], (coming, *got), "v" * (count + 1), name="finish")[0]
     return (activated, grad_feats, grad_weight)
 
 

time: 56.6 us -> 55.8 us (0.986)
  waiting for transfers between devices: 16.8 us -> 15.9 us
  other arithmetic: 0.82 us -> 0.2 us
    ppermute x18, waiting for transfers between devices: 12.4 us -> 11.6 us  [swapped(): lax.ppermute(value, axis, [(i, i ^ k) for i in range(lax.axis_size(axis))])]
    convert_element_type x4, other arithmetic: 0.69 us -> 0.08 us  [joined(): return (part.astype(F32) + swapped(part, axis, k).astype(F32)).astype(BF16)]
    pallas_call x4 -> x5, Pallas kernels: 9.05 us -> 9.57 us  [call(): pl.pallas_call(body, out_shape=outs, in_specs=[pl.BlockSpec(memory_space=...]
    unnamed x18 -> x20, local copies, waits for them, and re-layouts: 1.85 us -> 1.85 us
  transfers between devices with their start and end apart: 20 -> 20, of which waited for: 8 -> 8; matrix products, arithmetic and copies ran while one was open for 1% -> 0% of each run, Pallas kernels for 5% -> 7%
where the time goes in v5:
time: 55.8 us; the launch traced here: 55.5 us
  starting transfers between devices  27.1 us (49%)
  waiting for transfers between devices  15.9 us (28%)
  Pallas kernels  9.57 us (17%)
  local copies, waits for them, and re-layouts  1.85 us (3%)
  between operations  0.8 us (1%)
    ppermute x18, starting transfers between devices, swapped(): lax.ppermute(value, axis, [(i, i ^ k) for i in range(lax.axis_size(axis))])  18.6 us
    ppermute x18, waiting for transfers between devices, swapped(): lax.ppermute(value, axis, [(i, i ^ k) for i in range(lax.axis_size(axis))])  11.6 us
    pallas_call x5, Pallas kernels, call(): pl.pallas_call(body, out_shape=outs, in_specs=[pl.BlockSpec(memory_space=...  9.57 us
    ppermute x1, starting transfers between devices, relayed(): return lax.ppermute(value, 'rep', [pair[::turns] for pair in pairs])  4.25 us
    all_to_all x1, starting transfers between devices, exchange(): lax.all_to_all(outer, 'dom', split_axis=0, concat_axis=0, tiled=True)  4.19 us
    ppermute x1, waiting for transfers between devices, relayed(): return lax.ppermute(value, 'rep', [pair[::turns] for pair in pairs])  2.97 us
    unnamed x20, local copies, waits for them, and re-layouts  1.85 us
    all_to_all x1, waiting for transfers between devices, exchange(): lax.all_to_all(outer, 'dom', split_axis=0, concat_axis=0, tiled=True)  1.39 us
  transfers between devices with their start and end apart: 20, of which 8 were waited for; matrix products, arithmetic and copies ran while one was open for 0% of the time, Pallas kernels for 7%

profile of v5, /device:TPU:0, one launch (start us, length us, event | category | flops | bytes accessed | tf_op | source)
XLA Modules:
  0.0 55.5 jit_solution(4598590475702916306)
XLA Ops:
  0.6 0.5 collective-permute-start.7
  1.1 2.6 %collective-permute-start.9 = (bf16[384,256]{1,0:T(8,128)(2,1)}, bf16[384,256]{1,0:T(8,128)(2,1)S(1)}, u32[]{:S(2)}, u32[]{:S(2)}) collective-permute-start(bf16[384,256]{1,0:T(8,128)(2,1)} %args_0_.4), channel_id=1, source_target_pairs={{0,4},{1,5},{2,6},{3,7},{4,0},{5,1},{6,2},{7,3},{8,12},{9,13},{10,... | collective-permute-start | bytes 589832 | tf_op jit(solution)/shard_map/ppermute | solution.py:17
  3.7 3.6 %collective-permute-start.4 = (bf16[384,256]{1,0:T(8,128)(2,1)}, bf16[384,256]{1,0:T(8,128)(2,1)S(1)}, u32[]{:S(2)}, u32[]{:S(2)}) collective-permute-start(bf16[384,256]{1,0:T(8,128)(2,1)} %args_0_.4), channel_id=1, source_target_pairs={{0,24},{8,16},{16,8},{24,0},{1,25},{9,17},{17,9},{25,1},{2,26},{10... | collective-permute-start | bytes 589832 | tf_op jit(solution)/shard_map/ppermute | solution.py:17
  7.3 0.1 pad_add_fusion.me_ref
  7.4 1.5 %collective-permute-start.8 = (bf16[384,256]{1,0:T(8,128)(2,1)}, bf16[384,256]{1,0:T(8,128)(2,1)S(1)}, u32[]{:S(2)}, u32[]{:S(2)}) collective-permute-start(bf16[384,256]{1,0:T(8,128)(2,1)} %args_0_.4), channel_id=1, source_target_pairs={{0,2},{1,3},{2,0},{3,1},{4,6},{5,7},{6,4},{7,5},{8,10},{9,11},{10,... | collective-permute-start | bytes 589832 | tf_op jit(solution)/shard_map/ppermute | solution.py:17
  8.9 0.5 collective-permute-start.12
  9.4 1.1 %copy-done.1 = bf16[3,4,2,128,128]{4,3,2,1,0:T(8,128)(2,1)S(1)} copy-done((bf16[3,4,2,128,128]{4,3,2,1,0:T(8,128)(2,1)S(1)}, bf16[3,4,2,128,128]{4,3,2,1,0:T(8,128)(2,1)}, u32[]{:S(2)}) %copy-start.1) | copy-done | bytes 786456
  10.6 0.7 %copy-done.5 = s32[3,4,2]{1,2,0:T(2,128)S(1)} copy-done((s32[3,4,2]{1,2,0:T(2,128)S(1)}, s32[3,4,2]{1,2,0:T(2,128)}, u32[]{:S(2)}) %copy-start.5) | copy-done | bytes 120
  11.3 0.9 %arrange.1.args_11_ = bf16[384,1536]{1,0:T(8,128)(2,1)S(1)} custom-call(s32[2]{0:T(128)S(1)} %pad_add_fusion.me_ref, s32[3,2,4]{2,1,0:T(2,128)S(1)} %bitcast.7, bf16[3,4,2,128,128]{4,3,2,1,0:T(8,128)(2,1)S(1)} %copy-done.1), custom_call_target="tpu_custom_call" | custom-call | bytes 1966184 | tf_op jit(solution)/shard_map/arrange/pallas_call | solution.py:38
  12.2 0.1 collective-permute-start.11
  12.3 1.2 %collective-permute-done.4.args_1_ = bf16[384,256]{1,0:T(8,128)(2,1)S(1)} collective-permute-done((bf16[384,256]{1,0:T(8,128)(2,1)}, bf16[384,256]{1,0:T(8,128)(2,1)S(1)}, u32[]{:S(2)}, u32[]{:S(2)}) %collective-permute-start.4) | collective-permute-done | bytes 196640 | tf_op jit(solution)/shard_map/ppermute | solution.py:17
  13.6 4.3 %collective-permute-start.5 = (bf16[384,256]{1,0:T(8,128)(2,1)S(1)}, bf16[384,256]{1,0:T(8,128)(2,1)S(1)}, u32[]{:S(2)}, u32[]{:S(2)}) collective-permute-start(bf16[384,256]{1,0:T(8,128)(2,1)S(1)} %broadcast_select_fusion), channel_id=1, source_target_pairs={{8,0},{24,8},{16,24},{0,16},{9,1},{25,9},{17,25},{1,17},{10,2},{26... | collective-permute-start | bytes 589832 | tf_op jit(solution)/shard_map/ppermute | solution.py:22
  17.8 0.7 %collective-permute-done.12.args_9_ = bf16[384,256]{1,0:T(8,128)(2,1)S(1)} collective-permute-done((bf16[384,256]{1,0:T(8,128)(2,1)}, bf16[384,256]{1,0:T(8,128)(2,1)S(1)}, u32[]{:S(2)}, u32[]{:S(2)}) %collective-permute-start.12) | collective-permute-done | bytes 196640 | tf_op jit(solution)/shard_map/ppermute | solution.py:17
  18.5 3.0 %collective-permute-done.5.args_2_ = bf16[384,256]{1,0:T(8,128)(2,1)S(1)} collective-permute-done((bf16[384,256]{1,0:T(8,128)(2,1)S(1)}, bf16[384,256]{1,0:T(8,128)(2,1)S(1)}, u32[]{:S(2)}, u32[]{:S(2)}) %collective-permute-start.5) | collective-permute-done | bytes 196640 | tf_op jit(solution)/shard_map/ppermute | solution.py:22
  21.5 3.7 %layer.1 = (bf16[384,256]{1,0:T(8,128)(2,1)}, bf16[128,256]{1,0:T(8,128)(2,1)S(1)}, bf16[128,256]{1,0:T(8,128)(2,1)S(1)}, bf16[384,256]{1,0:T(8,128)(2,1)S(1)}, ...) custom-call(s32[2]{0:T(128)S(1)} %pad_add_fusion.me_ref, ...), custom_call_target="tpu_custom_call" | custom-call | flops 1000000000 | bytes 5866644 | tf_op jit(solution)/shard_map/layer/pallas_call | solution.py:38
  25.3 2.3 %collective-permute-start.16 = (bf16[384,256]{1,0:T(8,128)(2,1)S(1)}, bf16[384,256]{1,0:T(8,128)(2,1)S(1)}, u32[]{:S(2)}, u32[]{:S(2)}) collective-permute-start(bf16[384,256]{1,0:T(8,128)(2,1)S(1)} %get-tuple-element.41), channel_id=1, source_target_pairs={{0,24},{8,16},{16,8},{24,0},{1,25},{9,17},{17,9},{25,1},{2,26},{10... | collective-permute-start | bytes 589832 | tf_op jit(solution)/shard_map/ppermute | solution.py:17
  27.6 1.6 %collective-permute-start.17 = (bf16[384,256]{1,0:T(8,128)(2,1)S(1)}, bf16[384,256]{1,0:T(8,128)(2,1)S(1)}, u32[]{:S(2)}, u32[]{:S(2)}) collective-permute-start(bf16[384,256]{1,0:T(8,128)(2,1)S(1)} %get-tuple-element.42), channel_id=1, source_target_pairs={{0,16},{8,24},{16,0},{24,8},{1,17},{9,25},{17,1},{25,9},{2,18},{10... | collective-permute-start | bytes 589832 | tf_op jit(solution)/shard_map/ppermute | solution.py:17
  29.2 0.6 %collective-permute-start.15 = (bf16[128,256]{1,0:T(8,128)(2,1)S(1)}, bf16[128,256]{1,0:T(8,128)(2,1)S(1)}, u32[]{:S(2)}, u32[]{:S(2)}) collective-permute-start(bf16[128,256]{1,0:T(8,128)(2,1)S(1)} %add_convert_fusion.4), channel_id=1, source_target_pairs={{0,4},{1,5},{2,6},{3,7},{4,0},{5,1},{6,2},{7,3},{8,12},{9,13},{10,... | collective-permute-start | bytes 196616 | tf_op jit(solution)/shard_map/ppermute | solution.py:17
  29.8 2.1 %outer.1 = bf16[8,144,256]{2,1,0:T(8,128)(2,1)} custom-call(s32[1,8]{1,0:T(1,128)S(1)} %bitcast.11, s32[3,9]{1,0:T(4,128)S(1)} %copy-done.6, bf16[3,9,128,128]{3,2,1,0:T(8,128)(2,1)S(1)} %copy-done, bf16[384,256]{1,0:T(8,128)(2,1)S(1)} %get-tuple-element.36.grad_ref), custom_call_target="tpu_custom_call" | custom-call | flops 1000000000 | bytes 1671308 | tf_op jit(solution)/shard_map/outer/pallas_call | solution.py:38
  31.9 0.6 %collective-permute-start.18 = (bf16[384,256]{1,0:T(8,128)(2,1)S(1)}, bf16[384,256]{1,0:T(8,128)(2,1)S(1)}, u32[]{:S(2)}, u32[]{:S(2)}) collective-permute-start(bf16[384,256]{1,0:T(8,128)(2,1)S(1)} %get-tuple-element.44), channel_id=1, source_target_pairs={{0,8},{8,0},{16,24},{24,16},{1,9},{9,1},{17,25},{25,17},{2,10},{10... | collective-permute-start | bytes 589832 | tf_op jit(solution)/shard_map/ppermute | solution.py:17
  32.5 1.1 %collective-permute-done.15 = bf16[128,256]{1,0:T(8,128)(2,1)S(1)} collective-permute-done((bf16[128,256]{1,0:T(8,128)(2,1)S(1)}, bf16[128,256]{1,0:T(8,128)(2,1)S(1)}, u32[]{:S(2)}, u32[]{:S(2)}) %collective-permute-start.15) | collective-permute-done | bytes 65568 | tf_op jit(solution)/shard_map/ppermute | solution.py:17
  33.6 19.7 %conditional.1 = (bf16[8,144,256]{2,1,0:T(8,128)(2,1)}, bf16[256,256]{1,0:T(8,128)(2,1)S(1)}) conditional(s32[]{:T(128)} %bitcast.5, () %tuple.29, (bf16[8,144,256]{2,1,0:T(8,128)(2,1)}, bf16[128,256]{1,0:T(8,128)(2,1)S(1)}, s32[2]{0:T(128)S(1)}) %tuple.30), branch_computations={%region_0.1_spmd, %region_1.2_spmd} | conditional | flops 393216 | bytes 3670232 | solution.py:31
  33.6 1.6 %collective-permute-start = (bf16[128,256]{1,0:T(8,128)(2,1)S(1)}, bf16[128,256]{1,0:T(8,128)(2,1)S(1)}, u32[]{:S(2)}, u32[]{:S(2)}) collective-permute-start(bf16[128,256]{1,0:T(8,128)(2,1)S(1)} %get-tuple-element.8), channel_id=1, source_target_pairs={{0,2},{1,3},{2,0},{3,1},{4,6},{5,7},{6,4},{7,5},{8,10},{9,11},{10,... | collective-permute-start | bytes 196616 | tf_op jit(solution)/shard_map/cond/branch_1_fun/ppermute | solution.py:17
  35.2 2.8 %collective-permute-done = bf16[128,256]{1,0:T(8,128)(2,1)S(1)} collective-permute-done((bf16[128,256]{1,0:T(8,128)(2,1)S(1)}, bf16[128,256]{1,0:T(8,128)(2,1)S(1)}, u32[]{:S(2)}, u32[]{:S(2)}) %collective-permute-start) | collective-permute-done | bytes 65568 | tf_op jit(solution)/shard_map/cond/branch_1_fun/ppermute | solution.py:17
  38.0 0.6 %collective-permute-start.1 = (bf16[128,256]{1,0:T(8,128)(2,1)S(1)}, bf16[128,256]{1,0:T(8,128)(2,1)S(1)}, u32[]{:S(2)}, u32[]{:S(2)}) collective-permute-start(bf16[128,256]{1,0:T(8,128)(2,1)S(1)} %add_convert_fusion.2), channel_id=1, source_target_pairs={{0,8},{8,0},{16,24},{24,16},{1,9},{9,1},{17,25},{25,17},{2,10},{10... | collective-permute-start | bytes 196616 | tf_op jit(solution)/shard_map/cond/branch_1_fun/ppermute | solution.py:17
  38.6 4.2 %all-to-all-start = ((bf16[8,144,256]{2,1,0:T(8,128)(2,1)}), bf16[8,144,256]{2,1,0:T(8,128)(2,1)}, u32[]{:S(2)}, u32[]{:S(2)}) async-start(bf16[8,144,256]{2,1,0:T(8,128)(2,1)} %get-tuple-element.6), calls=%async_computation | async-start | bytes 1179648 | tf_op jit(solution)/shard_map/cond/branch_1_fun/all_to_all | solution.py:164
  42.8 2.6 %collective-permute-start.2 = (bf16[128,256]{1,0:T(8,128)(2,1)S(1)}, bf16[128,256]{1,0:T(8,128)(2,1)S(1)}, u32[]{:S(2)}, u32[]{:S(2)}) collective-permute-start(bf16[128,256]{1,0:T(8,128)(2,1)S(1)} %add_convert_fusion.1), channel_id=1, source_target_pairs={{0,16},{8,24},{16,0},{24,8},{1,17},{9,25},{17,1},{25,9},{2,18},{10... | collective-permute-start | bytes 196616 | tf_op jit(solution)/shard_map/cond/branch_1_fun/ppermute | solution.py:17
  45.4 4.6 %collective-permute-done.2 = bf16[128,256]{1,0:T(8,128)(2,1)S(1)} collective-permute-done((bf16[128,256]{1,0:T(8,128)(2,1)S(1)}, bf16[128,256]{1,0:T(8,128)(2,1)S(1)}, u32[]{:S(2)}, u32[]{:S(2)}) %collective-permute-start.2) | collective-permute-done | bytes 65568 | tf_op jit(solution)/shard_map/cond/branch_1_fun/ppermute | solution.py:17
  50.0 1.2 %collective-permute-done.3.other_ref = bf16[128,256]{1,0:T(8,128)(2,1)S(1)} collective-permute-done((bf16[128,256]{1,0:T(8,128)(2,1)S(1)}, bf16[128,256]{1,0:T(8,128)(2,1)S(1)}, u32[]{:S(2)}, u32[]{:S(2)}) %collective-permute-start.3) | collective-permute-done | bytes 65568 | tf_op jit(solution)/shard_map/cond/branch_1_fun/ppermute | solution.py:17
  51.3 0.6 %join.1 = bf16[256,256]{1,0:T(8,128)(2,1)S(1)} custom-call(s32[2]{0:T(128)S(1)} %get-tuple-element.7.me_ref, bf16[128,256]{1,0:T(8,128)(2,1)S(1)} %add_convert_fusion.part_ref, bf16[128,256]{1,0:T(8,128)(2,1)S(1)} %collective-permute-done.3.other_ref), custom_call_target="tpu_custom_call" | custom-call | bytes 262152 | tf_op jit(solution)/shard_map/cond/branch_1_fun/join/pallas_call | solution.py:38
  51.9 1.4 %all-to-all-done = bf16[8,144,256]{2,1,0:T(8,128)(2,1)} async-done(((bf16[8,144,256]{2,1,0:T(8,128)(2,1)}), bf16[8,144,256]{2,1,0:T(8,128)(2,1)}, u32[]{:S(2)}, u32[]{:S(2)}) %all-to-all-start) | async-done | bytes 589856 | tf_op jit(solution)/shard_map/cond/branch_1_fun/all_to_all | solution.py:164
  53.3 2.2 %finish.1 = bf16[384,256]{1,0:T(8,128)(2,1)} custom-call(bf16[8,144,256]{2,1,0:T(8,128)(2,1)} %get-tuple-element.39.coming_ref, bf16[384,256]{1,0:T(8,128)(2,1)S(1)} %get-tuple-element.40.args_0_, bf16[384,256]{1,0:T(8,128)(2,1)S(1)} %collective-permute-done.16.args_1_, bf16[384,256]{1,0:T(8,128)(2,1)S(1)} %collective-permute-done.17.args_2_, ...), custom_call_target="tpu_custom_call" | custom-call | bytes 1572864 | tf_op jit(solution)/shard_map/finish/pallas_call | solution.py:38
  (41 shorter events, 0.3 us)
Async XLA Ops:
  0.6 6.8 %collective-permute-start.7 = (bf16[384,256]{1,0:T(8,128)(2,1)}, bf16[384,256]{1,0:T(8,128)(2,1)S(1)}, u32[]{:S(2)}, u32[]{:S(2)}) collective-permute-start(bf16[384,256]{1,0:T(8,128)(2,1)} %args_0_.4), channel_id=1, source_target_pairs={{0,1},{1,0},{2,3},{3,2},{4,5},{5,4},{6,7},{7,6},{8,9},{9,8},{10,11... | collective-permute-start | bytes 589832 | tf_op jit(solution)/shard_map/ppermute | solution.py:17
  1.1 8.3 %collective-permute-start.9 = (bf16[384,256]{1,0:T(8,128)(2,1)}, bf16[384,256]{1,0:T(8,128)(2,1)S(1)}, u32[]{:S(2)}, u32[]{:S(2)}) collective-permute-start(bf16[384,256]{1,0:T(8,128)(2,1)} %args_0_.4), channel_id=1, source_target_pairs={{0,4},{1,5},{2,6},{3,7},{4,0},{5,1},{6,2},{7,3},{8,12},{9,13},{10,... | collective-permute-start | bytes 589832 | tf_op jit(solution)/shard_map/ppermute | solution.py:17
  3.7 9.8 %collective-permute-start.4 = (bf16[384,256]{1,0:T(8,128)(2,1)}, bf16[384,256]{1,0:T(8,128)(2,1)S(1)}, u32[]{:S(2)}, u32[]{:S(2)}) collective-permute-start(bf16[384,256]{1,0:T(8,128)(2,1)} %args_0_.4), channel_id=1, source_target_pairs={{0,24},{8,16},{16,8},{24,0},{1,25},{9,17},{17,9},{25,1},{2,26},{10... | collective-permute-start | bytes 589832 | tf_op jit(solution)/shard_map/ppermute | solution.py:17
  7.3 11.2 %collective-permute-start.6 = (bf16[384,256]{1,0:T(8,128)(2,1)}, bf16[384,256]{1,0:T(8,128)(2,1)S(1)}, u32[]{:S(2)}, u32[]{:S(2)}) collective-permute-start(bf16[384,256]{1,0:T(8,128)(2,1)} %args_0_.4), channel_id=1, source_target_pairs={{0,8},{8,0},{16,24},{24,16},{1,9},{9,1},{17,25},{25,17},{2,10},{10... | collective-permute-start | bytes 589832 | tf_op jit(solution)/shard_map/ppermute | solution.py:17
  7.4 10.4 %collective-permute-start.8 = (bf16[384,256]{1,0:T(8,128)(2,1)}, bf16[384,256]{1,0:T(8,128)(2,1)S(1)}, u32[]{:S(2)}, u32[]{:S(2)}) collective-permute-start(bf16[384,256]{1,0:T(8,128)(2,1)} %args_0_.4), channel_id=1, source_target_pairs={{0,2},{1,3},{2,0},{3,1},{4,6},{5,7},{6,4},{7,5},{8,10},{9,11},{10,... | collective-permute-start | bytes 589832 | tf_op jit(solution)/shard_map/ppermute | solution.py:17
  8.9 9.6 %collective-permute-start.12 = (bf16[384,256]{1,0:T(8,128)(2,1)}, bf16[384,256]{1,0:T(8,128)(2,1)S(1)}, u32[]{:S(2)}, u32[]{:S(2)}) collective-permute-start(bf16[384,256]{1,0:T(8,128)(2,1)} %args_0_.4), channel_id=1, source_target_pairs={{0,6},{1,7},{2,4},{3,5},{4,2},{5,3},{6,0},{7,1},{8,14},{9,15},{10,... | collective-permute-start | bytes 589832 | tf_op jit(solution)/shard_map/ppermute | solution.py:17
  9.4 1.1 %copy-start.1 = (bf16[3,4,2,128,128]{4,3,2,1,0:T(8,128)(2,1)S(1)}, bf16[3,4,2,128,128]{4,3,2,1,0:T(8,128)(2,1)}, u32[]{:S(2)}) copy-start(bf16[3,4,2,128,128]{4,3,2,1,0:T(8,128)(2,1)} %in_hbm.1) | copy-start | bytes 2359300
  10.6 0.7 %copy-start.5 = (s32[3,4,2]{1,2,0:T(2,128)S(1)}, s32[3,4,2]{1,2,0:T(2,128)}, u32[]{:S(2)}) copy-start(s32[3,4,2]{1,2,0:T(2,128)} %param.16) | copy-start | bytes 292
  11.3 2.3 %copy-start.2 = (bf16[384,256]{1,0:T(8,128)(2,1)S(1)}, bf16[384,256]{1,0:T(8,128)(2,1)}, u32[]{:S(2)}) copy-start(bf16[384,256]{1,0:T(8,128)(2,1)} %args_0_.4) | copy-start | bytes 589828
  11.3 10.2 %copy-start = (bf16[3,9,128,128]{3,2,1,0:T(8,128)(2,1)S(1)}, bf16[3,9,128,128]{3,2,1,0:T(8,128)(2,1)}, u32[]{:S(2)}) copy-start(bf16[3,9,128,128]{3,2,1,0:T(8,128)(2,1)} %off_ref.1) | copy-start | bytes 2654212
  11.3 10.2 %copy-start.3 = (bf16[384,256]{1,0:T(8,128)(2,1)S(1)}, bf16[384,256]{1,0:T(8,128)(2,1)}, u32[]{:S(2)}) copy-start(bf16[384,256]{1,0:T(8,128)(2,1)} %args_15_.1) | copy-start | bytes 589828
  11.3 10.2 %copy-start.4 = (bf16[256,256]{1,0:T(8,128)(2,1)S(1)}, bf16[256,256]{1,0:T(8,128)(2,1)}, u32[]{:S(2)}) copy-start(bf16[256,256]{1,0:T(8,128)(2,1)} %args_13_.1) | copy-start | bytes 393220
  11.3 10.2 %copy-start.6 = (s32[3,9]{1,0:T(4,128)S(1)}, s32[3,9]{1,0:T(4,128)}, u32[]{:S(2)}) copy-start(s32[3,9]{1,0:T(4,128)} %refs_ref.3) | copy-start | bytes 328
  11.3 10.2 %copy-start.7 = (f32[256]{0:T(256)S(1)}, f32[256]{0:T(256)}, u32[]{:S(2)}) copy-start(f32[256]{0:T(256)} %param.14) | copy-start | bytes 3076
  11.3 10.2 %copy-start.8 = (s32[1,1,8,1]{2,3,1,0:T(1,128)S(1)}, s32[1,1,8,1]{2,3,1,0:T(1,128)}, u32[]{:S(2)}) copy-start(s32[1,1,8,1]{2,3,1,0:T(1,128)} %param.19) | copy-start | bytes 100
  12.2 6.3 %collective-permute-start.11 = (bf16[384,256]{1,0:T(8,128)(2,1)S(1)}, bf16[384,256]{1,0:T(8,128)(2,1)S(1)}, u32[]{:S(2)}, u32[]{:S(2)}) collective-permute-start(bf16[384,256]{1,0:T(8,128)(2,1)S(1)} %collective-permute-done.9.args_7_), channel_id=1, source_target_pairs={{0,1},{1,0},{2,3},{3,2},{4,5},{5,4},{6,7},{7,6},{8,9},{9,8},{10,11... | collective-permute-start | bytes 589832 | tf_op jit(solution)/shard_map/ppermute | solution.py:17
  13.6 7.9 %collective-permute-start.5 = (bf16[384,256]{1,0:T(8,128)(2,1)S(1)}, bf16[384,256]{1,0:T(8,128)(2,1)S(1)}, u32[]{:S(2)}, u32[]{:S(2)}) collective-permute-start(bf16[384,256]{1,0:T(8,128)(2,1)S(1)} %broadcast_select_fusion), channel_id=1, source_target_pairs={{8,0},{24,8},{16,24},{0,16},{9,1},{25,9},{17,25},{1,17},{10,2},{26... | collective-permute-start | bytes 589832 | tf_op jit(solution)/shard_map/ppermute | solution.py:22
  17.8 3.7 %collective-permute-start.10 = (bf16[384,256]{1,0:T(8,128)(2,1)S(1)}, bf16[384,256]{1,0:T(8,128)(2,1)S(1)}, u32[]{:S(2)}, u32[]{:S(2)}) collective-permute-start(bf16[384,256]{1,0:T(8,128)(2,1)S(1)} %collective-permute-done.8.args_5_), channel_id=1, source_target_pairs={{0,1},{1,0},{2,3},{3,2},{4,5},{5,4},{6,7},{7,6},{8,9},{9,8},{10,11... | collective-permute-start | bytes 589832 | tf_op jit(solution)/shard_map/ppermute | solution.py:17
  18.5 3.0 %collective-permute-start.13 = (bf16[384,256]{1,0:T(8,128)(2,1)S(1)}, bf16[384,256]{1,0:T(8,128)(2,1)S(1)}, u32[]{:S(2)}, u32[]{:S(2)}) collective-permute-start(bf16[384,256]{1,0:T(8,128)(2,1)S(1)} %collective-permute-done.12.args_9_), channel_id=1, source_target_pairs={{0,1},{1,0},{2,3},{3,2},{4,5},{5,4},{6,7},{7,6},{8,9},{9,8},{10,11... | collective-permute-start | bytes 589832 | tf_op jit(solution)/shard_map/ppermute | solution.py:17
  25.3 3.9 %collective-permute-start.14 = (bf16[128,256]{1,0:T(8,128)(2,1)S(1)}, bf16[128,256]{1,0:T(8,128)(2,1)S(1)}, u32[]{:S(2)}, u32[]{:S(2)}) collective-permute-start(bf16[128,256]{1,0:T(8,128)(2,1)S(1)} %get-tuple-element.38), channel_id=1, source_target_pairs={{0,1},{1,0},{2,3},{3,2},{4,5},{5,4},{6,7},{7,6},{8,9},{9,8},{10,11... | collective-permute-start | bytes 196616 | tf_op jit(solution)/shard_map/ppermute | solution.py:17
  25.3 27.9 %collective-permute-start.16 = (bf16[384,256]{1,0:T(8,128)(2,1)S(1)}, bf16[384,256]{1,0:T(8,128)(2,1)S(1)}, u32[]{:S(2)}, u32[]{:S(2)}) collective-permute-start(bf16[384,256]{1,0:T(8,128)(2,1)S(1)} %get-tuple-element.41), channel_id=1, source_target_pairs={{0,24},{8,16},{16,8},{24,0},{1,25},{9,17},{17,9},{25,1},{2,26},{10... | collective-permute-start | bytes 589832 | tf_op jit(solution)/shard_map/ppermute | solution.py:17
  27.6 25.7 %collective-permute-start.17 = (bf16[384,256]{1,0:T(8,128)(2,1)S(1)}, bf16[384,256]{1,0:T(8,128)(2,1)S(1)}, u32[]{:S(2)}, u32[]{:S(2)}) collective-permute-start(bf16[384,256]{1,0:T(8,128)(2,1)S(1)} %get-tuple-element.42), channel_id=1, source_target_pairs={{0,16},{8,24},{16,0},{24,8},{1,17},{9,25},{17,1},{25,9},{2,18},{10... | collective-permute-start | bytes 589832 | tf_op jit(solution)/shard_map/ppermute | solution.py:17
  29.2 4.3 %collective-permute-start.15 = (bf16[128,256]{1,0:T(8,128)(2,1)S(1)}, bf16[128,256]{1,0:T(8,128)(2,1)S(1)}, u32[]{:S(2)}, u32[]{:S(2)}) collective-permute-start(bf16[128,256]{1,0:T(8,128)(2,1)S(1)} %add_convert_fusion.4), channel_id=1, source_target_pairs={{0,4},{1,5},{2,6},{3,7},{4,0},{5,1},{6,2},{7,3},{8,12},{9,13},{10,... | collective-permute-start | bytes 196616 | tf_op jit(solution)/shard_map/ppermute | solution.py:17
  31.9 21.3 %collective-permute-start.18 = (bf16[384,256]{1,0:T(8,128)(2,1)S(1)}, bf16[384,256]{1,0:T(8,128)(2,1)S(1)}, u32[]{:S(2)}, u32[]{:S(2)}) collective-permute-start(bf16[384,256]{1,0:T(8,128)(2,1)S(1)} %get-tuple-element.44), channel_id=1, source_target_pairs={{0,8},{8,0},{16,24},{24,16},{1,9},{9,1},{17,25},{25,17},{2,10},{10... | collective-permute-start | bytes 589832 | tf_op jit(solution)/shard_map/ppermute | solution.py:17
  33.6 4.3 %collective-permute-start = (bf16[128,256]{1,0:T(8,128)(2,1)S(1)}, bf16[128,256]{1,0:T(8,128)(2,1)S(1)}, u32[]{:S(2)}, u32[]{:S(2)}) collective-permute-start(bf16[128,256]{1,0:T(8,128)(2,1)S(1)} %get-tuple-element.8), channel_id=1, source_target_pairs={{0,2},{1,3},{2,0},{3,1},{4,6},{5,7},{6,4},{7,5},{8,10},{9,11},{10,... | collective-permute-start | bytes 196616 | tf_op jit(solution)/shard_map/cond/branch_1_fun/ppermute | solution.py:17
  38.0 4.8 %collective-permute-start.1 = (bf16[128,256]{1,0:T(8,128)(2,1)S(1)}, bf16[128,256]{1,0:T(8,128)(2,1)S(1)}, u32[]{:S(2)}, u32[]{:S(2)}) collective-permute-start(bf16[128,256]{1,0:T(8,128)(2,1)S(1)} %add_convert_fusion.2), channel_id=1, source_target_pairs={{0,8},{8,0},{16,24},{24,16},{1,9},{9,1},{17,25},{25,17},{2,10},{10... | collective-permute-start | bytes 196616 | tf_op jit(solution)/shard_map/cond/branch_1_fun/ppermute | solution.py:17
  38.6 14.7 %all-to-all-start = ((bf16[8,144,256]{2,1,0:T(8,128)(2,1)}), bf16[8,144,256]{2,1,0:T(8,128)(2,1)}, u32[]{:S(2)}, u32[]{:S(2)}) async-start(bf16[8,144,256]{2,1,0:T(8,128)(2,1)} %get-tuple-element.6), calls=%async_computation | async-start | bytes 1179648 | tf_op jit(solution)/shard_map/cond/branch_1_fun/all_to_all | solution.py:164
  42.8 7.1 %collective-permute-start.2 = (bf16[128,256]{1,0:T(8,128)(2,1)S(1)}, bf16[128,256]{1,0:T(8,128)(2,1)S(1)}, u32[]{:S(2)}, u32[]{:S(2)}) collective-permute-start(bf16[128,256]{1,0:T(8,128)(2,1)S(1)} %add_convert_fusion.1), channel_id=1, source_target_pairs={{0,16},{8,24},{16,0},{24,8},{1,17},{9,25},{17,1},{25,9},{2,18},{10... | collective-permute-start | bytes 196616 | tf_op jit(solution)/shard_map/cond/branch_1_fun/ppermute | solution.py:17
  50.0 1.3 %collective-permute-start.3 = (bf16[128,256]{1,0:T(8,128)(2,1)S(1)}, bf16[128,256]{1,0:T(8,128)(2,1)S(1)}, u32[]{:S(2)}, u32[]{:S(2)}) collective-permute-start(bf16[128,256]{1,0:T(8,128)(2,1)S(1)} %add_convert_fusion.part_ref), channel_id=1, source_target_pairs={{0,1},{1,0},{2,3},{3,2},{4,5},{5,4},{6,7},{7,6},{8,9},{9,8},{10,11... | collective-permute-start | bytes 196616 | tf_op jit(solution)/shard_map/cond/branch_1_fun/ppermute | solution.py:17
  53.2 2.2 %copy-start.9 = (bf16[256,256]{1,0:T(8,128)(2,1)}, bf16[256,256]{1,0:T(8,128)(2,1)S(1)}, u32[]{:S(2)}) copy-start(bf16[256,256]{1,0:T(8,128)(2,1)S(1)} %get-tuple-element.28) | copy-start | bytes 393220

commit v6 on v5

--- a/solution.py
+++ b/solution.py
@@ -11,6 +11,10 @@
 F32, BF16 = jnp.float32, jnp.bfloat16
 ROOT = math.sqrt(2.0 / math.pi)
 CUBIC = 0.044715
+
+
+def turns(count):
+    return [0, 3, 1, 2] if count == 4 else [0] + list(range(count - 1, 0, -1))
 
 
 def swapped(value, axis, k):
@@ -57,7 +61,7 @@
     for b in range(blocks):
         copies[b].wait()
         for n in range(count):
-            s = me_ref[0] ^ ((count - n) % count)
+            s = me_ref[0] ^ turns(count)[n]
             for k in range(pairs):
                 start = pl.multiple_of(n * rows + cols_ref[b, k, s] * edge, edge)
                 a_ref[b * edge:(b + 1) * edge, pl.ds(start, edge)] = in_ref[b, s, k]
@@ -71,10 +75,16 @@
     return lax.dot_general(left, right, (((0,), (0,)), ((), ())), preferred_element_type=F32)
 
 
+def begin(a_ref, *args):
+    panels, sum_ref = args[:-1], args[-1]
+    rows = sum_ref.shape[0]
+    sum_ref[...] = dot(a_ref[:, :len(panels) * rows], jnp.concatenate([ref[...] for ref in panels], axis=0))
+
+
 def layer(count, doms, me_ref, want_ref, refs_ref, *args):
-    panels, others = args[:count], args[count:count + doms - 1]
+    last_ref, sum_ref, others = args[0], args[1], args[2:doms + 1]
     (a_ref, off_ref, weight_ref, bias_ref, cot_ref,
-     act_ref, keep_ref, give_ref, *rest) = args[count + doms - 1:]
+     act_ref, keep_ref, give_ref, *rest) = args[doms + 1:]
     outs, (grad_ref, term_ref, block_ref) = rest[:count], rest[count:]
     blocks, tiles, edge, _ = off_ref.shape
     rows, cap = blocks * edge, want_ref.shape[0]
@@ -82,7 +92,7 @@
         f = me_ref[1] ^ n
         for c in range(cap):
             block_ref[f * cap + c] = others[n - 1][pl.ds(pl.multiple_of(want_ref[c, f] * edge, edge), edge), :]
-    inner = dot(a_ref[...], jnp.concatenate([ref[...] for ref in panels], axis=0))
+    inner = sum_ref[...] + dot(a_ref[:, (count - 1) * rows:], last_ref[...])
     sums = []
     for b in range(blocks):
         left = jnp.concatenate([off_ref[b, k] for k in range(tiles)], axis=1)
@@ -160,19 +170,21 @@
     sure = requests[0, 0] >= 0
     scale = 1.0 / math.sqrt(rows * count * doms)
 
-    def exchange(outer, part):
+    def exchange(outer, part, one):
+        one = swapped(one, "rep", 1)
         coming = lax.all_to_all(outer, "dom", split_axis=0, concat_axis=0, tiled=True)
         for axis, k, size in (("dom", 2, 4), ("rep", 1, count)):
             while k < size:
                 part, k = joined(part, axis, k), 2 * k
-        return coming, call(functools.partial(join, scale), [shape((width, width), BF16)], (me, part, swapped(part, "dom", 1)), "svv", name="join")[0]
+        return coming, one, call(functools.partial(join, scale), [shape((width, width), BF16)], (me, part, swapped(part, "dom", 1)), "svv", name="join")[0]
 
     near = swapped(feats, "dom", 1)
     even = [feats] + [swapped(feats if k == 4 else after(feats, near), "dom", k) for k in range(2, doms, 2)]
     inside = (lax.axis_index("rep") == 1) | (lax.axis_index("rep") == 2)
     if count == 4:
         far = swapped(feats, "rep", 3)
-        panels = [feats, far, relayed(jnp.where(inside, far, feats), -1), swapped(feats, "rep", 1)]
+        two = relayed(jnp.where(inside, far, feats), -1)
+        panels = [feats, far, swapped(feats, "rep", 1), two]
     else:
         panels = [feats] + [swapped(feats, "rep", k) for k in range(count - 1, 0, -1)]
     a = call(
@@ -181,22 +193,23 @@
         scratch=[pltpu.VMEM(in_vals.shape, BF16), pltpu.SemaphoreType.DMA((blocks,))], name="arrange")[0]
     odd = [near] + [swapped(after(value, a), "dom", 1) for n, value in enumerate(even) if n]
     others = [value for pair in zip(even, odd) for value in pair][1:]
+    begun = call(begin, [shape((rows, width), F32)], (a, *panels[:-1]), "v" * count, name="begin")[0]
     activated, keep, give, *terms, grad_agg = call(
         functools.partial(layer, count, doms),
         [flat] + [shape((width // 2, width), BF16)] * 2 + [flat] * (count + 1),
-        (me, requests, off_ref, *panels, *others, a, off_vals, weight, bias.reshape(1, width), cotangent),
-        "sss" + "v" * (count + doms + 4),
+        (me, requests, off_ref, panels[-1], begun, *others, a, off_vals, weight, bias.reshape(1, width), cotangent),
+        "sss" + "v" * (doms + 6),
         scratch=[pltpu.VMEM((width, width), F32), pltpu.VMEM((slots, edge, width), BF16)],
         flops=10**9, name="layer")
     part = (keep.astype(F32) + swapped(give, "dom", 1).astype(F32)).astype(BF16)
     first = part
     part = joined(part, "dom", 4)
-    got = [terms[0]] + [swapped(after(terms[count - k], first if k == 1 else None), "rep", k) for k in range(count - 1, 0, -1)]
+    got = [terms[0]] + [swapped(after(terms[turns(count).index(k)], first if k == 2 else None), "rep", k) for k in range(count - 1, 1, -1)]
     outer = call(
         spread_outer, [shape((doms, cap * (edge + 16), width), BF16)], (requests, off_ref, off_vals, grad_agg), "ssvv",
         scratch=[pltpu.VMEM((slots, edge, width), F32)], flops=10**9, name="outer")[0]
-    coming, grad_weight = fenced(sure, exchange, outer, part)
-    grad_feats = call(functools.partial(finish, cap, edge), [flat], (coming, *got), "v" * (count + 1), name="finish")[0]
+    coming, one, grad_weight = fenced(sure, exchange, outer, part, terms[turns(count).index(1)])
+    grad_feats = call(functools.partial(finish, cap, edge), [flat], (coming, *got, one), "v" * (count + 1), name="finish")[0]
     return (activated, grad_feats, grad_weight)
 
 

time: 55.8 us -> 54.9 us (0.984)
  waiting for transfers between devices: 15.9 us -> 14.4 us
  starting transfers between devices: 27.1 us -> 27.8 us
    all_to_all x1, waiting for transfers between devices: 1.39 us -> 0.01 us  [exchange(): lax.all_to_all(outer, 'dom', split_axis=0, concat_axis=0, tiled=True)]
    ppermute x18, starting transfers between devices: 18.6 us -> 19.4 us  [swapped(): lax.ppermute(value, axis, [(i, i ^ k) for i in range(lax.axis_size(axis))])]
    pallas_call x5 -> x6, Pallas kernels: 9.57 us -> 9.44 us  [call(): pl.pallas_call(body, out_shape=outs, in_specs=[pl.BlockSpec(memory_space=...]
  transfers between devices with their start and end apart: 20 -> 20, of which waited for: 8 -> 7; matrix products, arithmetic and copies ran while one was open for 0% -> 0% of each run, Pallas kernels for 7% -> 7%
where the time goes in v6:
time: 54.9 us; the launch traced here: 54.6 us
  starting transfers between devices  27.8 us (51%)
  waiting for transfers between devices  14.4 us (26%)
  Pallas kernels  9.44 us (17%)
  local copies, waits for them, and re-layouts  1.86 us (3%)
  between operations  0.84 us (2%)
    ppermute x18, starting transfers between devices, swapped(): lax.ppermute(value, axis, [(i, i ^ k) for i in range(lax.axis_size(axis))])  19.4 us
    ppermute x18, waiting for transfers between devices, swapped(): lax.ppermute(value, axis, [(i, i ^ k) for i in range(lax.axis_size(axis))])  11.8 us
    pallas_call x6, Pallas kernels, call(): pl.pallas_call(body, out_shape=outs, in_specs=[pl.BlockSpec(memory_space=...  9.44 us
    ppermute x1, starting transfers between devices, relayed(): return lax.ppermute(value, 'rep', [pair[::turns] for pair in pairs])  4.25 us
    all_to_all x1, starting transfers between devices, exchange(): lax.all_to_all(outer, 'dom', split_axis=0, concat_axis=0, tiled=True)  4.19 us
    ppermute x1, waiting for transfers between devices, relayed(): return lax.ppermute(value, 'rep', [pair[::turns] for pair in pairs])  2.6 us
    unnamed x20, local copies, waits for them, and re-layouts  1.86 us
  transfers between devices with their start and end apart: 20, of which 7 were waited for; matrix products, arithmetic and copies ran while one was open for 0% of the time, Pallas kernels for 7%

profile of v6, /device:TPU:0, one launch (start us, length us, event | category | flops | bytes accessed | tf_op | source)
XLA Modules:
  0.0 54.6 jit_solution(11875084192471850513)
XLA Ops:
  0.6 0.5 collective-permute-start.7
  1.1 2.6 %collective-permute-start.8 = (bf16[384,256]{1,0:T(8,128)(2,1)}, bf16[384,256]{1,0:T(8,128)(2,1)S(1)}, u32[]{:S(2)}, u32[]{:S(2)}) collective-permute-start(bf16[384,256]{1,0:T(8,128)(2,1)} %args_0_.4), channel_id=1, source_target_pairs={{0,4},{1,5},{2,6},{3,7},{4,0},{5,1},{6,2},{7,3},{8,12},{9,13},{10,... | collective-permute-start | bytes 589832 | tf_op jit(solution)/shard_map/ppermute | solution.py:21
  3.7 3.6 %collective-permute-start.5 = (bf16[384,256]{1,0:T(8,128)(2,1)}, bf16[384,256]{1,0:T(8,128)(2,1)S(1)}, u32[]{:S(2)}, u32[]{:S(2)}) collective-permute-start(bf16[384,256]{1,0:T(8,128)(2,1)} %args_0_.4), channel_id=1, source_target_pairs={{0,24},{8,16},{16,8},{24,0},{1,25},{9,17},{17,9},{25,1},{2,26},{10... | collective-permute-start | bytes 589832 | tf_op jit(solution)/shard_map/ppermute | solution.py:21
  7.3 0.1 pad_add_fusion.me_ref
  7.4 1.5 %collective-permute-start.10 = (bf16[384,256]{1,0:T(8,128)(2,1)}, bf16[384,256]{1,0:T(8,128)(2,1)S(1)}, u32[]{:S(2)}, u32[]{:S(2)}) collective-permute-start(bf16[384,256]{1,0:T(8,128)(2,1)} %args_0_.4), channel_id=1, source_target_pairs={{0,2},{1,3},{2,0},{3,1},{4,6},{5,7},{6,4},{7,5},{8,10},{9,11},{10,... | collective-permute-start | bytes 589832 | tf_op jit(solution)/shard_map/ppermute | solution.py:21
  8.9 0.5 collective-permute-start.13
  9.4 1.1 %copy-done.1 = bf16[3,4,2,128,128]{4,3,2,1,0:T(8,128)(2,1)S(1)} copy-done((bf16[3,4,2,128,128]{4,3,2,1,0:T(8,128)(2,1)S(1)}, bf16[3,4,2,128,128]{4,3,2,1,0:T(8,128)(2,1)}, u32[]{:S(2)}) %copy-start.1) | copy-done | bytes 786456
  10.6 0.7 %copy-done.5 = s32[3,4,2]{1,2,0:T(2,128)S(1)} copy-done((s32[3,4,2]{1,2,0:T(2,128)S(1)}, s32[3,4,2]{1,2,0:T(2,128)}, u32[]{:S(2)}) %copy-start.5) | copy-done | bytes 120
  11.3 0.9 %arrange.1.a_ref.args_9_ = bf16[384,1536]{1,0:T(8,128)(2,1)S(1)} custom-call(s32[2]{0:T(128)S(1)} %pad_add_fusion.me_ref, s32[3,2,4]{2,1,0:T(2,128)S(1)} %bitcast.7, bf16[3,4,2,128,128]{4,3,2,1,0:T(8,128)(2,1)S(1)} %copy-done.1), custom_call_target="tpu_custom_call" | custom-call | bytes 1966184 | tf_op jit(solution)/shard_map/arrange/pallas_call | solution.py:42
  12.3 1.3 %collective-permute-done.5.args_1_ = bf16[384,256]{1,0:T(8,128)(2,1)S(1)} collective-permute-done((bf16[384,256]{1,0:T(8,128)(2,1)}, bf16[384,256]{1,0:T(8,128)(2,1)S(1)}, u32[]{:S(2)}, u32[]{:S(2)}) %collective-permute-start.5) | collective-permute-done | bytes 196640 | tf_op jit(solution)/shard_map/ppermute | solution.py:21
  13.6 4.3 %collective-permute-start.6 = (bf16[384,256]{1,0:T(8,128)(2,1)S(1)}, bf16[384,256]{1,0:T(8,128)(2,1)S(1)}, u32[]{:S(2)}, u32[]{:S(2)}) collective-permute-start(bf16[384,256]{1,0:T(8,128)(2,1)S(1)} %broadcast_select_fusion), channel_id=1, source_target_pairs={{8,0},{24,8},{16,24},{0,16},{9,1},{25,9},{17,25},{1,17},{10,2},{26... | collective-permute-start | bytes 589832 | tf_op jit(solution)/shard_map/ppermute | solution.py:26
  17.9 0.6 %collective-permute-done.13.args_7_ = bf16[384,256]{1,0:T(8,128)(2,1)S(1)} collective-permute-done((bf16[384,256]{1,0:T(8,128)(2,1)}, bf16[384,256]{1,0:T(8,128)(2,1)S(1)}, u32[]{:S(2)}, u32[]{:S(2)}) %collective-permute-start.13) | collective-permute-done | bytes 196640 | tf_op jit(solution)/shard_map/ppermute | solution.py:21
  18.5 0.4 begin.1.args_1_
  18.9 2.6 %collective-permute-done.6.args_0_ = bf16[384,256]{1,0:T(8,128)(2,1)S(1)} collective-permute-done((bf16[384,256]{1,0:T(8,128)(2,1)S(1)}, bf16[384,256]{1,0:T(8,128)(2,1)S(1)}, u32[]{:S(2)}, u32[]{:S(2)}) %collective-permute-start.6) | collective-permute-done | bytes 196640 | tf_op jit(solution)/shard_map/ppermute | solution.py:26
  21.6 3.1 %layer.1 = (bf16[384,256]{1,0:T(8,128)(2,1)}, bf16[128,256]{1,0:T(8,128)(2,1)S(1)}, bf16[128,256]{1,0:T(8,128)(2,1)S(1)}, bf16[384,256]{1,0:T(8,128)(2,1)S(1)}, ...) custom-call(s32[2]{0:T(128)S(1)} %pad_add_fusion.me_ref, ...), custom_call_target="tpu_custom_call" | custom-call | flops 1000000000 | bytes 5670036 | tf_op jit(solution)/shard_map/layer/pallas_call | solution.py:42
  24.8 2.3 %collective-permute-start.17 = (bf16[384,256]{1,0:T(8,128)(2,1)S(1)}, bf16[384,256]{1,0:T(8,128)(2,1)S(1)}, u32[]{:S(2)}, u32[]{:S(2)}) collective-permute-start(bf16[384,256]{1,0:T(8,128)(2,1)S(1)} %get-tuple-element.46), channel_id=1, source_target_pairs={{0,24},{8,16},{16,8},{24,0},{1,25},{9,17},{17,9},{25,1},{2,26},{10... | collective-permute-start | bytes 589832 | tf_op jit(solution)/shard_map/ppermute | solution.py:21
  27.1 1.4 %collective-permute-start.16 = (bf16[128,256]{1,0:T(8,128)(2,1)S(1)}, bf16[128,256]{1,0:T(8,128)(2,1)S(1)}, u32[]{:S(2)}, u32[]{:S(2)}) collective-permute-start(bf16[128,256]{1,0:T(8,128)(2,1)S(1)} %add_convert_fusion.4), channel_id=1, source_target_pairs={{0,4},{1,5},{2,6},{3,7},{4,0},{5,1},{6,2},{7,3},{8,12},{9,13},{10,... | collective-permute-start | bytes 196616 | tf_op jit(solution)/shard_map/ppermute | solution.py:21
  28.5 2.1 %outer.1 = bf16[8,144,256]{2,1,0:T(8,128)(2,1)} custom-call(s32[1,8]{1,0:T(1,128)S(1)} %bitcast.11, s32[3,9]{1,0:T(4,128)S(1)} %copy-done.6, bf16[3,9,128,128]{3,2,1,0:T(8,128)(2,1)S(1)} %copy-done, bf16[384,256]{1,0:T(8,128)(2,1)S(1)} %get-tuple-element.40.grad_ref), custom_call_target="tpu_custom_call" | custom-call | flops 1000000000 | bytes 1671308 | tf_op jit(solution)/shard_map/outer/pallas_call | solution.py:42
  30.6 1.5 %collective-permute-start.18 = (bf16[384,256]{1,0:T(8,128)(2,1)S(1)}, bf16[384,256]{1,0:T(8,128)(2,1)S(1)}, u32[]{:S(2)}, u32[]{:S(2)}) collective-permute-start(bf16[384,256]{1,0:T(8,128)(2,1)S(1)} %get-tuple-element.48), channel_id=1, source_target_pairs={{0,16},{8,24},{16,0},{24,8},{1,17},{9,25},{17,1},{25,9},{2,18},{10... | collective-permute-start | bytes 589832 | tf_op jit(solution)/shard_map/ppermute | solution.py:21
  32.1 20.2 %conditional.1 = (bf16[8,144,256]{2,1,0:T(8,128)(2,1)}, bf16[384,256]{1,0:T(8,128)(2,1)}, bf16[256,256]{1,0:T(8,128)(2,1)S(1)}) conditional(s32[]{:T(128)} %bitcast.5, () %tuple.29, (bf16[8,144,256]{2,1,0:T(8,128)(2,1)}, bf16[384,256]{1,0:T(8,128)(2,1)S(1)}, bf16[128,256]{1,0:T(8,128)(2,1)S(1)}, s32[2]{0:T(128)S(1)}) %tuple.30), branch_computations={%region_0.1_spmd, %region_1.2_spmd} | conditional | flops 393216 | bytes 4456712 | solution.py:35
  32.1 1.6 %collective-permute-start.1 = (bf16[128,256]{1,0:T(8,128)(2,1)S(1)}, bf16[128,256]{1,0:T(8,128)(2,1)S(1)}, u32[]{:S(2)}, u32[]{:S(2)}) collective-permute-start(bf16[128,256]{1,0:T(8,128)(2,1)S(1)} %get-tuple-element.11), channel_id=1, source_target_pairs={{0,2},{1,3},{2,0},{3,1},{4,6},{5,7},{6,4},{7,5},{8,10},{9,11},{10,... | collective-permute-start | bytes 196616 | tf_op jit(solution)/shard_map/cond/branch_1_fun/ppermute | solution.py:21
  33.7 2.8 %collective-permute-done.1 = bf16[128,256]{1,0:T(8,128)(2,1)S(1)} collective-permute-done((bf16[128,256]{1,0:T(8,128)(2,1)S(1)}, bf16[128,256]{1,0:T(8,128)(2,1)S(1)}, u32[]{:S(2)}, u32[]{:S(2)}) %collective-permute-start.1) | collective-permute-done | bytes 65568 | tf_op jit(solution)/shard_map/cond/branch_1_fun/ppermute | solution.py:21
  36.5 1.1 %collective-permute-start.2 = (bf16[128,256]{1,0:T(8,128)(2,1)S(1)}, bf16[128,256]{1,0:T(8,128)(2,1)S(1)}, u32[]{:S(2)}, u32[]{:S(2)}) collective-permute-start(bf16[128,256]{1,0:T(8,128)(2,1)S(1)} %add_convert_fusion.2), channel_id=1, source_target_pairs={{0,8},{8,0},{16,24},{24,16},{1,9},{9,1},{17,25},{25,17},{2,10},{10... | collective-permute-start | bytes 196616 | tf_op jit(solution)/shard_map/cond/branch_1_fun/ppermute | solution.py:21
  37.6 4.2 %all-to-all-start = ((bf16[8,144,256]{2,1,0:T(8,128)(2,1)}), bf16[8,144,256]{2,1,0:T(8,128)(2,1)}, u32[]{:S(2)}, u32[]{:S(2)}) async-start(bf16[8,144,256]{2,1,0:T(8,128)(2,1)} %get-tuple-element.8), calls=%async_computation | async-start | bytes 1179648 | tf_op jit(solution)/shard_map/cond/branch_1_fun/all_to_all | solution.py:175
  41.9 1.4 %collective-permute-start.3 = (bf16[128,256]{1,0:T(8,128)(2,1)S(1)}, bf16[128,256]{1,0:T(8,128)(2,1)S(1)}, u32[]{:S(2)}, u32[]{:S(2)}) collective-permute-start(bf16[128,256]{1,0:T(8,128)(2,1)S(1)} %add_convert_fusion.1), channel_id=1, source_target_pairs={{0,16},{8,24},{16,0},{24,8},{1,17},{9,25},{17,1},{25,9},{2,18},{10... | collective-permute-start | bytes 196616 | tf_op jit(solution)/shard_map/cond/branch_1_fun/ppermute | solution.py:21
  43.2 1.3 %collective-permute-start = (bf16[384,256]{1,0:T(8,128)(2,1)S(1)}, bf16[384,256]{1,0:T(8,128)(2,1)}, u32[]{:S(2)}, u32[]{:S(2)}) collective-permute-start(bf16[384,256]{1,0:T(8,128)(2,1)S(1)} %get-tuple-element.9), channel_id=1, source_target_pairs={{0,8},{8,0},{16,24},{24,16},{1,9},{9,1},{17,25},{25,17},{2,10},{10... | collective-permute-start | bytes 589832 | tf_op jit(solution)/shard_map/cond/branch_1_fun/ppermute | solution.py:21
  44.5 5.0 %collective-permute-done.3 = bf16[128,256]{1,0:T(8,128)(2,1)S(1)} collective-permute-done((bf16[128,256]{1,0:T(8,128)(2,1)S(1)}, bf16[128,256]{1,0:T(8,128)(2,1)S(1)}, u32[]{:S(2)}, u32[]{:S(2)}) %collective-permute-start.3) | collective-permute-done | bytes 65568 | tf_op jit(solution)/shard_map/cond/branch_1_fun/ppermute | solution.py:21
  49.5 0.1 collective-permute-start.4
  49.6 1.2 %collective-permute-done.4.other_ref = bf16[128,256]{1,0:T(8,128)(2,1)S(1)} collective-permute-done((bf16[128,256]{1,0:T(8,128)(2,1)S(1)}, bf16[128,256]{1,0:T(8,128)(2,1)S(1)}, u32[]{:S(2)}, u32[]{:S(2)}) %collective-permute-start.4) | collective-permute-done | bytes 65568 | tf_op jit(solution)/shard_map/cond/branch_1_fun/ppermute | solution.py:21
  50.9 0.6 %join.1 = bf16[256,256]{1,0:T(8,128)(2,1)S(1)} custom-call(s32[2]{0:T(128)S(1)} %get-tuple-element.10.me_ref, bf16[128,256]{1,0:T(8,128)(2,1)S(1)} %add_convert_fusion.part_ref, bf16[128,256]{1,0:T(8,128)(2,1)S(1)} %collective-permute-done.4.other_ref), custom_call_target="tpu_custom_call" | custom-call | bytes 262152 | tf_op jit(solution)/shard_map/cond/branch_1_fun/join/pallas_call | solution.py:42
  51.4 0.9 %collective-permute-done = bf16[384,256]{1,0:T(8,128)(2,1)} collective-permute-done((bf16[384,256]{1,0:T(8,128)(2,1)S(1)}, bf16[384,256]{1,0:T(8,128)(2,1)}, u32[]{:S(2)}, u32[]{:S(2)}) %collective-permute-start) | collective-permute-done | bytes 196640 | tf_op jit(solution)/shard_map/cond/branch_1_fun/ppermute | solution.py:21
  52.3 2.3 %finish.1 = bf16[384,256]{1,0:T(8,128)(2,1)} custom-call(bf16[8,144,256]{2,1,0:T(8,128)(2,1)} %get-tuple-element.44.coming_ref, bf16[384,256]{1,0:T(8,128)(2,1)S(1)} %get-tuple-element.45.args_0_, bf16[384,256]{1,0:T(8,128)(2,1)S(1)} %collective-permute-done.17.args_1_, bf16[384,256]{1,0:T(8,128)(2,1)S(1)} %collective-permute-done.18.args_2_, ...), custom_call_target="tpu_custom_call" | custom-call | bytes 1572864 | tf_op jit(solution)/shard_map/finish/pallas_call | solution.py:42
  (42 shorter events, 0.3 us)
Async XLA Ops:
  0.6 6.8 %collective-permute-start.7 = (bf16[384,256]{1,0:T(8,128)(2,1)}, bf16[384,256]{1,0:T(8,128)(2,1)S(1)}, u32[]{:S(2)}, u32[]{:S(2)}) collective-permute-start(bf16[384,256]{1,0:T(8,128)(2,1)} %args_0_.4), channel_id=1, source_target_pairs={{0,1},{1,0},{2,3},{3,2},{4,5},{5,4},{6,7},{7,6},{8,9},{9,8},{10,11... | collective-permute-start | bytes 589832 | tf_op jit(solution)/shard_map/ppermute | solution.py:21
  1.1 8.3 %collective-permute-start.8 = (bf16[384,256]{1,0:T(8,128)(2,1)}, bf16[384,256]{1,0:T(8,128)(2,1)S(1)}, u32[]{:S(2)}, u32[]{:S(2)}) collective-permute-start(bf16[384,256]{1,0:T(8,128)(2,1)} %args_0_.4), channel_id=1, source_target_pairs={{0,4},{1,5},{2,6},{3,7},{4,0},{5,1},{6,2},{7,3},{8,12},{9,13},{10,... | collective-permute-start | bytes 589832 | tf_op jit(solution)/shard_map/ppermute | solution.py:21
  3.7 9.8 %collective-permute-start.5 = (bf16[384,256]{1,0:T(8,128)(2,1)}, bf16[384,256]{1,0:T(8,128)(2,1)S(1)}, u32[]{:S(2)}, u32[]{:S(2)}) collective-permute-start(bf16[384,256]{1,0:T(8,128)(2,1)} %args_0_.4), channel_id=1, source_target_pairs={{0,24},{8,16},{16,8},{24,0},{1,25},{9,17},{17,9},{25,1},{2,26},{10... | collective-permute-start | bytes 589832 | tf_op jit(solution)/shard_map/ppermute | solution.py:21
  7.3 11.2 %collective-permute-start.9 = (bf16[384,256]{1,0:T(8,128)(2,1)}, bf16[384,256]{1,0:T(8,128)(2,1)S(1)}, u32[]{:S(2)}, u32[]{:S(2)}) collective-permute-start(bf16[384,256]{1,0:T(8,128)(2,1)} %args_0_.4), channel_id=1, source_target_pairs={{0,8},{8,0},{16,24},{24,16},{1,9},{9,1},{17,25},{25,17},{2,10},{10... | collective-permute-start | bytes 589832 | tf_op jit(solution)/shard_map/ppermute | solution.py:21
  7.4 10.5 %collective-permute-start.10 = (bf16[384,256]{1,0:T(8,128)(2,1)}, bf16[384,256]{1,0:T(8,128)(2,1)S(1)}, u32[]{:S(2)}, u32[]{:S(2)}) collective-permute-start(bf16[384,256]{1,0:T(8,128)(2,1)} %args_0_.4), channel_id=1, source_target_pairs={{0,2},{1,3},{2,0},{3,1},{4,6},{5,7},{6,4},{7,5},{8,10},{9,11},{10,... | collective-permute-start | bytes 589832 | tf_op jit(solution)/shard_map/ppermute | solution.py:21
  8.9 9.6 %collective-permute-start.13 = (bf16[384,256]{1,0:T(8,128)(2,1)}, bf16[384,256]{1,0:T(8,128)(2,1)S(1)}, u32[]{:S(2)}, u32[]{:S(2)}) collective-permute-start(bf16[384,256]{1,0:T(8,128)(2,1)} %args_0_.4), channel_id=1, source_target_pairs={{0,6},{1,7},{2,4},{3,5},{4,2},{5,3},{6,0},{7,1},{8,14},{9,15},{10,... | collective-permute-start | bytes 589832 | tf_op jit(solution)/shard_map/ppermute | solution.py:21
  9.4 1.1 %copy-start.1 = (bf16[3,4,2,128,128]{4,3,2,1,0:T(8,128)(2,1)S(1)}, bf16[3,4,2,128,128]{4,3,2,1,0:T(8,128)(2,1)}, u32[]{:S(2)}) copy-start(bf16[3,4,2,128,128]{4,3,2,1,0:T(8,128)(2,1)} %in_hbm.1) | copy-start | bytes 2359300
  10.6 0.7 %copy-start.5 = (s32[3,4,2]{1,2,0:T(2,128)S(1)}, s32[3,4,2]{1,2,0:T(2,128)}, u32[]{:S(2)}) copy-start(s32[3,4,2]{1,2,0:T(2,128)} %param.16) | copy-start | bytes 292
  11.3 2.3 %copy-start.2 = (bf16[384,256]{1,0:T(8,128)(2,1)S(1)}, bf16[384,256]{1,0:T(8,128)(2,1)}, u32[]{:S(2)}) copy-start(bf16[384,256]{1,0:T(8,128)(2,1)} %args_0_.4) | copy-start | bytes 589828
  12.2 6.7 %collective-permute-start.12 = (bf16[384,256]{1,0:T(8,128)(2,1)S(1)}, bf16[384,256]{1,0:T(8,128)(2,1)S(1)}, u32[]{:S(2)}, u32[]{:S(2)}) collective-permute-start(bf16[384,256]{1,0:T(8,128)(2,1)S(1)} %collective-permute-done.8.args_5_), channel_id=1, source_target_pairs={{0,1},{1,0},{2,3},{3,2},{4,5},{5,4},{6,7},{7,6},{8,9},{9,8},{10,11... | collective-permute-start | bytes 589832 | tf_op jit(solution)/shard_map/ppermute | solution.py:21
  13.6 8.0 %copy-start = (bf16[3,9,128,128]{3,2,1,0:T(8,128)(2,1)S(1)}, bf16[3,9,128,128]{3,2,1,0:T(8,128)(2,1)}, u32[]{:S(2)}) copy-start(bf16[3,9,128,128]{3,2,1,0:T(8,128)(2,1)} %off_ref.1) | copy-start | bytes 2654212
  13.6 8.0 %copy-start.3 = (bf16[384,256]{1,0:T(8,128)(2,1)S(1)}, bf16[384,256]{1,0:T(8,128)(2,1)}, u32[]{:S(2)}) copy-start(bf16[384,256]{1,0:T(8,128)(2,1)} %args_13_.1) | copy-start | bytes 589828
  13.6 8.0 %copy-start.4 = (bf16[256,256]{1,0:T(8,128)(2,1)S(1)}, bf16[256,256]{1,0:T(8,128)(2,1)}, u32[]{:S(2)}) copy-start(bf16[256,256]{1,0:T(8,128)(2,1)} %args_11_.1) | copy-start | bytes 393220
  13.6 8.0 %copy-start.6 = (s32[3,9]{1,0:T(4,128)S(1)}, s32[3,9]{1,0:T(4,128)}, u32[]{:S(2)}) copy-start(s32[3,9]{1,0:T(4,128)} %refs_ref.3) | copy-start | bytes 328
  13.6 8.0 %copy-start.7 = (f32[256]{0:T(256)S(1)}, f32[256]{0:T(256)}, u32[]{:S(2)}) copy-start(f32[256]{0:T(256)} %param.14) | copy-start | bytes 3076
  13.6 8.0 %copy-start.8 = (s32[1,1,8,1]{2,3,1,0:T(1,128)S(1)}, s32[1,1,8,1]{2,3,1,0:T(1,128)}, u32[]{:S(2)}) copy-start(s32[1,1,8,1]{2,3,1,0:T(1,128)} %param.19) | copy-start | bytes 100
  13.6 7.9 %collective-permute-start.6 = (bf16[384,256]{1,0:T(8,128)(2,1)S(1)}, bf16[384,256]{1,0:T(8,128)(2,1)S(1)}, u32[]{:S(2)}, u32[]{:S(2)}) collective-permute-start(bf16[384,256]{1,0:T(8,128)(2,1)S(1)} %broadcast_select_fusion), channel_id=1, source_target_pairs={{8,0},{24,8},{16,24},{0,16},{9,1},{25,9},{17,25},{1,17},{10,2},{26... | collective-permute-start | bytes 589832 | tf_op jit(solution)/shard_map/ppermute | solution.py:26
  17.9 3.7 %collective-permute-start.11 = (bf16[384,256]{1,0:T(8,128)(2,1)S(1)}, bf16[384,256]{1,0:T(8,128)(2,1)S(1)}, u32[]{:S(2)}, u32[]{:S(2)}) collective-permute-start(bf16[384,256]{1,0:T(8,128)(2,1)S(1)} %collective-permute-done.10.args_3_), channel_id=1, source_target_pairs={{0,1},{1,0},{2,3},{3,2},{4,5},{5,4},{6,7},{7,6},{8,9},{9,8},{10,11... | collective-permute-start | bytes 589832 | tf_op jit(solution)/shard_map/ppermute | solution.py:21
  18.5 3.1 %collective-permute-start.14 = (bf16[384,256]{1,0:T(8,128)(2,1)S(1)}, bf16[384,256]{1,0:T(8,128)(2,1)S(1)}, u32[]{:S(2)}, u32[]{:S(2)}) collective-permute-start(bf16[384,256]{1,0:T(8,128)(2,1)S(1)} %collective-permute-done.13.args_7_), channel_id=1, source_target_pairs={{0,1},{1,0},{2,3},{3,2},{4,5},{5,4},{6,7},{7,6},{8,9},{9,8},{10,11... | collective-permute-start | bytes 589832 | tf_op jit(solution)/shard_map/ppermute | solution.py:21
  24.7 2.3 %collective-permute-start.15 = (bf16[128,256]{1,0:T(8,128)(2,1)S(1)}, bf16[128,256]{1,0:T(8,128)(2,1)S(1)}, u32[]{:S(2)}, u32[]{:S(2)}) collective-permute-start(bf16[128,256]{1,0:T(8,128)(2,1)S(1)} %get-tuple-element.43), channel_id=1, source_target_pairs={{0,1},{1,0},{2,3},{3,2},{4,5},{5,4},{6,7},{7,6},{8,9},{9,8},{10,11... | collective-permute-start | bytes 196616 | tf_op jit(solution)/shard_map/ppermute | solution.py:21
  24.8 27.5 %collective-permute-start.17 = (bf16[384,256]{1,0:T(8,128)(2,1)S(1)}, bf16[384,256]{1,0:T(8,128)(2,1)S(1)}, u32[]{:S(2)}, u32[]{:S(2)}) collective-permute-start(bf16[384,256]{1,0:T(8,128)(2,1)S(1)} %get-tuple-element.46), channel_id=1, source_target_pairs={{0,24},{8,16},{16,8},{24,0},{1,25},{9,17},{17,9},{25,1},{2,26},{10... | collective-permute-start | bytes 589832 | tf_op jit(solution)/shard_map/ppermute | solution.py:21
  27.1 5.0 %collective-permute-start.16 = (bf16[128,256]{1,0:T(8,128)(2,1)S(1)}, bf16[128,256]{1,0:T(8,128)(2,1)S(1)}, u32[]{:S(2)}, u32[]{:S(2)}) collective-permute-start(bf16[128,256]{1,0:T(8,128)(2,1)S(1)} %add_convert_fusion.4), channel_id=1, source_target_pairs={{0,4},{1,5},{2,6},{3,7},{4,0},{5,1},{6,2},{7,3},{8,12},{9,13},{10,... | collective-permute-start | bytes 196616 | tf_op jit(solution)/shard_map/ppermute | solution.py:21
  30.6 21.7 %collective-permute-start.18 = (bf16[384,256]{1,0:T(8,128)(2,1)S(1)}, bf16[384,256]{1,0:T(8,128)(2,1)S(1)}, u32[]{:S(2)}, u32[]{:S(2)}) collective-permute-start(bf16[384,256]{1,0:T(8,128)(2,1)S(1)} %get-tuple-element.48), channel_id=1, source_target_pairs={{0,16},{8,24},{16,0},{24,8},{1,17},{9,25},{17,1},{25,9},{2,18},{10... | collective-permute-start | bytes 589832 | tf_op jit(solution)/shard_map/ppermute | solution.py:21
  32.1 4.3 %collective-permute-start.1 = (bf16[128,256]{1,0:T(8,128)(2,1)S(1)}, bf16[128,256]{1,0:T(8,128)(2,1)S(1)}, u32[]{:S(2)}, u32[]{:S(2)}) collective-permute-start(bf16[128,256]{1,0:T(8,128)(2,1)S(1)} %get-tuple-element.11), channel_id=1, source_target_pairs={{0,2},{1,3},{2,0},{3,1},{4,6},{5,7},{6,4},{7,5},{8,10},{9,11},{10,... | collective-permute-start | bytes 196616 | tf_op jit(solution)/shard_map/cond/branch_1_fun/ppermute | solution.py:21
  36.5 5.3 %collective-permute-start.2 = (bf16[128,256]{1,0:T(8,128)(2,1)S(1)}, bf16[128,256]{1,0:T(8,128)(2,1)S(1)}, u32[]{:S(2)}, u32[]{:S(2)}) collective-permute-start(bf16[128,256]{1,0:T(8,128)(2,1)S(1)} %add_convert_fusion.2), channel_id=1, source_target_pairs={{0,8},{8,0},{16,24},{24,16},{1,9},{9,1},{17,25},{25,17},{2,10},{10... | collective-permute-start | bytes 196616 | tf_op jit(solution)/shard_map/cond/branch_1_fun/ppermute | solution.py:21
  37.6 14.7 %all-to-all-start = ((bf16[8,144,256]{2,1,0:T(8,128)(2,1)}), bf16[8,144,256]{2,1,0:T(8,128)(2,1)}, u32[]{:S(2)}, u32[]{:S(2)}) async-start(bf16[8,144,256]{2,1,0:T(8,128)(2,1)} %get-tuple-element.8), calls=%async_computation | async-start | bytes 1179648 | tf_op jit(solution)/shard_map/cond/branch_1_fun/all_to_all | solution.py:175
  41.9 7.7 %collective-permute-start.3 = (bf16[128,256]{1,0:T(8,128)(2,1)S(1)}, bf16[128,256]{1,0:T(8,128)(2,1)S(1)}, u32[]{:S(2)}, u32[]{:S(2)}) collective-permute-start(bf16[128,256]{1,0:T(8,128)(2,1)S(1)} %add_convert_fusion.1), channel_id=1, source_target_pairs={{0,16},{8,24},{16,0},{24,8},{1,17},{9,25},{17,1},{25,9},{2,18},{10... | collective-permute-start | bytes 196616 | tf_op jit(solution)/shard_map/cond/branch_1_fun/ppermute | solution.py:21
  43.2 9.1 %collective-permute-start = (bf16[384,256]{1,0:T(8,128)(2,1)S(1)}, bf16[384,256]{1,0:T(8,128)(2,1)}, u32[]{:S(2)}, u32[]{:S(2)}) collective-permute-start(bf16[384,256]{1,0:T(8,128)(2,1)S(1)} %get-tuple-element.9), channel_id=1, source_target_pairs={{0,8},{8,0},{16,24},{24,16},{1,9},{9,1},{17,25},{25,17},{2,10},{10... | collective-permute-start | bytes 589832 | tf_op jit(solution)/shard_map/cond/branch_1_fun/ppermute | solution.py:21
  49.5 1.3 %collective-permute-start.4 = (bf16[128,256]{1,0:T(8,128)(2,1)S(1)}, bf16[128,256]{1,0:T(8,128)(2,1)S(1)}, u32[]{:S(2)}, u32[]{:S(2)}) collective-permute-start(bf16[128,256]{1,0:T(8,128)(2,1)S(1)} %add_convert_fusion.part_ref), channel_id=1, source_target_pairs={{0,1},{1,0},{2,3},{3,2},{4,5},{5,4},{6,7},{7,6},{8,9},{9,8},{10,11... | collective-permute-start | bytes 196616 | tf_op jit(solution)/shard_map/cond/branch_1_fun/ppermute | solution.py:21
  52.3 2.3 %copy-start.9 = (bf16[256,256]{1,0:T(8,128)(2,1)}, bf16[256,256]{1,0:T(8,128)(2,1)S(1)}, u32[]{:S(2)}) copy-start(bf16[256,256]{1,0:T(8,128)(2,1)S(1)} %get-tuple-element.32) | copy-start | bytes 393220

commit v7 on v6

--- a/solution.py
+++ b/solution.py
@@ -85,7 +85,7 @@
     last_ref, sum_ref, others = args[0], args[1], args[2:doms + 1]
     (a_ref, off_ref, weight_ref, bias_ref, cot_ref,
      act_ref, keep_ref, give_ref, *rest) = args[doms + 1:]
-    outs, (grad_ref, term_ref, block_ref) = rest[:count], rest[count:]
+    outs, (grad_ref, term_ref, block_ref) = rest[:-3], rest[-3:]
     blocks, tiles, edge, _ = off_ref.shape
     rows, cap = blocks * edge, want_ref.shape[0]
     for n in range(1, doms):
@@ -107,18 +107,22 @@
     grad_agg = lax.dot_general(
         grad_pre, weight_ref[...], (((1,), (1,)), ((), ())), preferred_element_type=F32).astype(BF16)
     grad_ref[...] = grad_agg
-    for n in range(count):
-        outs[n][...] = dot_t(a_ref[:, n * rows:(n + 1) * rows], grad_agg).astype(BF16)
+    for out, n in zip(outs, [n for n, k in enumerate(turns(count)) if k > 2]):
+        out[...] = dot_t(a_ref[:, n * rows:(n + 1) * rows], grad_agg).astype(BF16)
     term_ref[...] = dot_t(agg, grad_pre)
     half, core = keep_ref.shape[0], me_ref[1] & 1
     keep_ref[...] = term_ref[pl.ds(pl.multiple_of(core * half, half), half), :].astype(BF16)
     give_ref[...] = term_ref[pl.ds(pl.multiple_of((1 - core) * half, half), half), :].astype(BF16)
 
 
-def spread_outer(want_ref, refs_ref, off_ref, grad_ref, out_ref, total_ref):
+def spread_rest(want_ref, refs_ref, a_ref, off_ref, grad_ref, own_ref, near_ref, next_ref, out_ref, total_ref):
     blocks, tiles, edge, _ = off_ref.shape
     cap, doms = want_ref.shape
     grad_agg = grad_ref[...]
+    rows = grad_agg.shape[0]
+    order = turns(a_ref.shape[1] // rows)
+    for ref, n in ((own_ref, order.index(0)), (near_ref, order.index(1)), (next_ref, order.index(2))):
+        ref[...] = dot_t(a_ref[:, n * rows:(n + 1) * rows], grad_agg).astype(BF16)
     total_ref[...] = jnp.zeros_like(total_ref)
     for b in range(blocks):
         grad_b = grad_agg[b * edge:(b + 1) * edge]
@@ -170,12 +174,14 @@
     sure = requests[0, 0] >= 0
     scale = 1.0 / math.sqrt(rows * count * doms)
 
+    dom_steps = [k for k in (4, 2) if k < doms] + [1 << n for n in range(3, doms.bit_length() - 1)]
+
     def exchange(outer, part, one):
         one = swapped(one, "rep", 1)
         coming = lax.all_to_all(outer, "dom", split_axis=0, concat_axis=0, tiled=True)
-        for axis, k, size in (("dom", 2, 4), ("rep", 1, count)):
-            while k < size:
-                part, k = joined(part, axis, k), 2 * k
+        for axis, steps in (("dom", dom_steps[1:]), ("rep", [1 << n for n in range(count.bit_length() - 1)])):
+            for k in steps:
+                part = joined(part, axis, k)
         return coming, one, call(functools.partial(join, scale), [shape((width, width), BF16)], (me, part, swapped(part, "dom", 1)), "svv", name="join")[0]
 
     near = swapped(feats, "dom", 1)
@@ -196,20 +202,21 @@
     begun = call(begin, [shape((rows, width), F32)], (a, *panels[:-1]), "v" * count, name="begin")[0]
     activated, keep, give, *terms, grad_agg = call(
         functools.partial(layer, count, doms),
-        [flat] + [shape((width // 2, width), BF16)] * 2 + [flat] * (count + 1),
+        [flat] + [shape((width // 2, width), BF16)] * 2 + [flat] * (count - 2),
         (me, requests, off_ref, panels[-1], begun, *others, a, off_vals, weight, bias.reshape(1, width), cotangent),
         "sss" + "v" * (doms + 6),
         scratch=[pltpu.VMEM((width, width), F32), pltpu.VMEM((slots, edge, width), BF16)],
         flops=10**9, name="layer")
     part = (keep.astype(F32) + swapped(give, "dom", 1).astype(F32)).astype(BF16)
     first = part
-    part = joined(part, "dom", 4)
-    got = [terms[0]] + [swapped(after(terms[turns(count).index(k)], first if k == 2 else None), "rep", k) for k in range(count - 1, 1, -1)]
-    outer = call(
-        spread_outer, [shape((doms, cap * (edge + 16), width), BF16)], (requests, off_ref, off_vals, grad_agg), "ssvv",
-        scratch=[pltpu.VMEM((slots, edge, width), F32)], flops=10**9, name="outer")[0]
-    coming, one, grad_weight = fenced(sure, exchange, outer, part, terms[turns(count).index(1)])
-    grad_feats = call(functools.partial(finish, cap, edge), [flat], (coming, *got, one), "v" * (count + 1), name="finish")[0]
+    part = joined(part, "dom", dom_steps[0])
+    own, near_terms, next_terms, outer = call(
+        spread_rest, [flat, flat, flat, shape((doms, cap * (edge + 16), width), BF16)], (requests, off_ref, a, off_vals, grad_agg), "ssvvv",
+        scratch=[pltpu.VMEM((slots, edge, width), F32)], flops=10**9, name="rest")
+    terms = dict(zip([k for k in turns(count) if k > 2], terms)) | {2: next_terms}
+    got = [swapped(after(terms[k], first if k == 2 else None), "rep", k) for k in range(count - 1, 1, -1)]
+    coming, one, grad_weight = fenced(sure, exchange, outer, part, near_terms)
+    grad_feats = call(functools.partial(finish, cap, edge), [flat], (coming, own, *got, one), "v" * (count + 1), name="finish")[0]
     return (activated, grad_feats, grad_weight)
 
 

time: 54.9 us -> 54.4 us (level)
  transfers between devices with their start and end apart: 20 -> 20, of which waited for: 7 -> 7; matrix products, arithmetic and copies ran while one was open for 0% -> 0% of each run, Pallas kernels for 7% -> 8%
where the time goes in v7:
time: 54.4 us; the launch traced here: 54.1 us
  starting transfers between devices  27.6 us (51%)
  waiting for transfers between devices  14.2 us (26%)
  Pallas kernels  9.29 us (17%)
  local copies, waits for them, and re-layouts  1.86 us (3%)
  between operations  0.84 us (2%)
    ppermute x18, starting transfers between devices, swapped(): lax.ppermute(value, axis, [(i, i ^ k) for i in range(lax.axis_size(axis))])  19.2 us
    ppermute x18, waiting for transfers between devices, swapped(): lax.ppermute(value, axis, [(i, i ^ k) for i in range(lax.axis_size(axis))])  11.6 us
    pallas_call x6, Pallas kernels, call(): pl.pallas_call(body, out_shape=outs, in_specs=[pl.BlockSpec(memory_space=...  9.29 us
    ppermute x1, starting transfers between devices, relayed(): return lax.ppermute(value, 'rep', [pair[::turns] for pair in pairs])  4.25 us
    all_to_all x1, starting transfers between devices, exchange(): lax.all_to_all(outer, 'dom', split_axis=0, concat_axis=0, tiled=True)  4.19 us
    ppermute x1, waiting for transfers between devices, relayed(): return lax.ppermute(value, 'rep', [pair[::turns] for pair in pairs])  2.6 us
    unnamed x20, local copies, waits for them, and re-layouts  1.86 us
  transfers between devices with their start and end apart: 20, of which 7 were waited for; matrix products, arithmetic and copies ran while one was open for 0% of the time, Pallas kernels for 8%

profile of v7, /device:TPU:0, one launch (start us, length us, event | category | flops | bytes accessed | tf_op | source)
XLA Modules:
  0.0 54.1 jit_solution(16760408121244830200)
XLA Ops:
  0.6 0.5 collective-permute-start.7
  1.1 2.6 %collective-permute-start.8 = (bf16[384,256]{1,0:T(8,128)(2,1)}, bf16[384,256]{1,0:T(8,128)(2,1)S(1)}, u32[]{:S(2)}, u32[]{:S(2)}) collective-permute-start(bf16[384,256]{1,0:T(8,128)(2,1)} %args_0_.4), channel_id=1, source_target_pairs={{0,4},{1,5},{2,6},{3,7},{4,0},{5,1},{6,2},{7,3},{8,12},{9,13},{10,... | collective-permute-start | bytes 589832 | tf_op jit(solution)/shard_map/ppermute | solution.py:21
  3.7 3.6 %collective-permute-start.5 = (bf16[384,256]{1,0:T(8,128)(2,1)}, bf16[384,256]{1,0:T(8,128)(2,1)S(1)}, u32[]{:S(2)}, u32[]{:S(2)}) collective-permute-start(bf16[384,256]{1,0:T(8,128)(2,1)} %args_0_.4), channel_id=1, source_target_pairs={{0,24},{8,16},{16,8},{24,0},{1,25},{9,17},{17,9},{25,1},{2,26},{10... | collective-permute-start | bytes 589832 | tf_op jit(solution)/shard_map/ppermute | solution.py:21
  7.3 0.1 pad_add_fusion.me_ref
  7.4 1.5 %collective-permute-start.10 = (bf16[384,256]{1,0:T(8,128)(2,1)}, bf16[384,256]{1,0:T(8,128)(2,1)S(1)}, u32[]{:S(2)}, u32[]{:S(2)}) collective-permute-start(bf16[384,256]{1,0:T(8,128)(2,1)} %args_0_.4), channel_id=1, source_target_pairs={{0,2},{1,3},{2,0},{3,1},{4,6},{5,7},{6,4},{7,5},{8,10},{9,11},{10,... | collective-permute-start | bytes 589832 | tf_op jit(solution)/shard_map/ppermute | solution.py:21
  8.9 0.5 collective-permute-start.13
  9.4 1.1 %copy-done.1 = bf16[3,4,2,128,128]{4,3,2,1,0:T(8,128)(2,1)S(1)} copy-done((bf16[3,4,2,128,128]{4,3,2,1,0:T(8,128)(2,1)S(1)}, bf16[3,4,2,128,128]{4,3,2,1,0:T(8,128)(2,1)}, u32[]{:S(2)}) %copy-start.1) | copy-done | bytes 786456
  10.6 0.7 %copy-done.5 = s32[3,4,2]{1,2,0:T(2,128)S(1)} copy-done((s32[3,4,2]{1,2,0:T(2,128)S(1)}, s32[3,4,2]{1,2,0:T(2,128)}, u32[]{:S(2)}) %copy-start.5) | copy-done | bytes 120
  11.3 0.9 %arrange.1.a_ref.args_9_ = bf16[384,1536]{1,0:T(8,128)(2,1)S(1)} custom-call(s32[2]{0:T(128)S(1)} %pad_add_fusion.me_ref, s32[3,2,4]{2,1,0:T(2,128)S(1)} %bitcast.7, bf16[3,4,2,128,128]{4,3,2,1,0:T(8,128)(2,1)S(1)} %copy-done.1), custom_call_target="tpu_custom_call" | custom-call | bytes 1966184 | tf_op jit(solution)/shard_map/arrange/pallas_call | solution.py:42
  12.2 0.1 collective-permute-start.12
  12.3 1.3 %collective-permute-done.5.args_1_ = bf16[384,256]{1,0:T(8,128)(2,1)S(1)} collective-permute-done((bf16[384,256]{1,0:T(8,128)(2,1)}, bf16[384,256]{1,0:T(8,128)(2,1)S(1)}, u32[]{:S(2)}, u32[]{:S(2)}) %collective-permute-start.5) | collective-permute-done | bytes 196640 | tf_op jit(solution)/shard_map/ppermute | solution.py:21
  13.6 4.3 %collective-permute-start.6 = (bf16[384,256]{1,0:T(8,128)(2,1)S(1)}, bf16[384,256]{1,0:T(8,128)(2,1)S(1)}, u32[]{:S(2)}, u32[]{:S(2)}) collective-permute-start(bf16[384,256]{1,0:T(8,128)(2,1)S(1)} %broadcast_select_fusion), channel_id=1, source_target_pairs={{8,0},{24,8},{16,24},{0,16},{9,1},{25,9},{17,25},{1,17},{10,2},{26... | collective-permute-start | bytes 589832 | tf_op jit(solution)/shard_map/ppermute | solution.py:26
  17.9 0.6 %collective-permute-done.13.args_7_ = bf16[384,256]{1,0:T(8,128)(2,1)S(1)} collective-permute-done((bf16[384,256]{1,0:T(8,128)(2,1)}, bf16[384,256]{1,0:T(8,128)(2,1)S(1)}, u32[]{:S(2)}, u32[]{:S(2)}) %collective-permute-start.13) | collective-permute-done | bytes 196640 | tf_op jit(solution)/shard_map/ppermute | solution.py:21
  18.5 0.4 begin.1.args_1_
  18.9 2.6 %collective-permute-done.6.args_0_ = bf16[384,256]{1,0:T(8,128)(2,1)S(1)} collective-permute-done((bf16[384,256]{1,0:T(8,128)(2,1)S(1)}, bf16[384,256]{1,0:T(8,128)(2,1)S(1)}, u32[]{:S(2)}, u32[]{:S(2)}) %collective-permute-start.6) | collective-permute-done | bytes 196640 | tf_op jit(solution)/shard_map/ppermute | solution.py:26
  21.6 2.6 %layer.1 = (bf16[384,256]{1,0:T(8,128)(2,1)}, bf16[128,256]{1,0:T(8,128)(2,1)S(1)}, bf16[128,256]{1,0:T(8,128)(2,1)S(1)}, bf16[384,256]{1,0:T(8,128)(2,1)S(1)}, bf16[384,256]{1,0:T(8,128)(2,1)S(1)}) custom-call(s32[2]{0:T(128)S(1)} %pad_add_fusion.me_ref, s32[1,8]{1,0:T(1,128)S(1)} %bitcast.9, s32[3,9]{1,0:T(4,128)S(1)} %copy-done.6, ...), custom_call_target="tpu_custom_call" | custom-call | flops 1000000000 | bytes 5080212 | tf_op jit(solution)/shard_map/layer/pallas_call | solution.py:42
  24.3 2.3 %collective-permute-start.17 = (bf16[384,256]{1,0:T(8,128)(2,1)S(1)}, bf16[384,256]{1,0:T(8,128)(2,1)S(1)}, u32[]{:S(2)}, u32[]{:S(2)}) collective-permute-start(bf16[384,256]{1,0:T(8,128)(2,1)S(1)} %get-tuple-element.48), channel_id=1, source_target_pairs={{0,24},{8,16},{16,8},{24,0},{1,25},{9,17},{17,9},{25,1},{2,26},{10... | collective-permute-start | bytes 589832 | tf_op jit(solution)/shard_map/ppermute | solution.py:21
  26.6 1.4 %collective-permute-start.16 = (bf16[128,256]{1,0:T(8,128)(2,1)S(1)}, bf16[128,256]{1,0:T(8,128)(2,1)S(1)}, u32[]{:S(2)}, u32[]{:S(2)}) collective-permute-start(bf16[128,256]{1,0:T(8,128)(2,1)S(1)} %add_convert_fusion.4), channel_id=1, source_target_pairs={{0,4},{1,5},{2,6},{3,7},{4,0},{5,1},{6,2},{7,3},{8,12},{9,13},{10,... | collective-permute-start | bytes 196616 | tf_op jit(solution)/shard_map/ppermute | solution.py:21
  28.0 2.5 %rest.1 = (bf16[384,256]{1,0:T(8,128)(2,1)S(1)}, bf16[384,256]{1,0:T(8,128)(2,1)S(1)}, bf16[384,256]{1,0:T(8,128)(2,1)S(1)}, bf16[8,144,256]{2,1,0:T(8,128)(2,1)}) custom-call(s32[1,8]{1,0:T(1,128)S(1)} %bitcast.11, s32[3,9]{1,0:T(4,128)S(1)} %copy-done.6, bf16[384,1536]{1,0:T(8,128)(2,1)S(1)} %arrange.1.a_ref.args_9_, bf16[3,9,128,128]{3,2,1,0:T(8,128)(2,1)S(1)} %copy-done, ...), custom_call_target="tpu_custom_call" | custom-call | flops 1000000000 | bytes 3440780 | tf_op jit(solution)/shard_map/rest/pallas_call | solution.py:42
  30.5 1.5 %collective-permute-start.18 = (bf16[384,256]{1,0:T(8,128)(2,1)S(1)}, bf16[384,256]{1,0:T(8,128)(2,1)S(1)}, u32[]{:S(2)}, u32[]{:S(2)}) collective-permute-start(bf16[384,256]{1,0:T(8,128)(2,1)S(1)} %get-tuple-element.50), channel_id=1, source_target_pairs={{0,16},{8,24},{16,0},{24,8},{1,17},{9,25},{17,1},{25,9},{2,18},{10... | collective-permute-start | bytes 589832 | tf_op jit(solution)/shard_map/ppermute | solution.py:21
  32.0 19.8 %conditional.1 = (bf16[8,144,256]{2,1,0:T(8,128)(2,1)}, bf16[384,256]{1,0:T(8,128)(2,1)}, bf16[256,256]{1,0:T(8,128)(2,1)S(1)}) conditional(s32[]{:T(128)} %bitcast.5, () %tuple.29, (bf16[8,144,256]{2,1,0:T(8,128)(2,1)}, bf16[384,256]{1,0:T(8,128)(2,1)S(1)}, bf16[128,256]{1,0:T(8,128)(2,1)S(1)}, s32[2]{0:T(128)S(1)}) %tuple.30), branch_computations={%region_0.1_spmd, %region_1.2_spmd} | conditional | flops 393216 | bytes 4456712 | solution.py:35
  32.0 1.6 %collective-permute-start.1 = (bf16[128,256]{1,0:T(8,128)(2,1)S(1)}, bf16[128,256]{1,0:T(8,128)(2,1)S(1)}, u32[]{:S(2)}, u32[]{:S(2)}) collective-permute-start(bf16[128,256]{1,0:T(8,128)(2,1)S(1)} %get-tuple-element.11), channel_id=1, source_target_pairs={{0,2},{1,3},{2,0},{3,1},{4,6},{5,7},{6,4},{7,5},{8,10},{9,11},{10,... | collective-permute-start | bytes 196616 | tf_op jit(solution)/shard_map/cond/branch_1_fun/ppermute | solution.py:21
  33.6 2.8 %collective-permute-done.1 = bf16[128,256]{1,0:T(8,128)(2,1)S(1)} collective-permute-done((bf16[128,256]{1,0:T(8,128)(2,1)S(1)}, bf16[128,256]{1,0:T(8,128)(2,1)S(1)}, u32[]{:S(2)}, u32[]{:S(2)}) %collective-permute-start.1) | collective-permute-done | bytes 65568 | tf_op jit(solution)/shard_map/cond/branch_1_fun/ppermute | solution.py:21
  36.3 0.8 %collective-permute-start.2 = (bf16[128,256]{1,0:T(8,128)(2,1)S(1)}, bf16[128,256]{1,0:T(8,128)(2,1)S(1)}, u32[]{:S(2)}, u32[]{:S(2)}) collective-permute-start(bf16[128,256]{1,0:T(8,128)(2,1)S(1)} %add_convert_fusion.2), channel_id=1, source_target_pairs={{0,8},{8,0},{16,24},{24,16},{1,9},{9,1},{17,25},{25,17},{2,10},{10... | collective-permute-start | bytes 196616 | tf_op jit(solution)/shard_map/cond/branch_1_fun/ppermute | solution.py:21
  37.1 4.2 %all-to-all-start = ((bf16[8,144,256]{2,1,0:T(8,128)(2,1)}), bf16[8,144,256]{2,1,0:T(8,128)(2,1)}, u32[]{:S(2)}, u32[]{:S(2)}) async-start(bf16[8,144,256]{2,1,0:T(8,128)(2,1)} %get-tuple-element.8), calls=%async_computation | async-start | bytes 1179648 | tf_op jit(solution)/shard_map/cond/branch_1_fun/all_to_all | solution.py:181
  41.3 1.7 %collective-permute-start.3 = (bf16[128,256]{1,0:T(8,128)(2,1)S(1)}, bf16[128,256]{1,0:T(8,128)(2,1)S(1)}, u32[]{:S(2)}, u32[]{:S(2)}) collective-permute-start(bf16[128,256]{1,0:T(8,128)(2,1)S(1)} %add_convert_fusion.1), channel_id=1, source_target_pairs={{0,16},{8,24},{16,0},{24,8},{1,17},{9,25},{17,1},{25,9},{2,18},{10... | collective-permute-start | bytes 196616 | tf_op jit(solution)/shard_map/cond/branch_1_fun/ppermute | solution.py:21
  43.1 1.1 %collective-permute-start = (bf16[384,256]{1,0:T(8,128)(2,1)S(1)}, bf16[384,256]{1,0:T(8,128)(2,1)}, u32[]{:S(2)}, u32[]{:S(2)}) collective-permute-start(bf16[384,256]{1,0:T(8,128)(2,1)S(1)} %get-tuple-element.9), channel_id=1, source_target_pairs={{0,8},{8,0},{16,24},{24,16},{1,9},{9,1},{17,25},{25,17},{2,10},{10... | collective-permute-start | bytes 589832 | tf_op jit(solution)/shard_map/cond/branch_1_fun/ppermute | solution.py:21
  44.2 4.8 %collective-permute-done.3 = bf16[128,256]{1,0:T(8,128)(2,1)S(1)} collective-permute-done((bf16[128,256]{1,0:T(8,128)(2,1)S(1)}, bf16[128,256]{1,0:T(8,128)(2,1)S(1)}, u32[]{:S(2)}, u32[]{:S(2)}) %collective-permute-start.3) | collective-permute-done | bytes 65568 | tf_op jit(solution)/shard_map/cond/branch_1_fun/ppermute | solution.py:21
  49.1 1.2 %collective-permute-done.4.other_ref = bf16[128,256]{1,0:T(8,128)(2,1)S(1)} collective-permute-done((bf16[128,256]{1,0:T(8,128)(2,1)S(1)}, bf16[128,256]{1,0:T(8,128)(2,1)S(1)}, u32[]{:S(2)}, u32[]{:S(2)}) %collective-permute-start.4) | collective-permute-done | bytes 65568 | tf_op jit(solution)/shard_map/cond/branch_1_fun/ppermute | solution.py:21
  50.3 0.6 %join.1 = bf16[256,256]{1,0:T(8,128)(2,1)S(1)} custom-call(s32[2]{0:T(128)S(1)} %get-tuple-element.10.me_ref, bf16[128,256]{1,0:T(8,128)(2,1)S(1)} %add_convert_fusion.part_ref, bf16[128,256]{1,0:T(8,128)(2,1)S(1)} %collective-permute-done.4.other_ref), custom_call_target="tpu_custom_call" | custom-call | bytes 262152 | tf_op jit(solution)/shard_map/cond/branch_1_fun/join/pallas_call | solution.py:42
  50.9 0.9 %collective-permute-done = bf16[384,256]{1,0:T(8,128)(2,1)} collective-permute-done((bf16[384,256]{1,0:T(8,128)(2,1)S(1)}, bf16[384,256]{1,0:T(8,128)(2,1)}, u32[]{:S(2)}, u32[]{:S(2)}) %collective-permute-start) | collective-permute-done | bytes 196640 | tf_op jit(solution)/shard_map/cond/branch_1_fun/ppermute | solution.py:21
  51.8 2.3 %finish.1 = bf16[384,256]{1,0:T(8,128)(2,1)} custom-call(bf16[8,144,256]{2,1,0:T(8,128)(2,1)} %get-tuple-element.46.coming_ref, bf16[384,256]{1,0:T(8,128)(2,1)S(1)} %get-tuple-element.47.args_0_, bf16[384,256]{1,0:T(8,128)(2,1)S(1)} %collective-permute-done.17.args_1_, bf16[384,256]{1,0:T(8,128)(2,1)S(1)} %collective-permute-done.18.args_2_, ...), custom_call_target="tpu_custom_call" | custom-call | bytes 1572864 | tf_op jit(solution)/shard_map/finish/pallas_call | solution.py:42
  (42 shorter events, 0.3 us)
Async XLA Ops:
  0.6 6.8 %collective-permute-start.7 = (bf16[384,256]{1,0:T(8,128)(2,1)}, bf16[384,256]{1,0:T(8,128)(2,1)S(1)}, u32[]{:S(2)}, u32[]{:S(2)}) collective-permute-start(bf16[384,256]{1,0:T(8,128)(2,1)} %args_0_.4), channel_id=1, source_target_pairs={{0,1},{1,0},{2,3},{3,2},{4,5},{5,4},{6,7},{7,6},{8,9},{9,8},{10,11... | collective-permute-start | bytes 589832 | tf_op jit(solution)/shard_map/ppermute | solution.py:21
  1.1 8.3 %collective-permute-start.8 = (bf16[384,256]{1,0:T(8,128)(2,1)}, bf16[384,256]{1,0:T(8,128)(2,1)S(1)}, u32[]{:S(2)}, u32[]{:S(2)}) collective-permute-start(bf16[384,256]{1,0:T(8,128)(2,1)} %args_0_.4), channel_id=1, source_target_pairs={{0,4},{1,5},{2,6},{3,7},{4,0},{5,1},{6,2},{7,3},{8,12},{9,13},{10,... | collective-permute-start | bytes 589832 | tf_op jit(solution)/shard_map/ppermute | solution.py:21
  3.7 9.8 %collective-permute-start.5 = (bf16[384,256]{1,0:T(8,128)(2,1)}, bf16[384,256]{1,0:T(8,128)(2,1)S(1)}, u32[]{:S(2)}, u32[]{:S(2)}) collective-permute-start(bf16[384,256]{1,0:T(8,128)(2,1)} %args_0_.4), channel_id=1, source_target_pairs={{0,24},{8,16},{16,8},{24,0},{1,25},{9,17},{17,9},{25,1},{2,26},{10... | collective-permute-start | bytes 589832 | tf_op jit(solution)/shard_map/ppermute | solution.py:21
  7.3 11.2 %collective-permute-start.9 = (bf16[384,256]{1,0:T(8,128)(2,1)}, bf16[384,256]{1,0:T(8,128)(2,1)S(1)}, u32[]{:S(2)}, u32[]{:S(2)}) collective-permute-start(bf16[384,256]{1,0:T(8,128)(2,1)} %args_0_.4), channel_id=1, source_target_pairs={{0,8},{8,0},{16,24},{24,16},{1,9},{9,1},{17,25},{25,17},{2,10},{10... | collective-permute-start | bytes 589832 | tf_op jit(solution)/shard_map/ppermute | solution.py:21
  7.4 10.5 %collective-permute-start.10 = (bf16[384,256]{1,0:T(8,128)(2,1)}, bf16[384,256]{1,0:T(8,128)(2,1)S(1)}, u32[]{:S(2)}, u32[]{:S(2)}) collective-permute-start(bf16[384,256]{1,0:T(8,128)(2,1)} %args_0_.4), channel_id=1, source_target_pairs={{0,2},{1,3},{2,0},{3,1},{4,6},{5,7},{6,4},{7,5},{8,10},{9,11},{10,... | collective-permute-start | bytes 589832 | tf_op jit(solution)/shard_map/ppermute | solution.py:21
  8.9 9.6 %collective-permute-start.13 = (bf16[384,256]{1,0:T(8,128)(2,1)}, bf16[384,256]{1,0:T(8,128)(2,1)S(1)}, u32[]{:S(2)}, u32[]{:S(2)}) collective-permute-start(bf16[384,256]{1,0:T(8,128)(2,1)} %args_0_.4), channel_id=1, source_target_pairs={{0,6},{1,7},{2,4},{3,5},{4,2},{5,3},{6,0},{7,1},{8,14},{9,15},{10,... | collective-permute-start | bytes 589832 | tf_op jit(solution)/shard_map/ppermute | solution.py:21
  9.4 1.1 %copy-start.1 = (bf16[3,4,2,128,128]{4,3,2,1,0:T(8,128)(2,1)S(1)}, bf16[3,4,2,128,128]{4,3,2,1,0:T(8,128)(2,1)}, u32[]{:S(2)}) copy-start(bf16[3,4,2,128,128]{4,3,2,1,0:T(8,128)(2,1)} %in_hbm.1) | copy-start | bytes 2359300
  10.6 0.7 %copy-start.5 = (s32[3,4,2]{1,2,0:T(2,128)S(1)}, s32[3,4,2]{1,2,0:T(2,128)}, u32[]{:S(2)}) copy-start(s32[3,4,2]{1,2,0:T(2,128)} %param.16) | copy-start | bytes 292
  11.3 2.3 %copy-start.2 = (bf16[384,256]{1,0:T(8,128)(2,1)S(1)}, bf16[384,256]{1,0:T(8,128)(2,1)}, u32[]{:S(2)}) copy-start(bf16[384,256]{1,0:T(8,128)(2,1)} %args_0_.4) | copy-start | bytes 589828
  12.2 6.7 %collective-permute-start.12 = (bf16[384,256]{1,0:T(8,128)(2,1)S(1)}, bf16[384,256]{1,0:T(8,128)(2,1)S(1)}, u32[]{:S(2)}, u32[]{:S(2)}) collective-permute-start(bf16[384,256]{1,0:T(8,128)(2,1)S(1)} %collective-permute-done.8.args_5_), channel_id=1, source_target_pairs={{0,1},{1,0},{2,3},{3,2},{4,5},{5,4},{6,7},{7,6},{8,9},{9,8},{10,11... | collective-permute-start | bytes 589832 | tf_op jit(solution)/shard_map/ppermute | solution.py:21
  13.6 8.0 %copy-start = (bf16[3,9,128,128]{3,2,1,0:T(8,128)(2,1)S(1)}, bf16[3,9,128,128]{3,2,1,0:T(8,128)(2,1)}, u32[]{:S(2)}) copy-start(bf16[3,9,128,128]{3,2,1,0:T(8,128)(2,1)} %off_ref.1) | copy-start | bytes 2654212
  13.6 8.0 %copy-start.3 = (bf16[384,256]{1,0:T(8,128)(2,1)S(1)}, bf16[384,256]{1,0:T(8,128)(2,1)}, u32[]{:S(2)}) copy-start(bf16[384,256]{1,0:T(8,128)(2,1)} %args_13_.1) | copy-start | bytes 589828
  13.6 8.0 %copy-start.4 = (bf16[256,256]{1,0:T(8,128)(2,1)S(1)}, bf16[256,256]{1,0:T(8,128)(2,1)}, u32[]{:S(2)}) copy-start(bf16[256,256]{1,0:T(8,128)(2,1)} %args_11_.1) | copy-start | bytes 393220
  13.6 8.0 %copy-start.6 = (s32[3,9]{1,0:T(4,128)S(1)}, s32[3,9]{1,0:T(4,128)}, u32[]{:S(2)}) copy-start(s32[3,9]{1,0:T(4,128)} %refs_ref.3) | copy-start | bytes 328
  13.6 8.0 %copy-start.7 = (f32[256]{0:T(256)S(1)}, f32[256]{0:T(256)}, u32[]{:S(2)}) copy-start(f32[256]{0:T(256)} %param.14) | copy-start | bytes 3076
  13.6 8.0 %copy-start.8 = (s32[1,1,8,1]{2,3,1,0:T(1,128)S(1)}, s32[1,1,8,1]{2,3,1,0:T(1,128)}, u32[]{:S(2)}) copy-start(s32[1,1,8,1]{2,3,1,0:T(1,128)} %param.19) | copy-start | bytes 100
  13.6 7.9 %collective-permute-start.6 = (bf16[384,256]{1,0:T(8,128)(2,1)S(1)}, bf16[384,256]{1,0:T(8,128)(2,1)S(1)}, u32[]{:S(2)}, u32[]{:S(2)}) collective-permute-start(bf16[384,256]{1,0:T(8,128)(2,1)S(1)} %broadcast_select_fusion), channel_id=1, source_target_pairs={{8,0},{24,8},{16,24},{0,16},{9,1},{25,9},{17,25},{1,17},{10,2},{26... | collective-permute-start | bytes 589832 | tf_op jit(solution)/shard_map/ppermute | solution.py:26
  17.9 3.7 %collective-permute-start.11 = (bf16[384,256]{1,0:T(8,128)(2,1)S(1)}, bf16[384,256]{1,0:T(8,128)(2,1)S(1)}, u32[]{:S(2)}, u32[]{:S(2)}) collective-permute-start(bf16[384,256]{1,0:T(8,128)(2,1)S(1)} %collective-permute-done.10.args_3_), channel_id=1, source_target_pairs={{0,1},{1,0},{2,3},{3,2},{4,5},{5,4},{6,7},{7,6},{8,9},{9,8},{10,11... | collective-permute-start | bytes 589832 | tf_op jit(solution)/shard_map/ppermute | solution.py:21
  18.5 3.1 %collective-permute-start.14 = (bf16[384,256]{1,0:T(8,128)(2,1)S(1)}, bf16[384,256]{1,0:T(8,128)(2,1)S(1)}, u32[]{:S(2)}, u32[]{:S(2)}) collective-permute-start(bf16[384,256]{1,0:T(8,128)(2,1)S(1)} %collective-permute-done.13.args_7_), channel_id=1, source_target_pairs={{0,1},{1,0},{2,3},{3,2},{4,5},{5,4},{6,7},{7,6},{8,9},{9,8},{10,11... | collective-permute-start | bytes 589832 | tf_op jit(solution)/shard_map/ppermute | solution.py:21
  24.2 2.3 %collective-permute-start.15 = (bf16[128,256]{1,0:T(8,128)(2,1)S(1)}, bf16[128,256]{1,0:T(8,128)(2,1)S(1)}, u32[]{:S(2)}, u32[]{:S(2)}) collective-permute-start(bf16[128,256]{1,0:T(8,128)(2,1)S(1)} %get-tuple-element.45), channel_id=1, source_target_pairs={{0,1},{1,0},{2,3},{3,2},{4,5},{5,4},{6,7},{7,6},{8,9},{9,8},{10,11... | collective-permute-start | bytes 196616 | tf_op jit(solution)/shard_map/ppermute | solution.py:21
  24.3 27.5 %collective-permute-start.17 = (bf16[384,256]{1,0:T(8,128)(2,1)S(1)}, bf16[384,256]{1,0:T(8,128)(2,1)S(1)}, u32[]{:S(2)}, u32[]{:S(2)}) collective-permute-start(bf16[384,256]{1,0:T(8,128)(2,1)S(1)} %get-tuple-element.48), channel_id=1, source_target_pairs={{0,24},{8,16},{16,8},{24,0},{1,25},{9,17},{17,9},{25,1},{2,26},{10... | collective-permute-start | bytes 589832 | tf_op jit(solution)/shard_map/ppermute | solution.py:21
  26.6 5.4 %collective-permute-start.16 = (bf16[128,256]{1,0:T(8,128)(2,1)S(1)}, bf16[128,256]{1,0:T(8,128)(2,1)S(1)}, u32[]{:S(2)}, u32[]{:S(2)}) collective-permute-start(bf16[128,256]{1,0:T(8,128)(2,1)S(1)} %add_convert_fusion.4), channel_id=1, source_target_pairs={{0,4},{1,5},{2,6},{3,7},{4,0},{5,1},{6,2},{7,3},{8,12},{9,13},{10,... | collective-permute-start | bytes 196616 | tf_op jit(solution)/shard_map/ppermute | solution.py:21
  30.5 21.4 %collective-permute-start.18 = (bf16[384,256]{1,0:T(8,128)(2,1)S(1)}, bf16[384,256]{1,0:T(8,128)(2,1)S(1)}, u32[]{:S(2)}, u32[]{:S(2)}) collective-permute-start(bf16[384,256]{1,0:T(8,128)(2,1)S(1)} %get-tuple-element.50), channel_id=1, source_target_pairs={{0,16},{8,24},{16,0},{24,8},{1,17},{9,25},{17,1},{25,9},{2,18},{10... | collective-permute-start | bytes 589832 | tf_op jit(solution)/shard_map/ppermute | solution.py:21
  32.0 4.3 %collective-permute-start.1 = (bf16[128,256]{1,0:T(8,128)(2,1)S(1)}, bf16[128,256]{1,0:T(8,128)(2,1)S(1)}, u32[]{:S(2)}, u32[]{:S(2)}) collective-permute-start(bf16[128,256]{1,0:T(8,128)(2,1)S(1)} %get-tuple-element.11), channel_id=1, source_target_pairs={{0,2},{1,3},{2,0},{3,1},{4,6},{5,7},{6,4},{7,5},{8,10},{9,11},{10,... | collective-permute-start | bytes 196616 | tf_op jit(solution)/shard_map/cond/branch_1_fun/ppermute | solution.py:21
  36.3 5.0 %collective-permute-start.2 = (bf16[128,256]{1,0:T(8,128)(2,1)S(1)}, bf16[128,256]{1,0:T(8,128)(2,1)S(1)}, u32[]{:S(2)}, u32[]{:S(2)}) collective-permute-start(bf16[128,256]{1,0:T(8,128)(2,1)S(1)} %add_convert_fusion.2), channel_id=1, source_target_pairs={{0,8},{8,0},{16,24},{24,16},{1,9},{9,1},{17,25},{25,17},{2,10},{10... | collective-permute-start | bytes 196616 | tf_op jit(solution)/shard_map/cond/branch_1_fun/ppermute | solution.py:21
  37.1 14.7 %all-to-all-start = ((bf16[8,144,256]{2,1,0:T(8,128)(2,1)}), bf16[8,144,256]{2,1,0:T(8,128)(2,1)}, u32[]{:S(2)}, u32[]{:S(2)}) async-start(bf16[8,144,256]{2,1,0:T(8,128)(2,1)} %get-tuple-element.8), calls=%async_computation | async-start | bytes 1179648 | tf_op jit(solution)/shard_map/cond/branch_1_fun/all_to_all | solution.py:181
  41.3 7.7 %collective-permute-start.3 = (bf16[128,256]{1,0:T(8,128)(2,1)S(1)}, bf16[128,256]{1,0:T(8,128)(2,1)S(1)}, u32[]{:S(2)}, u32[]{:S(2)}) collective-permute-start(bf16[128,256]{1,0:T(8,128)(2,1)S(1)} %add_convert_fusion.1), channel_id=1, source_target_pairs={{0,16},{8,24},{16,0},{24,8},{1,17},{9,25},{17,1},{25,9},{2,18},{10... | collective-permute-start | bytes 196616 | tf_op jit(solution)/shard_map/cond/branch_1_fun/ppermute | solution.py:21
  43.1 8.7 %collective-permute-start = (bf16[384,256]{1,0:T(8,128)(2,1)S(1)}, bf16[384,256]{1,0:T(8,128)(2,1)}, u32[]{:S(2)}, u32[]{:S(2)}) collective-permute-start(bf16[384,256]{1,0:T(8,128)(2,1)S(1)} %get-tuple-element.9), channel_id=1, source_target_pairs={{0,8},{8,0},{16,24},{24,16},{1,9},{9,1},{17,25},{25,17},{2,10},{10... | collective-permute-start | bytes 589832 | tf_op jit(solution)/shard_map/cond/branch_1_fun/ppermute | solution.py:21
  49.0 1.3 %collective-permute-start.4 = (bf16[128,256]{1,0:T(8,128)(2,1)S(1)}, bf16[128,256]{1,0:T(8,128)(2,1)S(1)}, u32[]{:S(2)}, u32[]{:S(2)}) collective-permute-start(bf16[128,256]{1,0:T(8,128)(2,1)S(1)} %add_convert_fusion.part_ref), channel_id=1, source_target_pairs={{0,1},{1,0},{2,3},{3,2},{4,5},{5,4},{6,7},{7,6},{8,9},{9,8},{10,11... | collective-permute-start | bytes 196616 | tf_op jit(solution)/shard_map/cond/branch_1_fun/ppermute | solution.py:21
  51.8 2.3 %copy-start.9 = (bf16[256,256]{1,0:T(8,128)(2,1)}, bf16[256,256]{1,0:T(8,128)(2,1)S(1)}, u32[]{:S(2)}) copy-start(bf16[256,256]{1,0:T(8,128)(2,1)S(1)} %get-tuple-element.33) | copy-start | bytes 393220

commit v8 on v7

--- a/solution.py
+++ b/solution.py
@@ -115,9 +115,10 @@
     give_ref[...] = term_ref[pl.ds(pl.multiple_of((1 - core) * half, half), half), :].astype(BF16)
 
 
-def spread_rest(want_ref, refs_ref, a_ref, off_ref, grad_ref, own_ref, near_ref, next_ref, out_ref, total_ref):
+def spread_rest(want_ref, refs_ref, a_ref, off_ref, grad_ref, made_ref, act_ref, own_ref, near_ref, next_ref, out_ref, total_ref):
     blocks, tiles, edge, _ = off_ref.shape
     cap, doms = want_ref.shape
+    act_ref[...] = made_ref[...]
     grad_agg = grad_ref[...]
     rows = grad_agg.shape[0]
     order = turns(a_ref.shape[1] // rows)
@@ -200,7 +201,7 @@
     odd = [near] + [swapped(after(value, a), "dom", 1) for n, value in enumerate(even) if n]
     others = [value for pair in zip(even, odd) for value in pair][1:]
     begun = call(begin, [shape((rows, width), F32)], (a, *panels[:-1]), "v" * count, name="begin")[0]
-    activated, keep, give, *terms, grad_agg = call(
+    made, keep, give, *terms, grad_agg = call(
         functools.partial(layer, count, doms),
         [flat] + [shape((width // 2, width), BF16)] * 2 + [flat] * (count - 2),
         (me, requests, off_ref, panels[-1], begun, *others, a, off_vals, weight, bias.reshape(1, width), cotangent),
@@ -210,8 +211,8 @@
     part = (keep.astype(F32) + swapped(give, "dom", 1).astype(F32)).astype(BF16)
     first = part
     part = joined(part, "dom", dom_steps[0])
-    own, near_terms, next_terms, outer = call(
-        spread_rest, [flat, flat, flat, shape((doms, cap * (edge + 16), width), BF16)], (requests, off_ref, a, off_vals, grad_agg), "ssvvv",
+    activated, own, near_terms, next_terms, outer = call(
+        spread_rest, [flat, flat, flat, flat, shape((doms, cap * (edge + 16), width), BF16)], (requests, off_ref, a, off_vals, grad_agg, made), "ssvvvv",
         scratch=[pltpu.VMEM((slots, edge, width), F32)], flops=10**9, name="rest")
     terms = dict(zip([k for k in turns(count) if k > 2], terms)) | {2: next_terms}
     got = [swapped(after(terms[k], first if k == 2 else None), "rep", k) for k in range(count - 1, 1, -1)]

time: 54.4 us -> 54 us (level)
  no operation moved by 1% of the time
where the time goes in v8:
time: 54 us; the launch traced here: 53.7 us
  starting transfers between devices  27.7 us (51%)
  waiting for transfers between devices  14.2 us (26%)
  Pallas kernels  8.79 us (16%)
  local copies, waits for them, and re-layouts  1.86 us (3%)
  between operations  0.84 us (2%)
    ppermute x18, starting transfers between devices, swapped(): lax.ppermute(value, axis, [(i, i ^ k) for i in range(lax.axis_size(axis))])  19.2 us
    ppermute x18, waiting for transfers between devices, swapped(): lax.ppermute(value, axis, [(i, i ^ k) for i in range(lax.axis_size(axis))])  11.6 us
    pallas_call x6, Pallas kernels, call(): pl.pallas_call(body, out_shape=outs, in_specs=[pl.BlockSpec(memory_space=...  8.79 us
    ppermute x1, starting transfers between devices, relayed(): return lax.ppermute(value, 'rep', [pair[::turns] for pair in pairs])  4.25 us
    all_to_all x1, starting transfers between devices, exchange(): lax.all_to_all(outer, 'dom', split_axis=0, concat_axis=0, tiled=True)  4.19 us
    ppermute x1, waiting for transfers between devices, relayed(): return lax.ppermute(value, 'rep', [pair[::turns] for pair in pairs])  2.6 us
    unnamed x20, local copies, waits for them, and re-layouts  1.86 us
  transfers between devices with their start and end apart: 20, of which 7 were waited for; matrix products, arithmetic and copies ran while one was open for 0% of the time, Pallas kernels for 8%

profile of v8, /device:TPU:0, one launch (start us, length us, event | category | flops | bytes accessed | tf_op | source)
XLA Modules:
  0.0 53.7 jit_solution(1928048416344476831)
XLA Ops:
  0.6 0.5 collective-permute-start.5
  1.1 2.6 %collective-permute-start.6 = (bf16[384,256]{1,0:T(8,128)(2,1)}, bf16[384,256]{1,0:T(8,128)(2,1)S(1)}, u32[]{:S(2)}, u32[]{:S(2)}) collective-permute-start(bf16[384,256]{1,0:T(8,128)(2,1)} %args_0_.4), channel_id=1, source_target_pairs={{0,4},{1,5},{2,6},{3,7},{4,0},{5,1},{6,2},{7,3},{8,12},{9,13},{10,... | collective-permute-start | bytes 589832 | tf_op jit(solution)/shard_map/ppermute | solution.py:21
  3.7 3.6 %collective-permute-start.7 = (bf16[384,256]{1,0:T(8,128)(2,1)}, bf16[384,256]{1,0:T(8,128)(2,1)S(1)}, u32[]{:S(2)}, u32[]{:S(2)}) collective-permute-start(bf16[384,256]{1,0:T(8,128)(2,1)} %args_0_.4), channel_id=1, source_target_pairs={{0,24},{8,16},{16,8},{24,0},{1,25},{9,17},{17,9},{25,1},{2,26},{10... | collective-permute-start | bytes 589832 | tf_op jit(solution)/shard_map/ppermute | solution.py:21
  7.3 0.1 pad_add_fusion.me_ref
  7.4 1.5 %collective-permute-start.10 = (bf16[384,256]{1,0:T(8,128)(2,1)}, bf16[384,256]{1,0:T(8,128)(2,1)S(1)}, u32[]{:S(2)}, u32[]{:S(2)}) collective-permute-start(bf16[384,256]{1,0:T(8,128)(2,1)} %args_0_.4), channel_id=1, source_target_pairs={{0,2},{1,3},{2,0},{3,1},{4,6},{5,7},{6,4},{7,5},{8,10},{9,11},{10,... | collective-permute-start | bytes 589832 | tf_op jit(solution)/shard_map/ppermute | solution.py:21
  8.9 0.5 collective-permute-start.13
  9.4 1.1 %copy-done.1 = bf16[3,4,2,128,128]{4,3,2,1,0:T(8,128)(2,1)S(1)} copy-done((bf16[3,4,2,128,128]{4,3,2,1,0:T(8,128)(2,1)S(1)}, bf16[3,4,2,128,128]{4,3,2,1,0:T(8,128)(2,1)}, u32[]{:S(2)}) %copy-start.1) | copy-done | bytes 786456
  10.6 0.7 %copy-done.5 = s32[3,4,2]{1,2,0:T(2,128)S(1)} copy-done((s32[3,4,2]{1,2,0:T(2,128)S(1)}, s32[3,4,2]{1,2,0:T(2,128)}, u32[]{:S(2)}) %copy-start.5) | copy-done | bytes 120
  11.3 0.9 %arrange.1.a_ref.args_9_ = bf16[384,1536]{1,0:T(8,128)(2,1)S(1)} custom-call(s32[2]{0:T(128)S(1)} %pad_add_fusion.me_ref, s32[3,2,4]{2,1,0:T(2,128)S(1)} %bitcast.7, bf16[3,4,2,128,128]{4,3,2,1,0:T(8,128)(2,1)S(1)} %copy-done.1), custom_call_target="tpu_custom_call" | custom-call | bytes 1966184 | tf_op jit(solution)/shard_map/arrange/pallas_call | solution.py:42
  12.2 0.1 collective-permute-start.12
  12.3 1.3 %collective-permute-done.7.args_1_ = bf16[384,256]{1,0:T(8,128)(2,1)S(1)} collective-permute-done((bf16[384,256]{1,0:T(8,128)(2,1)}, bf16[384,256]{1,0:T(8,128)(2,1)S(1)}, u32[]{:S(2)}, u32[]{:S(2)}) %collective-permute-start.7) | collective-permute-done | bytes 196640 | tf_op jit(solution)/shard_map/ppermute | solution.py:21
  13.6 4.3 %collective-permute-start.8 = (bf16[384,256]{1,0:T(8,128)(2,1)S(1)}, bf16[384,256]{1,0:T(8,128)(2,1)S(1)}, u32[]{:S(2)}, u32[]{:S(2)}) collective-permute-start(bf16[384,256]{1,0:T(8,128)(2,1)S(1)} %broadcast_select_fusion), channel_id=1, source_target_pairs={{8,0},{24,8},{16,24},{0,16},{9,1},{25,9},{17,25},{1,17},{10,2},{26... | collective-permute-start | bytes 589832 | tf_op jit(solution)/shard_map/ppermute | solution.py:26
  17.9 0.6 %collective-permute-done.13.args_7_ = bf16[384,256]{1,0:T(8,128)(2,1)S(1)} collective-permute-done((bf16[384,256]{1,0:T(8,128)(2,1)}, bf16[384,256]{1,0:T(8,128)(2,1)S(1)}, u32[]{:S(2)}, u32[]{:S(2)}) %collective-permute-start.13) | collective-permute-done | bytes 196640 | tf_op jit(solution)/shard_map/ppermute | solution.py:21
  18.5 0.4 begin.1.args_1_
  18.9 2.6 %collective-permute-done.8.args_0_ = bf16[384,256]{1,0:T(8,128)(2,1)S(1)} collective-permute-done((bf16[384,256]{1,0:T(8,128)(2,1)S(1)}, bf16[384,256]{1,0:T(8,128)(2,1)S(1)}, u32[]{:S(2)}, u32[]{:S(2)}) %collective-permute-start.8) | collective-permute-done | bytes 196640 | tf_op jit(solution)/shard_map/ppermute | solution.py:26
  21.6 2.1 %layer.1 = (bf16[384,256]{1,0:T(8,128)(2,1)S(1)}, bf16[128,256]{1,0:T(8,128)(2,1)S(1)}, bf16[128,256]{1,0:T(8,128)(2,1)S(1)}, bf16[384,256]{1,0:T(8,128)(2,1)S(1)}, bf16[384,256]{1,0:T(8,128)(2,1)S(1)}) custom-call(s32[2]{0:T(128)S(1)} %pad_add_fusion.me_ref, s32[1,8]{1,0:T(1,128)S(1)} %bitcast.9, s32[3,9]{1,0:T(4,128)S(1)} %copy-done.6, ...), custom_call_target="tpu_custom_call" | custom-call | flops 1000000000 | bytes 5080212 | tf_op jit(solution)/shard_map/layer/pallas_call | solution.py:42
  23.8 2.3 %collective-permute-start.17 = (bf16[384,256]{1,0:T(8,128)(2,1)S(1)}, bf16[384,256]{1,0:T(8,128)(2,1)S(1)}, u32[]{:S(2)}, u32[]{:S(2)}) collective-permute-start(bf16[384,256]{1,0:T(8,128)(2,1)S(1)} %get-tuple-element.50), channel_id=1, source_target_pairs={{0,24},{8,16},{16,8},{24,0},{1,25},{9,17},{17,9},{25,1},{2,26},{10... | collective-permute-start | bytes 589832 | tf_op jit(solution)/shard_map/ppermute | solution.py:21
  26.1 1.4 %collective-permute-start.16 = (bf16[128,256]{1,0:T(8,128)(2,1)S(1)}, bf16[128,256]{1,0:T(8,128)(2,1)S(1)}, u32[]{:S(2)}, u32[]{:S(2)}) collective-permute-start(bf16[128,256]{1,0:T(8,128)(2,1)S(1)} %add_convert_fusion.4), channel_id=1, source_target_pairs={{0,4},{1,5},{2,6},{3,7},{4,0},{5,1},{6,2},{7,3},{8,12},{9,13},{10,... | collective-permute-start | bytes 196616 | tf_op jit(solution)/shard_map/ppermute | solution.py:21
  27.6 2.5 %rest.1 = (bf16[384,256]{1,0:T(8,128)(2,1)}, bf16[384,256]{1,0:T(8,128)(2,1)S(1)}, bf16[384,256]{1,0:T(8,128)(2,1)S(1)}, bf16[384,256]{1,0:T(8,128)(2,1)S(1)}, bf16[8,144,256]{2,1,0:T(8,128)(2,1)}) custom-call(s32[1,8]{1,0:T(1,128)S(1)} %bitcast.11, s32[3,9]{1,0:T(4,128)S(1)} %copy-done.6, bf16[384,1536]{1,0:T(8,128)(2,1)S(1)} %arrange.1.a_ref.args_9_, ...), custom_call_target="tpu_custom_call" | custom-call | flops 1000000000 | bytes 3833996 | tf_op jit(solution)/shard_map/rest/pallas_call | solution.py:42
  30.0 1.5 %collective-permute-start.18 = (bf16[384,256]{1,0:T(8,128)(2,1)S(1)}, bf16[384,256]{1,0:T(8,128)(2,1)S(1)}, u32[]{:S(2)}, u32[]{:S(2)}) collective-permute-start(bf16[384,256]{1,0:T(8,128)(2,1)S(1)} %get-tuple-element.52), channel_id=1, source_target_pairs={{0,16},{8,24},{16,0},{24,8},{1,17},{9,25},{17,1},{25,9},{2,18},{10... | collective-permute-start | bytes 589832 | tf_op jit(solution)/shard_map/ppermute | solution.py:21
  31.6 19.8 %conditional.1 = (bf16[8,144,256]{2,1,0:T(8,128)(2,1)}, bf16[384,256]{1,0:T(8,128)(2,1)}, bf16[256,256]{1,0:T(8,128)(2,1)S(1)}) conditional(s32[]{:T(128)} %bitcast.5, () %tuple.29, (bf16[8,144,256]{2,1,0:T(8,128)(2,1)}, bf16[384,256]{1,0:T(8,128)(2,1)S(1)}, bf16[128,256]{1,0:T(8,128)(2,1)S(1)}, s32[2]{0:T(128)S(1)}) %tuple.30), branch_computations={%region_0.1_spmd, %region_1.2_spmd} | conditional | flops 393216 | bytes 4456712 | solution.py:35
  31.6 1.5 %collective-permute-start.1 = (bf16[128,256]{1,0:T(8,128)(2,1)S(1)}, bf16[128,256]{1,0:T(8,128)(2,1)S(1)}, u32[]{:S(2)}, u32[]{:S(2)}) collective-permute-start(bf16[128,256]{1,0:T(8,128)(2,1)S(1)} %get-tuple-element.11), channel_id=1, source_target_pairs={{0,2},{1,3},{2,0},{3,1},{4,6},{5,7},{6,4},{7,5},{8,10},{9,11},{10,... | collective-permute-start | bytes 196616 | tf_op jit(solution)/shard_map/cond/branch_1_fun/ppermute | solution.py:21
  33.1 2.8 %collective-permute-done.1 = bf16[128,256]{1,0:T(8,128)(2,1)S(1)} collective-permute-done((bf16[128,256]{1,0:T(8,128)(2,1)S(1)}, bf16[128,256]{1,0:T(8,128)(2,1)S(1)}, u32[]{:S(2)}, u32[]{:S(2)}) %collective-permute-start.1) | collective-permute-done | bytes 65568 | tf_op jit(solution)/shard_map/cond/branch_1_fun/ppermute | solution.py:21
  35.9 0.7 %collective-permute-start.2 = (bf16[128,256]{1,0:T(8,128)(2,1)S(1)}, bf16[128,256]{1,0:T(8,128)(2,1)S(1)}, u32[]{:S(2)}, u32[]{:S(2)}) collective-permute-start(bf16[128,256]{1,0:T(8,128)(2,1)S(1)} %add_convert_fusion.2), channel_id=1, source_target_pairs={{0,8},{8,0},{16,24},{24,16},{1,9},{9,1},{17,25},{25,17},{2,10},{10... | collective-permute-start | bytes 196616 | tf_op jit(solution)/shard_map/cond/branch_1_fun/ppermute | solution.py:21
  36.7 4.2 %all-to-all-start = ((bf16[8,144,256]{2,1,0:T(8,128)(2,1)}), bf16[8,144,256]{2,1,0:T(8,128)(2,1)}, u32[]{:S(2)}, u32[]{:S(2)}) async-start(bf16[8,144,256]{2,1,0:T(8,128)(2,1)} %get-tuple-element.8), calls=%async_computation | async-start | bytes 1179648 | tf_op jit(solution)/shard_map/cond/branch_1_fun/all_to_all | solution.py:182
  40.9 1.7 %collective-permute-start.3 = (bf16[128,256]{1,0:T(8,128)(2,1)S(1)}, bf16[128,256]{1,0:T(8,128)(2,1)S(1)}, u32[]{:S(2)}, u32[]{:S(2)}) collective-permute-start(bf16[128,256]{1,0:T(8,128)(2,1)S(1)} %add_convert_fusion.1), channel_id=1, source_target_pairs={{0,16},{8,24},{16,0},{24,8},{1,17},{9,25},{17,1},{25,9},{2,18},{10... | collective-permute-start | bytes 196616 | tf_op jit(solution)/shard_map/cond/branch_1_fun/ppermute | solution.py:21
  42.7 1.1 %collective-permute-start = (bf16[384,256]{1,0:T(8,128)(2,1)S(1)}, bf16[384,256]{1,0:T(8,128)(2,1)}, u32[]{:S(2)}, u32[]{:S(2)}) collective-permute-start(bf16[384,256]{1,0:T(8,128)(2,1)S(1)} %get-tuple-element.9), channel_id=1, source_target_pairs={{0,8},{8,0},{16,24},{24,16},{1,9},{9,1},{17,25},{25,17},{2,10},{10... | collective-permute-start | bytes 589832 | tf_op jit(solution)/shard_map/cond/branch_1_fun/ppermute | solution.py:21
  43.8 4.8 %collective-permute-done.3 = bf16[128,256]{1,0:T(8,128)(2,1)S(1)} collective-permute-done((bf16[128,256]{1,0:T(8,128)(2,1)S(1)}, bf16[128,256]{1,0:T(8,128)(2,1)S(1)}, u32[]{:S(2)}, u32[]{:S(2)}) %collective-permute-start.3) | collective-permute-done | bytes 65568 | tf_op jit(solution)/shard_map/cond/branch_1_fun/ppermute | solution.py:21
  48.7 1.2 %collective-permute-done.4.other_ref = bf16[128,256]{1,0:T(8,128)(2,1)S(1)} collective-permute-done((bf16[128,256]{1,0:T(8,128)(2,1)S(1)}, bf16[128,256]{1,0:T(8,128)(2,1)S(1)}, u32[]{:S(2)}, u32[]{:S(2)}) %collective-permute-start.4) | collective-permute-done | bytes 65568 | tf_op jit(solution)/shard_map/cond/branch_1_fun/ppermute | solution.py:21
  49.9 0.6 %join.1 = bf16[256,256]{1,0:T(8,128)(2,1)S(1)} custom-call(s32[2]{0:T(128)S(1)} %get-tuple-element.10.me_ref, bf16[128,256]{1,0:T(8,128)(2,1)S(1)} %add_convert_fusion.part_ref, bf16[128,256]{1,0:T(8,128)(2,1)S(1)} %collective-permute-done.4.other_ref), custom_call_target="tpu_custom_call" | custom-call | bytes 262152 | tf_op jit(solution)/shard_map/cond/branch_1_fun/join/pallas_call | solution.py:42
  50.5 0.9 %collective-permute-done = bf16[384,256]{1,0:T(8,128)(2,1)} collective-permute-done((bf16[384,256]{1,0:T(8,128)(2,1)S(1)}, bf16[384,256]{1,0:T(8,128)(2,1)}, u32[]{:S(2)}, u32[]{:S(2)}) %collective-permute-start) | collective-permute-done | bytes 196640 | tf_op jit(solution)/shard_map/cond/branch_1_fun/ppermute | solution.py:21
  51.4 2.3 %finish.1 = bf16[384,256]{1,0:T(8,128)(2,1)} custom-call(bf16[8,144,256]{2,1,0:T(8,128)(2,1)} %get-tuple-element.48.coming_ref, bf16[384,256]{1,0:T(8,128)(2,1)S(1)} %get-tuple-element.49.args_0_, bf16[384,256]{1,0:T(8,128)(2,1)S(1)} %collective-permute-done.17.args_1_, bf16[384,256]{1,0:T(8,128)(2,1)S(1)} %collective-permute-done.18.args_2_, ...), custom_call_target="tpu_custom_call" | custom-call | bytes 1572864 | tf_op jit(solution)/shard_map/finish/pallas_call | solution.py:42
  (42 shorter events, 0.4 us)
Async XLA Ops:
  0.6 6.8 %collective-permute-start.5 = (bf16[384,256]{1,0:T(8,128)(2,1)}, bf16[384,256]{1,0:T(8,128)(2,1)S(1)}, u32[]{:S(2)}, u32[]{:S(2)}) collective-permute-start(bf16[384,256]{1,0:T(8,128)(2,1)} %args_0_.4), channel_id=1, source_target_pairs={{0,1},{1,0},{2,3},{3,2},{4,5},{5,4},{6,7},{7,6},{8,9},{9,8},{10,11... | collective-permute-start | bytes 589832 | tf_op jit(solution)/shard_map/ppermute | solution.py:21
  1.1 8.3 %collective-permute-start.6 = (bf16[384,256]{1,0:T(8,128)(2,1)}, bf16[384,256]{1,0:T(8,128)(2,1)S(1)}, u32[]{:S(2)}, u32[]{:S(2)}) collective-permute-start(bf16[384,256]{1,0:T(8,128)(2,1)} %args_0_.4), channel_id=1, source_target_pairs={{0,4},{1,5},{2,6},{3,7},{4,0},{5,1},{6,2},{7,3},{8,12},{9,13},{10,... | collective-permute-start | bytes 589832 | tf_op jit(solution)/shard_map/ppermute | solution.py:21
  3.7 9.8 %collective-permute-start.7 = (bf16[384,256]{1,0:T(8,128)(2,1)}, bf16[384,256]{1,0:T(8,128)(2,1)S(1)}, u32[]{:S(2)}, u32[]{:S(2)}) collective-permute-start(bf16[384,256]{1,0:T(8,128)(2,1)} %args_0_.4), channel_id=1, source_target_pairs={{0,24},{8,16},{16,8},{24,0},{1,25},{9,17},{17,9},{25,1},{2,26},{10... | collective-permute-start | bytes 589832 | tf_op jit(solution)/shard_map/ppermute | solution.py:21
  7.3 11.2 %collective-permute-start.9 = (bf16[384,256]{1,0:T(8,128)(2,1)}, bf16[384,256]{1,0:T(8,128)(2,1)S(1)}, u32[]{:S(2)}, u32[]{:S(2)}) collective-permute-start(bf16[384,256]{1,0:T(8,128)(2,1)} %args_0_.4), channel_id=1, source_target_pairs={{0,8},{8,0},{16,24},{24,16},{1,9},{9,1},{17,25},{25,17},{2,10},{10... | collective-permute-start | bytes 589832 | tf_op jit(solution)/shard_map/ppermute | solution.py:21
  7.4 10.5 %collective-permute-start.10 = (bf16[384,256]{1,0:T(8,128)(2,1)}, bf16[384,256]{1,0:T(8,128)(2,1)S(1)}, u32[]{:S(2)}, u32[]{:S(2)}) collective-permute-start(bf16[384,256]{1,0:T(8,128)(2,1)} %args_0_.4), channel_id=1, source_target_pairs={{0,2},{1,3},{2,0},{3,1},{4,6},{5,7},{6,4},{7,5},{8,10},{9,11},{10,... | collective-permute-start | bytes 589832 | tf_op jit(solution)/shard_map/ppermute | solution.py:21
  8.9 9.6 %collective-permute-start.13 = (bf16[384,256]{1,0:T(8,128)(2,1)}, bf16[384,256]{1,0:T(8,128)(2,1)S(1)}, u32[]{:S(2)}, u32[]{:S(2)}) collective-permute-start(bf16[384,256]{1,0:T(8,128)(2,1)} %args_0_.4), channel_id=1, source_target_pairs={{0,6},{1,7},{2,4},{3,5},{4,2},{5,3},{6,0},{7,1},{8,14},{9,15},{10,... | collective-permute-start | bytes 589832 | tf_op jit(solution)/shard_map/ppermute | solution.py:21
  9.4 1.1 %copy-start.1 = (bf16[3,4,2,128,128]{4,3,2,1,0:T(8,128)(2,1)S(1)}, bf16[3,4,2,128,128]{4,3,2,1,0:T(8,128)(2,1)}, u32[]{:S(2)}) copy-start(bf16[3,4,2,128,128]{4,3,2,1,0:T(8,128)(2,1)} %in_hbm.1) | copy-start | bytes 2359300
  10.6 0.7 %copy-start.5 = (s32[3,4,2]{1,2,0:T(2,128)S(1)}, s32[3,4,2]{1,2,0:T(2,128)}, u32[]{:S(2)}) copy-start(s32[3,4,2]{1,2,0:T(2,128)} %param.16) | copy-start | bytes 292
  11.3 2.3 %copy-start.2 = (bf16[384,256]{1,0:T(8,128)(2,1)S(1)}, bf16[384,256]{1,0:T(8,128)(2,1)}, u32[]{:S(2)}) copy-start(bf16[384,256]{1,0:T(8,128)(2,1)} %args_0_.4) | copy-start | bytes 589828
  12.2 6.7 %collective-permute-start.12 = (bf16[384,256]{1,0:T(8,128)(2,1)S(1)}, bf16[384,256]{1,0:T(8,128)(2,1)S(1)}, u32[]{:S(2)}, u32[]{:S(2)}) collective-permute-start(bf16[384,256]{1,0:T(8,128)(2,1)S(1)} %collective-permute-done.6.args_5_), channel_id=1, source_target_pairs={{0,1},{1,0},{2,3},{3,2},{4,5},{5,4},{6,7},{7,6},{8,9},{9,8},{10,11... | collective-permute-start | bytes 589832 | tf_op jit(solution)/shard_map/ppermute | solution.py:21
  13.6 8.0 %copy-start = (bf16[3,9,128,128]{3,2,1,0:T(8,128)(2,1)S(1)}, bf16[3,9,128,128]{3,2,1,0:T(8,128)(2,1)}, u32[]{:S(2)}) copy-start(bf16[3,9,128,128]{3,2,1,0:T(8,128)(2,1)} %off_ref.1) | copy-start | bytes 2654212
  13.6 8.0 %copy-start.3 = (bf16[384,256]{1,0:T(8,128)(2,1)S(1)}, bf16[384,256]{1,0:T(8,128)(2,1)}, u32[]{:S(2)}) copy-start(bf16[384,256]{1,0:T(8,128)(2,1)} %args_13_.1) | copy-start | bytes 589828
  13.6 8.0 %copy-start.4 = (bf16[256,256]{1,0:T(8,128)(2,1)S(1)}, bf16[256,256]{1,0:T(8,128)(2,1)}, u32[]{:S(2)}) copy-start(bf16[256,256]{1,0:T(8,128)(2,1)} %args_11_.1) | copy-start | bytes 393220
  13.6 8.0 %copy-start.6 = (s32[3,9]{1,0:T(4,128)S(1)}, s32[3,9]{1,0:T(4,128)}, u32[]{:S(2)}) copy-start(s32[3,9]{1,0:T(4,128)} %refs_ref.3) | copy-start | bytes 328
  13.6 8.0 %copy-start.7 = (f32[256]{0:T(256)S(1)}, f32[256]{0:T(256)}, u32[]{:S(2)}) copy-start(f32[256]{0:T(256)} %param.14) | copy-start | bytes 3076
  13.6 8.0 %copy-start.8 = (s32[1,1,8,1]{2,3,1,0:T(1,128)S(1)}, s32[1,1,8,1]{2,3,1,0:T(1,128)}, u32[]{:S(2)}) copy-start(s32[1,1,8,1]{2,3,1,0:T(1,128)} %param.19) | copy-start | bytes 100
  13.6 7.9 %collective-permute-start.8 = (bf16[384,256]{1,0:T(8,128)(2,1)S(1)}, bf16[384,256]{1,0:T(8,128)(2,1)S(1)}, u32[]{:S(2)}, u32[]{:S(2)}) collective-permute-start(bf16[384,256]{1,0:T(8,128)(2,1)S(1)} %broadcast_select_fusion), channel_id=1, source_target_pairs={{8,0},{24,8},{16,24},{0,16},{9,1},{25,9},{17,25},{1,17},{10,2},{26... | collective-permute-start | bytes 589832 | tf_op jit(solution)/shard_map/ppermute | solution.py:26
  17.9 3.7 %collective-permute-start.11 = (bf16[384,256]{1,0:T(8,128)(2,1)S(1)}, bf16[384,256]{1,0:T(8,128)(2,1)S(1)}, u32[]{:S(2)}, u32[]{:S(2)}) collective-permute-start(bf16[384,256]{1,0:T(8,128)(2,1)S(1)} %collective-permute-done.10.args_3_), channel_id=1, source_target_pairs={{0,1},{1,0},{2,3},{3,2},{4,5},{5,4},{6,7},{7,6},{8,9},{9,8},{10,11... | collective-permute-start | bytes 589832 | tf_op jit(solution)/shard_map/ppermute | solution.py:21
  18.5 3.1 %collective-permute-start.14 = (bf16[384,256]{1,0:T(8,128)(2,1)S(1)}, bf16[384,256]{1,0:T(8,128)(2,1)S(1)}, u32[]{:S(2)}, u32[]{:S(2)}) collective-permute-start(bf16[384,256]{1,0:T(8,128)(2,1)S(1)} %collective-permute-done.13.args_7_), channel_id=1, source_target_pairs={{0,1},{1,0},{2,3},{3,2},{4,5},{5,4},{6,7},{7,6},{8,9},{9,8},{10,11... | collective-permute-start | bytes 589832 | tf_op jit(solution)/shard_map/ppermute | solution.py:21
  23.7 2.4 %collective-permute-start.15 = (bf16[128,256]{1,0:T(8,128)(2,1)S(1)}, bf16[128,256]{1,0:T(8,128)(2,1)S(1)}, u32[]{:S(2)}, u32[]{:S(2)}) collective-permute-start(bf16[128,256]{1,0:T(8,128)(2,1)S(1)} %get-tuple-element.47), channel_id=1, source_target_pairs={{0,1},{1,0},{2,3},{3,2},{4,5},{5,4},{6,7},{7,6},{8,9},{9,8},{10,11... | collective-permute-start | bytes 196616 | tf_op jit(solution)/shard_map/ppermute | solution.py:21
  23.8 27.5 %collective-permute-start.17 = (bf16[384,256]{1,0:T(8,128)(2,1)S(1)}, bf16[384,256]{1,0:T(8,128)(2,1)S(1)}, u32[]{:S(2)}, u32[]{:S(2)}) collective-permute-start(bf16[384,256]{1,0:T(8,128)(2,1)S(1)} %get-tuple-element.50), channel_id=1, source_target_pairs={{0,24},{8,16},{16,8},{24,0},{1,25},{9,17},{17,9},{25,1},{2,26},{10... | collective-permute-start | bytes 589832 | tf_op jit(solution)/shard_map/ppermute | solution.py:21
  26.1 5.4 %collective-permute-start.16 = (bf16[128,256]{1,0:T(8,128)(2,1)S(1)}, bf16[128,256]{1,0:T(8,128)(2,1)S(1)}, u32[]{:S(2)}, u32[]{:S(2)}) collective-permute-start(bf16[128,256]{1,0:T(8,128)(2,1)S(1)} %add_convert_fusion.4), channel_id=1, source_target_pairs={{0,4},{1,5},{2,6},{3,7},{4,0},{5,1},{6,2},{7,3},{8,12},{9,13},{10,... | collective-permute-start | bytes 196616 | tf_op jit(solution)/shard_map/ppermute | solution.py:21
  30.0 21.3 %collective-permute-start.18 = (bf16[384,256]{1,0:T(8,128)(2,1)S(1)}, bf16[384,256]{1,0:T(8,128)(2,1)S(1)}, u32[]{:S(2)}, u32[]{:S(2)}) collective-permute-start(bf16[384,256]{1,0:T(8,128)(2,1)S(1)} %get-tuple-element.52), channel_id=1, source_target_pairs={{0,16},{8,24},{16,0},{24,8},{1,17},{9,25},{17,1},{25,9},{2,18},{10... | collective-permute-start | bytes 589832 | tf_op jit(solution)/shard_map/ppermute | solution.py:21
  31.6 4.3 %collective-permute-start.1 = (bf16[128,256]{1,0:T(8,128)(2,1)S(1)}, bf16[128,256]{1,0:T(8,128)(2,1)S(1)}, u32[]{:S(2)}, u32[]{:S(2)}) collective-permute-start(bf16[128,256]{1,0:T(8,128)(2,1)S(1)} %get-tuple-element.11), channel_id=1, source_target_pairs={{0,2},{1,3},{2,0},{3,1},{4,6},{5,7},{6,4},{7,5},{8,10},{9,11},{10,... | collective-permute-start | bytes 196616 | tf_op jit(solution)/shard_map/cond/branch_1_fun/ppermute | solution.py:21
  35.9 4.9 %collective-permute-start.2 = (bf16[128,256]{1,0:T(8,128)(2,1)S(1)}, bf16[128,256]{1,0:T(8,128)(2,1)S(1)}, u32[]{:S(2)}, u32[]{:S(2)}) collective-permute-start(bf16[128,256]{1,0:T(8,128)(2,1)S(1)} %add_convert_fusion.2), channel_id=1, source_target_pairs={{0,8},{8,0},{16,24},{24,16},{1,9},{9,1},{17,25},{25,17},{2,10},{10... | collective-permute-start | bytes 196616 | tf_op jit(solution)/shard_map/cond/branch_1_fun/ppermute | solution.py:21
  36.7 14.7 %all-to-all-start = ((bf16[8,144,256]{2,1,0:T(8,128)(2,1)}), bf16[8,144,256]{2,1,0:T(8,128)(2,1)}, u32[]{:S(2)}, u32[]{:S(2)}) async-start(bf16[8,144,256]{2,1,0:T(8,128)(2,1)} %get-tuple-element.8), calls=%async_computation | async-start | bytes 1179648 | tf_op jit(solution)/shard_map/cond/branch_1_fun/all_to_all | solution.py:182
  40.9 7.7 %collective-permute-start.3 = (bf16[128,256]{1,0:T(8,128)(2,1)S(1)}, bf16[128,256]{1,0:T(8,128)(2,1)S(1)}, u32[]{:S(2)}, u32[]{:S(2)}) collective-permute-start(bf16[128,256]{1,0:T(8,128)(2,1)S(1)} %add_convert_fusion.1), channel_id=1, source_target_pairs={{0,16},{8,24},{16,0},{24,8},{1,17},{9,25},{17,1},{25,9},{2,18},{10... | collective-permute-start | bytes 196616 | tf_op jit(solution)/shard_map/cond/branch_1_fun/ppermute | solution.py:21
  42.7 8.7 %collective-permute-start = (bf16[384,256]{1,0:T(8,128)(2,1)S(1)}, bf16[384,256]{1,0:T(8,128)(2,1)}, u32[]{:S(2)}, u32[]{:S(2)}) collective-permute-start(bf16[384,256]{1,0:T(8,128)(2,1)S(1)} %get-tuple-element.9), channel_id=1, source_target_pairs={{0,8},{8,0},{16,24},{24,16},{1,9},{9,1},{17,25},{25,17},{2,10},{10... | collective-permute-start | bytes 589832 | tf_op jit(solution)/shard_map/cond/branch_1_fun/ppermute | solution.py:21
  48.6 1.3 %collective-permute-start.4 = (bf16[128,256]{1,0:T(8,128)(2,1)S(1)}, bf16[128,256]{1,0:T(8,128)(2,1)S(1)}, u32[]{:S(2)}, u32[]{:S(2)}) collective-permute-start(bf16[128,256]{1,0:T(8,128)(2,1)S(1)} %add_convert_fusion.part_ref), channel_id=1, source_target_pairs={{0,1},{1,0},{2,3},{3,2},{4,5},{5,4},{6,7},{7,6},{8,9},{9,8},{10,11... | collective-permute-start | bytes 196616 | tf_op jit(solution)/shard_map/cond/branch_1_fun/ppermute | solution.py:21
  51.4 2.3 %copy-start.9 = (bf16[256,256]{1,0:T(8,128)(2,1)}, bf16[256,256]{1,0:T(8,128)(2,1)S(1)}, u32[]{:S(2)}) copy-start(bf16[256,256]{1,0:T(8,128)(2,1)S(1)} %get-tuple-element.34) | copy-start | bytes 393220

commit v9 on v8

--- a/solution.py
+++ b/solution.py
@@ -147,18 +147,19 @@
 
 
 def finish(cap, edge, coming_ref, *args):
-    terms, out_ref = args[:-1], args[-1]
-    for j in range(out_ref.shape[0] // edge):
-        part = slice(j * edge, (j + 1) * edge)
-        total = terms[0][part, :].astype(F32)
-        for ref in terms[1:]:
-            total += ref[part, :].astype(F32)
-        for f in range(coming_ref.shape[0]):
-            for c in range(cap):
-                top = cap * edge + c * 16
-                place = coming_ref[f, top:top + 1, :].astype(F32)
-                total += jnp.where(place == j, coming_ref[f, c * edge:(c + 1) * edge, :].astype(F32), 0.0)
-        out_ref[part, :] = total.astype(BF16)
+    terms, (out_ref, total_ref) = args[:-2], args[-2:]
+    total = terms[0][...].astype(F32)
+    for ref in terms[1:]:
+        total += ref[...].astype(F32)
+    total_ref[...] = total
+    for f in range(coming_ref.shape[0]):
+        for c in range(cap):
+            top = cap * edge + c * 16
+            place = coming_ref[f, top:top + 1, :].astype(F32)
+            block = coming_ref[f, c * edge:(c + 1) * edge, :].astype(F32)
+            for j in range(out_ref.shape[0] // edge):
+                total_ref[j * edge:(j + 1) * edge, :] += jnp.where(place == j, block, 0.0)
+    out_ref[...] = total_ref[...].astype(BF16)
 
 
 def local(feats, cotangent, weight, bias, in_vals, in_cols, off_vals, off_ref, want):
@@ -217,7 +218,8 @@
     terms = dict(zip([k for k in turns(count) if k > 2], terms)) | {2: next_terms}
     got = [swapped(after(terms[k], first if k == 2 else None), "rep", k) for k in range(count - 1, 1, -1)]
     coming, one, grad_weight = fenced(sure, exchange, outer, part, near_terms)
-    grad_feats = call(functools.partial(finish, cap, edge), [flat], (coming, own, *got, one), "v" * (count + 1), name="finish")[0]
+    grad_feats = call(functools.partial(finish, cap, edge), [flat], (coming, own, *got, one), "v" * (count + 1),
+        scratch=[pltpu.VMEM((rows, width), F32)], name="finish")[0]
     return (activated, grad_feats, grad_weight)
 
 

time: 54 us -> 53.9 us (level)
  no operation moved by 1% of the time
where the time goes in v9:
time: 53.9 us; the launch traced here: 53.6 us
  starting transfers between devices  27.7 us (51%)
  waiting for transfers between devices  14.2 us (26%)
  Pallas kernels  8.72 us (16%)
  local copies, waits for them, and re-layouts  1.86 us (3%)
  between operations  0.84 us (2%)
    ppermute x18, starting transfers between devices, swapped(): lax.ppermute(value, axis, [(i, i ^ k) for i in range(lax.axis_size(axis))])  19.2 us
    ppermute x18, waiting for transfers between devices, swapped(): lax.ppermute(value, axis, [(i, i ^ k) for i in range(lax.axis_size(axis))])  11.6 us
    pallas_call x6, Pallas kernels, call(): pl.pallas_call(body, out_shape=outs, in_specs=[pl.BlockSpec(memory_space=...  8.72 us
    ppermute x1, starting transfers between devices, relayed(): return lax.ppermute(value, 'rep', [pair[::turns] for pair in pairs])  4.25 us
    all_to_all x1, starting transfers between devices, exchange(): lax.all_to_all(outer, 'dom', split_axis=0, concat_axis=0, tiled=True)  4.19 us
    ppermute x1, waiting for transfers between devices, relayed(): return lax.ppermute(value, 'rep', [pair[::turns] for pair in pairs])  2.6 us
    unnamed x20, local copies, waits for them, and re-layouts  1.86 us
  transfers between devices with their start and end apart: 20, of which 7 were waited for; matrix products, arithmetic and copies ran while one was open for 0% of the time, Pallas kernels for 8%

profile of v9, /device:TPU:0, one launch (start us, length us, event | category | flops | bytes accessed | tf_op | source)
XLA Modules:
  0.0 53.6 jit_solution(3965321549308138770)
XLA Ops:
  0.6 0.5 collective-permute-start.5
  1.1 2.6 %collective-permute-start.6 = (bf16[384,256]{1,0:T(8,128)(2,1)}, bf16[384,256]{1,0:T(8,128)(2,1)S(1)}, u32[]{:S(2)}, u32[]{:S(2)}) collective-permute-start(bf16[384,256]{1,0:T(8,128)(2,1)} %args_0_.4), channel_id=1, source_target_pairs={{0,4},{1,5},{2,6},{3,7},{4,0},{5,1},{6,2},{7,3},{8,12},{9,13},{10,... | collective-permute-start | bytes 589832 | tf_op jit(solution)/shard_map/ppermute | solution.py:21
  3.7 3.6 %collective-permute-start.7 = (bf16[384,256]{1,0:T(8,128)(2,1)}, bf16[384,256]{1,0:T(8,128)(2,1)S(1)}, u32[]{:S(2)}, u32[]{:S(2)}) collective-permute-start(bf16[384,256]{1,0:T(8,128)(2,1)} %args_0_.4), channel_id=1, source_target_pairs={{0,24},{8,16},{16,8},{24,0},{1,25},{9,17},{17,9},{25,1},{2,26},{10... | collective-permute-start | bytes 589832 | tf_op jit(solution)/shard_map/ppermute | solution.py:21
  7.3 0.1 pad_add_fusion.me_ref
  7.4 1.5 %collective-permute-start.10 = (bf16[384,256]{1,0:T(8,128)(2,1)}, bf16[384,256]{1,0:T(8,128)(2,1)S(1)}, u32[]{:S(2)}, u32[]{:S(2)}) collective-permute-start(bf16[384,256]{1,0:T(8,128)(2,1)} %args_0_.4), channel_id=1, source_target_pairs={{0,2},{1,3},{2,0},{3,1},{4,6},{5,7},{6,4},{7,5},{8,10},{9,11},{10,... | collective-permute-start | bytes 589832 | tf_op jit(solution)/shard_map/ppermute | solution.py:21
  8.9 0.5 collective-permute-start.13
  9.4 1.1 %copy-done.1 = bf16[3,4,2,128,128]{4,3,2,1,0:T(8,128)(2,1)S(1)} copy-done((bf16[3,4,2,128,128]{4,3,2,1,0:T(8,128)(2,1)S(1)}, bf16[3,4,2,128,128]{4,3,2,1,0:T(8,128)(2,1)}, u32[]{:S(2)}) %copy-start.1) | copy-done | bytes 786456
  10.6 0.7 %copy-done.5 = s32[3,4,2]{1,2,0:T(2,128)S(1)} copy-done((s32[3,4,2]{1,2,0:T(2,128)S(1)}, s32[3,4,2]{1,2,0:T(2,128)}, u32[]{:S(2)}) %copy-start.5) | copy-done | bytes 120
  11.3 0.9 %arrange.1.a_ref.args_9_ = bf16[384,1536]{1,0:T(8,128)(2,1)S(1)} custom-call(s32[2]{0:T(128)S(1)} %pad_add_fusion.me_ref, s32[3,2,4]{2,1,0:T(2,128)S(1)} %bitcast.7, bf16[3,4,2,128,128]{4,3,2,1,0:T(8,128)(2,1)S(1)} %copy-done.1), custom_call_target="tpu_custom_call" | custom-call | bytes 1966184 | tf_op jit(solution)/shard_map/arrange/pallas_call | solution.py:42
  12.2 0.1 collective-permute-start.12
  12.3 1.3 %collective-permute-done.7.args_1_ = bf16[384,256]{1,0:T(8,128)(2,1)S(1)} collective-permute-done((bf16[384,256]{1,0:T(8,128)(2,1)}, bf16[384,256]{1,0:T(8,128)(2,1)S(1)}, u32[]{:S(2)}, u32[]{:S(2)}) %collective-permute-start.7) | collective-permute-done | bytes 196640 | tf_op jit(solution)/shard_map/ppermute | solution.py:21
  13.6 4.3 %collective-permute-start.8 = (bf16[384,256]{1,0:T(8,128)(2,1)S(1)}, bf16[384,256]{1,0:T(8,128)(2,1)S(1)}, u32[]{:S(2)}, u32[]{:S(2)}) collective-permute-start(bf16[384,256]{1,0:T(8,128)(2,1)S(1)} %broadcast_select_fusion), channel_id=1, source_target_pairs={{8,0},{24,8},{16,24},{0,16},{9,1},{25,9},{17,25},{1,17},{10,2},{26... | collective-permute-start | bytes 589832 | tf_op jit(solution)/shard_map/ppermute | solution.py:26
  17.9 0.6 %collective-permute-done.13.args_7_ = bf16[384,256]{1,0:T(8,128)(2,1)S(1)} collective-permute-done((bf16[384,256]{1,0:T(8,128)(2,1)}, bf16[384,256]{1,0:T(8,128)(2,1)S(1)}, u32[]{:S(2)}, u32[]{:S(2)}) %collective-permute-start.13) | collective-permute-done | bytes 196640 | tf_op jit(solution)/shard_map/ppermute | solution.py:21
  18.5 0.4 begin.1.args_1_
  18.9 2.6 %collective-permute-done.8.args_0_ = bf16[384,256]{1,0:T(8,128)(2,1)S(1)} collective-permute-done((bf16[384,256]{1,0:T(8,128)(2,1)S(1)}, bf16[384,256]{1,0:T(8,128)(2,1)S(1)}, u32[]{:S(2)}, u32[]{:S(2)}) %collective-permute-start.8) | collective-permute-done | bytes 196640 | tf_op jit(solution)/shard_map/ppermute | solution.py:26
  21.6 2.1 %layer.1 = (bf16[384,256]{1,0:T(8,128)(2,1)S(1)}, bf16[128,256]{1,0:T(8,128)(2,1)S(1)}, bf16[128,256]{1,0:T(8,128)(2,1)S(1)}, bf16[384,256]{1,0:T(8,128)(2,1)S(1)}, bf16[384,256]{1,0:T(8,128)(2,1)S(1)}) custom-call(s32[2]{0:T(128)S(1)} %pad_add_fusion.me_ref, s32[1,8]{1,0:T(1,128)S(1)} %bitcast.9, s32[3,9]{1,0:T(4,128)S(1)} %copy-done.6, ...), custom_call_target="tpu_custom_call" | custom-call | flops 1000000000 | bytes 5080212 | tf_op jit(solution)/shard_map/layer/pallas_call | solution.py:42
  23.8 2.3 %collective-permute-start.17 = (bf16[384,256]{1,0:T(8,128)(2,1)S(1)}, bf16[384,256]{1,0:T(8,128)(2,1)S(1)}, u32[]{:S(2)}, u32[]{:S(2)}) collective-permute-start(bf16[384,256]{1,0:T(8,128)(2,1)S(1)} %get-tuple-element.50), channel_id=1, source_target_pairs={{0,24},{8,16},{16,8},{24,0},{1,25},{9,17},{17,9},{25,1},{2,26},{10... | collective-permute-start | bytes 589832 | tf_op jit(solution)/shard_map/ppermute | solution.py:21
  26.1 1.4 %collective-permute-start.16 = (bf16[128,256]{1,0:T(8,128)(2,1)S(1)}, bf16[128,256]{1,0:T(8,128)(2,1)S(1)}, u32[]{:S(2)}, u32[]{:S(2)}) collective-permute-start(bf16[128,256]{1,0:T(8,128)(2,1)S(1)} %add_convert_fusion.4), channel_id=1, source_target_pairs={{0,4},{1,5},{2,6},{3,7},{4,0},{5,1},{6,2},{7,3},{8,12},{9,13},{10,... | collective-permute-start | bytes 196616 | tf_op jit(solution)/shard_map/ppermute | solution.py:21
  27.6 2.5 %rest.1 = (bf16[384,256]{1,0:T(8,128)(2,1)}, bf16[384,256]{1,0:T(8,128)(2,1)S(1)}, bf16[384,256]{1,0:T(8,128)(2,1)S(1)}, bf16[384,256]{1,0:T(8,128)(2,1)S(1)}, bf16[8,144,256]{2,1,0:T(8,128)(2,1)}) custom-call(s32[1,8]{1,0:T(1,128)S(1)} %bitcast.11, s32[3,9]{1,0:T(4,128)S(1)} %copy-done.6, bf16[384,1536]{1,0:T(8,128)(2,1)S(1)} %arrange.1.a_ref.args_9_, ...), custom_call_target="tpu_custom_call" | custom-call | flops 1000000000 | bytes 3833996 | tf_op jit(solution)/shard_map/rest/pallas_call | solution.py:42
  30.0 1.5 %collective-permute-start.18 = (bf16[384,256]{1,0:T(8,128)(2,1)S(1)}, bf16[384,256]{1,0:T(8,128)(2,1)S(1)}, u32[]{:S(2)}, u32[]{:S(2)}) collective-permute-start(bf16[384,256]{1,0:T(8,128)(2,1)S(1)} %get-tuple-element.52), channel_id=1, source_target_pairs={{0,16},{8,24},{16,0},{24,8},{1,17},{9,25},{17,1},{25,9},{2,18},{10... | collective-permute-start | bytes 589832 | tf_op jit(solution)/shard_map/ppermute | solution.py:21
  31.5 19.8 %conditional.1 = (bf16[8,144,256]{2,1,0:T(8,128)(2,1)}, bf16[384,256]{1,0:T(8,128)(2,1)}, bf16[256,256]{1,0:T(8,128)(2,1)S(1)}) conditional(s32[]{:T(128)} %bitcast.5, () %tuple.29, (bf16[8,144,256]{2,1,0:T(8,128)(2,1)}, bf16[384,256]{1,0:T(8,128)(2,1)S(1)}, bf16[128,256]{1,0:T(8,128)(2,1)S(1)}, s32[2]{0:T(128)S(1)}) %tuple.30), branch_computations={%region_0.1_spmd, %region_1.2_spmd} | conditional | flops 393216 | bytes 4456712 | solution.py:35
  31.6 1.6 %collective-permute-start.1 = (bf16[128,256]{1,0:T(8,128)(2,1)S(1)}, bf16[128,256]{1,0:T(8,128)(2,1)S(1)}, u32[]{:S(2)}, u32[]{:S(2)}) collective-permute-start(bf16[128,256]{1,0:T(8,128)(2,1)S(1)} %get-tuple-element.11), channel_id=1, source_target_pairs={{0,2},{1,3},{2,0},{3,1},{4,6},{5,7},{6,4},{7,5},{8,10},{9,11},{10,... | collective-permute-start | bytes 196616 | tf_op jit(solution)/shard_map/cond/branch_1_fun/ppermute | solution.py:21
  33.1 2.8 %collective-permute-done.1 = bf16[128,256]{1,0:T(8,128)(2,1)S(1)} collective-permute-done((bf16[128,256]{1,0:T(8,128)(2,1)S(1)}, bf16[128,256]{1,0:T(8,128)(2,1)S(1)}, u32[]{:S(2)}, u32[]{:S(2)}) %collective-permute-start.1) | collective-permute-done | bytes 65568 | tf_op jit(solution)/shard_map/cond/branch_1_fun/ppermute | solution.py:21
  35.9 0.8 %collective-permute-start.2 = (bf16[128,256]{1,0:T(8,128)(2,1)S(1)}, bf16[128,256]{1,0:T(8,128)(2,1)S(1)}, u32[]{:S(2)}, u32[]{:S(2)}) collective-permute-start(bf16[128,256]{1,0:T(8,128)(2,1)S(1)} %add_convert_fusion.2), channel_id=1, source_target_pairs={{0,8},{8,0},{16,24},{24,16},{1,9},{9,1},{17,25},{25,17},{2,10},{10... | collective-permute-start | bytes 196616 | tf_op jit(solution)/shard_map/cond/branch_1_fun/ppermute | solution.py:21
  36.7 4.2 %all-to-all-start = ((bf16[8,144,256]{2,1,0:T(8,128)(2,1)}), bf16[8,144,256]{2,1,0:T(8,128)(2,1)}, u32[]{:S(2)}, u32[]{:S(2)}) async-start(bf16[8,144,256]{2,1,0:T(8,128)(2,1)} %get-tuple-element.8), calls=%async_computation | async-start | bytes 1179648 | tf_op jit(solution)/shard_map/cond/branch_1_fun/all_to_all | solution.py:183
  40.9 1.7 %collective-permute-start.3 = (bf16[128,256]{1,0:T(8,128)(2,1)S(1)}, bf16[128,256]{1,0:T(8,128)(2,1)S(1)}, u32[]{:S(2)}, u32[]{:S(2)}) collective-permute-start(bf16[128,256]{1,0:T(8,128)(2,1)S(1)} %add_convert_fusion.1), channel_id=1, source_target_pairs={{0,16},{8,24},{16,0},{24,8},{1,17},{9,25},{17,1},{25,9},{2,18},{10... | collective-permute-start | bytes 196616 | tf_op jit(solution)/shard_map/cond/branch_1_fun/ppermute | solution.py:21
  42.7 1.1 %collective-permute-start = (bf16[384,256]{1,0:T(8,128)(2,1)S(1)}, bf16[384,256]{1,0:T(8,128)(2,1)}, u32[]{:S(2)}, u32[]{:S(2)}) collective-permute-start(bf16[384,256]{1,0:T(8,128)(2,1)S(1)} %get-tuple-element.9), channel_id=1, source_target_pairs={{0,8},{8,0},{16,24},{24,16},{1,9},{9,1},{17,25},{25,17},{2,10},{10... | collective-permute-start | bytes 589832 | tf_op jit(solution)/shard_map/cond/branch_1_fun/ppermute | solution.py:21
  43.8 4.8 %collective-permute-done.3 = bf16[128,256]{1,0:T(8,128)(2,1)S(1)} collective-permute-done((bf16[128,256]{1,0:T(8,128)(2,1)S(1)}, bf16[128,256]{1,0:T(8,128)(2,1)S(1)}, u32[]{:S(2)}, u32[]{:S(2)}) %collective-permute-start.3) | collective-permute-done | bytes 65568 | tf_op jit(solution)/shard_map/cond/branch_1_fun/ppermute | solution.py:21
  48.7 1.2 %collective-permute-done.4.other_ref = bf16[128,256]{1,0:T(8,128)(2,1)S(1)} collective-permute-done((bf16[128,256]{1,0:T(8,128)(2,1)S(1)}, bf16[128,256]{1,0:T(8,128)(2,1)S(1)}, u32[]{:S(2)}, u32[]{:S(2)}) %collective-permute-start.4) | collective-permute-done | bytes 65568 | tf_op jit(solution)/shard_map/cond/branch_1_fun/ppermute | solution.py:21
  49.9 0.6 %join.1 = bf16[256,256]{1,0:T(8,128)(2,1)S(1)} custom-call(s32[2]{0:T(128)S(1)} %get-tuple-element.10.me_ref, bf16[128,256]{1,0:T(8,128)(2,1)S(1)} %add_convert_fusion.part_ref, bf16[128,256]{1,0:T(8,128)(2,1)S(1)} %collective-permute-done.4.other_ref), custom_call_target="tpu_custom_call" | custom-call | bytes 262152 | tf_op jit(solution)/shard_map/cond/branch_1_fun/join/pallas_call | solution.py:42
  50.5 0.9 %collective-permute-done = bf16[384,256]{1,0:T(8,128)(2,1)} collective-permute-done((bf16[384,256]{1,0:T(8,128)(2,1)S(1)}, bf16[384,256]{1,0:T(8,128)(2,1)}, u32[]{:S(2)}, u32[]{:S(2)}) %collective-permute-start) | collective-permute-done | bytes 196640 | tf_op jit(solution)/shard_map/cond/branch_1_fun/ppermute | solution.py:21
  51.4 2.2 %finish.1 = bf16[384,256]{1,0:T(8,128)(2,1)} custom-call(bf16[8,144,256]{2,1,0:T(8,128)(2,1)} %get-tuple-element.48.coming_ref, bf16[384,256]{1,0:T(8,128)(2,1)S(1)} %get-tuple-element.49.args_0_, bf16[384,256]{1,0:T(8,128)(2,1)S(1)} %collective-permute-done.17.args_1_, bf16[384,256]{1,0:T(8,128)(2,1)S(1)} %collective-permute-done.18.args_2_, ...), custom_call_target="tpu_custom_call" | custom-call | bytes 1572864 | tf_op jit(solution)/shard_map/finish/pallas_call | solution.py:42
  (42 shorter events, 0.4 us)
Async XLA Ops:
  0.6 6.8 %collective-permute-start.5 = (bf16[384,256]{1,0:T(8,128)(2,1)}, bf16[384,256]{1,0:T(8,128)(2,1)S(1)}, u32[]{:S(2)}, u32[]{:S(2)}) collective-permute-start(bf16[384,256]{1,0:T(8,128)(2,1)} %args_0_.4), channel_id=1, source_target_pairs={{0,1},{1,0},{2,3},{3,2},{4,5},{5,4},{6,7},{7,6},{8,9},{9,8},{10,11... | collective-permute-start | bytes 589832 | tf_op jit(solution)/shard_map/ppermute | solution.py:21
  1.1 8.3 %collective-permute-start.6 = (bf16[384,256]{1,0:T(8,128)(2,1)}, bf16[384,256]{1,0:T(8,128)(2,1)S(1)}, u32[]{:S(2)}, u32[]{:S(2)}) collective-permute-start(bf16[384,256]{1,0:T(8,128)(2,1)} %args_0_.4), channel_id=1, source_target_pairs={{0,4},{1,5},{2,6},{3,7},{4,0},{5,1},{6,2},{7,3},{8,12},{9,13},{10,... | collective-permute-start | bytes 589832 | tf_op jit(solution)/shard_map/ppermute | solution.py:21
  3.7 9.8 %collective-permute-start.7 = (bf16[384,256]{1,0:T(8,128)(2,1)}, bf16[384,256]{1,0:T(8,128)(2,1)S(1)}, u32[]{:S(2)}, u32[]{:S(2)}) collective-permute-start(bf16[384,256]{1,0:T(8,128)(2,1)} %args_0_.4), channel_id=1, source_target_pairs={{0,24},{8,16},{16,8},{24,0},{1,25},{9,17},{17,9},{25,1},{2,26},{10... | collective-permute-start | bytes 589832 | tf_op jit(solution)/shard_map/ppermute | solution.py:21
  7.3 11.2 %collective-permute-start.9 = (bf16[384,256]{1,0:T(8,128)(2,1)}, bf16[384,256]{1,0:T(8,128)(2,1)S(1)}, u32[]{:S(2)}, u32[]{:S(2)}) collective-permute-start(bf16[384,256]{1,0:T(8,128)(2,1)} %args_0_.4), channel_id=1, source_target_pairs={{0,8},{8,0},{16,24},{24,16},{1,9},{9,1},{17,25},{25,17},{2,10},{10... | collective-permute-start | bytes 589832 | tf_op jit(solution)/shard_map/ppermute | solution.py:21
  7.4 10.5 %collective-permute-start.10 = (bf16[384,256]{1,0:T(8,128)(2,1)}, bf16[384,256]{1,0:T(8,128)(2,1)S(1)}, u32[]{:S(2)}, u32[]{:S(2)}) collective-permute-start(bf16[384,256]{1,0:T(8,128)(2,1)} %args_0_.4), channel_id=1, source_target_pairs={{0,2},{1,3},{2,0},{3,1},{4,6},{5,7},{6,4},{7,5},{8,10},{9,11},{10,... | collective-permute-start | bytes 589832 | tf_op jit(solution)/shard_map/ppermute | solution.py:21
  8.9 9.6 %collective-permute-start.13 = (bf16[384,256]{1,0:T(8,128)(2,1)}, bf16[384,256]{1,0:T(8,128)(2,1)S(1)}, u32[]{:S(2)}, u32[]{:S(2)}) collective-permute-start(bf16[384,256]{1,0:T(8,128)(2,1)} %args_0_.4), channel_id=1, source_target_pairs={{0,6},{1,7},{2,4},{3,5},{4,2},{5,3},{6,0},{7,1},{8,14},{9,15},{10,... | collective-permute-start | bytes 589832 | tf_op jit(solution)/shard_map/ppermute | solution.py:21
  9.4 1.1 %copy-start.1 = (bf16[3,4,2,128,128]{4,3,2,1,0:T(8,128)(2,1)S(1)}, bf16[3,4,2,128,128]{4,3,2,1,0:T(8,128)(2,1)}, u32[]{:S(2)}) copy-start(bf16[3,4,2,128,128]{4,3,2,1,0:T(8,128)(2,1)} %in_hbm.1) | copy-start | bytes 2359300
  10.6 0.7 %copy-start.5 = (s32[3,4,2]{1,2,0:T(2,128)S(1)}, s32[3,4,2]{1,2,0:T(2,128)}, u32[]{:S(2)}) copy-start(s32[3,4,2]{1,2,0:T(2,128)} %param.16) | copy-start | bytes 292
  11.3 2.3 %copy-start.2 = (bf16[384,256]{1,0:T(8,128)(2,1)S(1)}, bf16[384,256]{1,0:T(8,128)(2,1)}, u32[]{:S(2)}) copy-start(bf16[384,256]{1,0:T(8,128)(2,1)} %args_0_.4) | copy-start | bytes 589828
  12.2 6.7 %collective-permute-start.12 = (bf16[384,256]{1,0:T(8,128)(2,1)S(1)}, bf16[384,256]{1,0:T(8,128)(2,1)S(1)}, u32[]{:S(2)}, u32[]{:S(2)}) collective-permute-start(bf16[384,256]{1,0:T(8,128)(2,1)S(1)} %collective-permute-done.6.args_5_), channel_id=1, source_target_pairs={{0,1},{1,0},{2,3},{3,2},{4,5},{5,4},{6,7},{7,6},{8,9},{9,8},{10,11... | collective-permute-start | bytes 589832 | tf_op jit(solution)/shard_map/ppermute | solution.py:21
  13.6 8.0 %copy-start = (bf16[3,9,128,128]{3,2,1,0:T(8,128)(2,1)S(1)}, bf16[3,9,128,128]{3,2,1,0:T(8,128)(2,1)}, u32[]{:S(2)}) copy-start(bf16[3,9,128,128]{3,2,1,0:T(8,128)(2,1)} %off_ref.1) | copy-start | bytes 2654212
  13.6 8.0 %copy-start.3 = (bf16[384,256]{1,0:T(8,128)(2,1)S(1)}, bf16[384,256]{1,0:T(8,128)(2,1)}, u32[]{:S(2)}) copy-start(bf16[384,256]{1,0:T(8,128)(2,1)} %args_13_.1) | copy-start | bytes 589828
  13.6 8.0 %copy-start.4 = (bf16[256,256]{1,0:T(8,128)(2,1)S(1)}, bf16[256,256]{1,0:T(8,128)(2,1)}, u32[]{:S(2)}) copy-start(bf16[256,256]{1,0:T(8,128)(2,1)} %args_11_.1) | copy-start | bytes 393220
  13.6 8.0 %copy-start.6 = (s32[3,9]{1,0:T(4,128)S(1)}, s32[3,9]{1,0:T(4,128)}, u32[]{:S(2)}) copy-start(s32[3,9]{1,0:T(4,128)} %refs_ref.3) | copy-start | bytes 328
  13.6 8.0 %copy-start.7 = (f32[256]{0:T(256)S(1)}, f32[256]{0:T(256)}, u32[]{:S(2)}) copy-start(f32[256]{0:T(256)} %param.14) | copy-start | bytes 3076
  13.6 8.0 %copy-start.8 = (s32[1,1,8,1]{2,3,1,0:T(1,128)S(1)}, s32[1,1,8,1]{2,3,1,0:T(1,128)}, u32[]{:S(2)}) copy-start(s32[1,1,8,1]{2,3,1,0:T(1,128)} %param.19) | copy-start | bytes 100
  13.6 7.9 %collective-permute-start.8 = (bf16[384,256]{1,0:T(8,128)(2,1)S(1)}, bf16[384,256]{1,0:T(8,128)(2,1)S(1)}, u32[]{:S(2)}, u32[]{:S(2)}) collective-permute-start(bf16[384,256]{1,0:T(8,128)(2,1)S(1)} %broadcast_select_fusion), channel_id=1, source_target_pairs={{8,0},{24,8},{16,24},{0,16},{9,1},{25,9},{17,25},{1,17},{10,2},{26... | collective-permute-start | bytes 589832 | tf_op jit(solution)/shard_map/ppermute | solution.py:26
  17.9 3.7 %collective-permute-start.11 = (bf16[384,256]{1,0:T(8,128)(2,1)S(1)}, bf16[384,256]{1,0:T(8,128)(2,1)S(1)}, u32[]{:S(2)}, u32[]{:S(2)}) collective-permute-start(bf16[384,256]{1,0:T(8,128)(2,1)S(1)} %collective-permute-done.10.args_3_), channel_id=1, source_target_pairs={{0,1},{1,0},{2,3},{3,2},{4,5},{5,4},{6,7},{7,6},{8,9},{9,8},{10,11... | collective-permute-start | bytes 589832 | tf_op jit(solution)/shard_map/ppermute | solution.py:21
  18.5 3.1 %collective-permute-start.14 = (bf16[384,256]{1,0:T(8,128)(2,1)S(1)}, bf16[384,256]{1,0:T(8,128)(2,1)S(1)}, u32[]{:S(2)}, u32[]{:S(2)}) collective-permute-start(bf16[384,256]{1,0:T(8,128)(2,1)S(1)} %collective-permute-done.13.args_7_), channel_id=1, source_target_pairs={{0,1},{1,0},{2,3},{3,2},{4,5},{5,4},{6,7},{7,6},{8,9},{9,8},{10,11... | collective-permute-start | bytes 589832 | tf_op jit(solution)/shard_map/ppermute | solution.py:21
  23.7 2.4 %collective-permute-start.15 = (bf16[128,256]{1,0:T(8,128)(2,1)S(1)}, bf16[128,256]{1,0:T(8,128)(2,1)S(1)}, u32[]{:S(2)}, u32[]{:S(2)}) collective-permute-start(bf16[128,256]{1,0:T(8,128)(2,1)S(1)} %get-tuple-element.47), channel_id=1, source_target_pairs={{0,1},{1,0},{2,3},{3,2},{4,5},{5,4},{6,7},{7,6},{8,9},{9,8},{10,11... | collective-permute-start | bytes 196616 | tf_op jit(solution)/shard_map/ppermute | solution.py:21
  23.8 27.5 %collective-permute-start.17 = (bf16[384,256]{1,0:T(8,128)(2,1)S(1)}, bf16[384,256]{1,0:T(8,128)(2,1)S(1)}, u32[]{:S(2)}, u32[]{:S(2)}) collective-permute-start(bf16[384,256]{1,0:T(8,128)(2,1)S(1)} %get-tuple-element.50), channel_id=1, source_target_pairs={{0,24},{8,16},{16,8},{24,0},{1,25},{9,17},{17,9},{25,1},{2,26},{10... | collective-permute-start | bytes 589832 | tf_op jit(solution)/shard_map/ppermute | solution.py:21
  26.1 5.4 %collective-permute-start.16 = (bf16[128,256]{1,0:T(8,128)(2,1)S(1)}, bf16[128,256]{1,0:T(8,128)(2,1)S(1)}, u32[]{:S(2)}, u32[]{:S(2)}) collective-permute-start(bf16[128,256]{1,0:T(8,128)(2,1)S(1)} %add_convert_fusion.4), channel_id=1, source_target_pairs={{0,4},{1,5},{2,6},{3,7},{4,0},{5,1},{6,2},{7,3},{8,12},{9,13},{10,... | collective-permute-start | bytes 196616 | tf_op jit(solution)/shard_map/ppermute | solution.py:21
  30.0 21.3 %collective-permute-start.18 = (bf16[384,256]{1,0:T(8,128)(2,1)S(1)}, bf16[384,256]{1,0:T(8,128)(2,1)S(1)}, u32[]{:S(2)}, u32[]{:S(2)}) collective-permute-start(bf16[384,256]{1,0:T(8,128)(2,1)S(1)} %get-tuple-element.52), channel_id=1, source_target_pairs={{0,16},{8,24},{16,0},{24,8},{1,17},{9,25},{17,1},{25,9},{2,18},{10... | collective-permute-start | bytes 589832 | tf_op jit(solution)/shard_map/ppermute | solution.py:21
  31.6 4.3 %collective-permute-start.1 = (bf16[128,256]{1,0:T(8,128)(2,1)S(1)}, bf16[128,256]{1,0:T(8,128)(2,1)S(1)}, u32[]{:S(2)}, u32[]{:S(2)}) collective-permute-start(bf16[128,256]{1,0:T(8,128)(2,1)S(1)} %get-tuple-element.11), channel_id=1, source_target_pairs={{0,2},{1,3},{2,0},{3,1},{4,6},{5,7},{6,4},{7,5},{8,10},{9,11},{10,... | collective-permute-start | bytes 196616 | tf_op jit(solution)/shard_map/cond/branch_1_fun/ppermute | solution.py:21
  35.9 5.0 %collective-permute-start.2 = (bf16[128,256]{1,0:T(8,128)(2,1)S(1)}, bf16[128,256]{1,0:T(8,128)(2,1)S(1)}, u32[]{:S(2)}, u32[]{:S(2)}) collective-permute-start(bf16[128,256]{1,0:T(8,128)(2,1)S(1)} %add_convert_fusion.2), channel_id=1, source_target_pairs={{0,8},{8,0},{16,24},{24,16},{1,9},{9,1},{17,25},{25,17},{2,10},{10... | collective-permute-start | bytes 196616 | tf_op jit(solution)/shard_map/cond/branch_1_fun/ppermute | solution.py:21
  36.7 14.7 %all-to-all-start = ((bf16[8,144,256]{2,1,0:T(8,128)(2,1)}), bf16[8,144,256]{2,1,0:T(8,128)(2,1)}, u32[]{:S(2)}, u32[]{:S(2)}) async-start(bf16[8,144,256]{2,1,0:T(8,128)(2,1)} %get-tuple-element.8), calls=%async_computation | async-start | bytes 1179648 | tf_op jit(solution)/shard_map/cond/branch_1_fun/all_to_all | solution.py:183
  40.9 7.7 %collective-permute-start.3 = (bf16[128,256]{1,0:T(8,128)(2,1)S(1)}, bf16[128,256]{1,0:T(8,128)(2,1)S(1)}, u32[]{:S(2)}, u32[]{:S(2)}) collective-permute-start(bf16[128,256]{1,0:T(8,128)(2,1)S(1)} %add_convert_fusion.1), channel_id=1, source_target_pairs={{0,16},{8,24},{16,0},{24,8},{1,17},{9,25},{17,1},{25,9},{2,18},{10... | collective-permute-start | bytes 196616 | tf_op jit(solution)/shard_map/cond/branch_1_fun/ppermute | solution.py:21
  42.7 8.7 %collective-permute-start = (bf16[384,256]{1,0:T(8,128)(2,1)S(1)}, bf16[384,256]{1,0:T(8,128)(2,1)}, u32[]{:S(2)}, u32[]{:S(2)}) collective-permute-start(bf16[384,256]{1,0:T(8,128)(2,1)S(1)} %get-tuple-element.9), channel_id=1, source_target_pairs={{0,8},{8,0},{16,24},{24,16},{1,9},{9,1},{17,25},{25,17},{2,10},{10... | collective-permute-start | bytes 589832 | tf_op jit(solution)/shard_map/cond/branch_1_fun/ppermute | solution.py:21
  48.6 1.3 %collective-permute-start.4 = (bf16[128,256]{1,0:T(8,128)(2,1)S(1)}, bf16[128,256]{1,0:T(8,128)(2,1)S(1)}, u32[]{:S(2)}, u32[]{:S(2)}) collective-permute-start(bf16[128,256]{1,0:T(8,128)(2,1)S(1)} %add_convert_fusion.part_ref), channel_id=1, source_target_pairs={{0,1},{1,0},{2,3},{3,2},{4,5},{5,4},{6,7},{7,6},{8,9},{9,8},{10,11... | collective-permute-start | bytes 196616 | tf_op jit(solution)/shard_map/cond/branch_1_fun/ppermute | solution.py:21
  51.4 2.2 %copy-start.9 = (bf16[256,256]{1,0:T(8,128)(2,1)}, bf16[256,256]{1,0:T(8,128)(2,1)S(1)}, u32[]{:S(2)}) copy-start(bf16[256,256]{1,0:T(8,128)(2,1)S(1)} %get-tuple-element.34) | copy-start | bytes 393220
